TPU v7x, 32 devices: a whole 2x2x4 slice. The times are simulated.
32 devices in a mesh: leaf: 16 (over z, x, core), head: 2 (over y).
Axes of the slice: x: 2, y: 2, z: 4, core: 2. Of those that a mesh axis runs over, the one named last changes fastest.
Arguments:
- queries: bfloat16 [3072, 73728], P('leaf', 'head'), may hold values from -80 to 80
- d_out: bfloat16 [3072, 65536], P('leaf', 'head'), may hold values from -24 to 24
- branch_latent: bfloat16 [3072, 576], P('leaf'), may hold values from -6 to 6
- trunk_latent: bfloat16 [256, 8, 576], P('leaf'), may hold values from -6 to 6
- ancestors: int32 [16, 32], replicated, may hold values from 0 to 255, as said below
- anc_count: int32 [16], replicated, may hold values from 24 to 32, as said below
Outputs:
- d_queries: bfloat16 [3072, 73728], P('leaf', 'head')
- d_branch: float32 [3072, 576], P(('leaf', 'head'))
- d_trunk: float32 [256, 8, 576], P('leaf', 'head')
Inputs may be any that keep to these rules, and one draw needn't show every extreme that they name: `ancestors`: each row lists 32 different trunk blocks; the owner of a block is its number // 16; a row lists 2 blocks of each owner that it names, never more. `anc_count`: some branch has all 32 slots live.
All inputs are finite; a program needn't handle non-finite values.
Results may differ from a plain program's by a relative error of at most 0.014.
Values may be sent and summed in bfloat16 or wider, within the bound.
No kernel may reach another device: no remote copies, remote signals or barrier semaphores. Data moves between devices by JAX's collectives and lax.ppermute only.
A program may use at most 192 MiB of HBM per device.

v0:
```python
import functools
import math

import jax
import jax.numpy as jnp
from jax import lax
from jax.experimental import pallas as pl
from jax.experimental.pallas import tpu as pltpu
from jax.sharding import PartitionSpec as P

RANK = 512
QK_HEAD = 192
LATENT = 576
BLK = 8
CAP = 2
ANC = 32
LEAST_LIVE = 24
LANES = 128
WIDTH = 640
HALF = WIDTH - LATENT
PAIRS = 4
MASKED = -1e30
FAR_OFF = 1 << 20
SCALE = float(QK_HEAD) ** -0.5
EXP_SCALE = SCALE * math.log2(math.e)
MIB = 1024 * 1024
NT = (((1,), (1,)), ((), ()))
NN = (((1,), (0,)), ((), ()))
TN = (((0,), (0,)), ((), ()))


def mm(a, b, dims):
    return lax.dot_general(a, b, dims, preferred_element_type=jnp.float32)


def pieces(total, size):
    return [(at, min(size, total - at)) for at in range(0, total, size)]


def div(x, n):
    return x >> (n.bit_length() - 1) if n & (n - 1) == 0 else lax.div(x, jnp.full_like(x, n))


def mod(x, n):
    return x - div(x, n) * n


def column(rows):
    return lax.broadcasted_iota(jnp.int32, (rows, 1), 0)


def one_hot(place, size):
    lane = lax.broadcasted_iota(jnp.int32, (place.shape[0], size), 1)
    return jnp.where(lane == place, 1.0, 0.0).astype(jnp.bfloat16)


def token_part(tok):
    return 64 if tok % 64 == 0 else tok


def listed_blocks(ancestors, owned, second):
    leafs = ancestors.shape[0]
    rows = leafs * CAP * BLK
    named = ancestors[...].astype(jnp.float32)
    named = jnp.broadcast_to(named[:, None, :], (leafs, CAP * BLK, ANC)).reshape(rows, ANC)
    first = lax.axis_index("leaf") * owned
    low_end = first.astype(jnp.float32)
    mine = (named >= low_end) & (named < low_end + owned)
    low = jnp.min(jnp.where(mine, named, float(FAR_OFF)), axis=1, keepdims=True)
    high = jnp.max(jnp.where(mine, named, -1.0), axis=1, keepdims=True)
    return jnp.where(second, high, low).astype(jnp.int32) - first


def pick_kernel(ancestors, trunk, out):
    owned = trunk.shape[0] // BLK
    row = column(out.shape[0])
    block = listed_blocks(ancestors, owned, mod(div(row, BLK), CAP) == 1)
    sel = one_hot(block * BLK + mod(row, BLK), trunk.shape[0])
    out[...] = mm(sel, trunk[...], NN).astype(out.dtype)


def pick(ancestors, trunk):
    rows = ancestors.shape[0] * CAP * BLK
    return pl.pallas_call(
        pick_kernel,
        out_shape=jax.ShapeDtypeStruct((rows, LATENT), trunk.dtype),
        name="pick_blocks",
    )(ancestors, trunk)


def finish_kernel(ancestors, got, mine, *rest):
    theirs, (d_branch, d_trunk) = rest[:-2], rest[-2:]
    owned, part_rows = d_trunk.shape[0], d_trunk.shape[1]
    row = column(got.shape[0])
    block = listed_blocks(ancestors, owned, mod(div(row, part_rows), CAP) == 1)
    sel = one_hot(block * part_rows + mod(row, part_rows), owned * part_rows)
    total = mm(sel, got[...], TN)
    for b in range(owned):
        d_trunk[b] = total[b * part_rows:(b + 1) * part_rows]
    own = mine[...]
    for other in theirs:
        own = own + other[...]
    d_branch[...] = own


def finish(ancestors, got, mine, theirs, owned, part_rows):
    return pl.pallas_call(
        finish_kernel,
        out_shape=[
            jax.ShapeDtypeStruct(mine.shape, jnp.float32),
            jax.ShapeDtypeStruct((owned, part_rows, LATENT), jnp.float32),
        ],
        name="sum_gradients",
    )(ancestors, got, mine, *theirs)


def slot_places(ancestors, owned):
    row = column(ANC * BLK)
    mine = ancestors[pl.ds(lax.axis_index("leaf"), 1), :].astype(jnp.float32)
    mine = jnp.broadcast_to(mine, (ANC * BLK, ANC))
    lane = lax.broadcasted_iota(jnp.int32, (ANC * BLK, ANC), 1)
    block = jnp.max(jnp.where(lane == div(row, BLK), mine, -1.0), axis=1, keepdims=True)
    owner = div(block.astype(jnp.int32), owned)
    low_end = (owner * owned).astype(jnp.float32)
    below = (mine >= low_end) & (mine < block)
    second = jnp.max(jnp.where(below, 1.0, 0.0), axis=1, keepdims=True).astype(jnp.int32)
    return row, owner, second


def attn_kernel(
    owned, head_parts, anc_count, ancestors, incoming, own, q, do, ds, keys_e, keys_o, sent, *rest
):
    own_parts = rest[:head_parts]
    far_bias, causal, s_e, s_o, dp_e, dp_o, p_e, p_o, acc_e, acc_o, acc_v = rest[head_parts:]
    tok = q.shape[0]
    far_rows, rows = ANC * BLK, ANC * BLK + tok
    sub = token_part(tok)
    parts = tok // sub
    stack = PAIRS * sub
    least = LEAST_LIVE * BLK
    step = pl.program_id(0)

    @pl.when(step == 0)
    def _():
        row, owner, second = slot_places(ancestors, owned)
        sel = one_hot((owner * CAP + second) * BLK + mod(row, BLK), incoming.shape[0])
        far = mm(sel, incoming[...], NN)
        joined = jnp.concatenate([far, own[...].astype(jnp.float32)], axis=0)
        padded = jnp.concatenate([joined, jnp.zeros((rows, HALF), jnp.float32)], axis=1)
        keys_e[...] = padded.astype(jnp.bfloat16)
        keys_o[...] = pltpu.roll(padded, HALF, axis=1).astype(jnp.bfloat16)
        live = anc_count[lax.axis_index("leaf")]
        slot = div(lax.broadcasted_iota(jnp.int32, far_bias.shape, 0) + least, BLK)
        far_bias[...] = jnp.where(slot < live, 0.0, MASKED)
        key_at = lax.broadcasted_iota(jnp.int32, (sub, stack), 0)
        tok_at = mod(lax.broadcasted_iota(jnp.int32, (sub, stack), 1), sub)
        causal[...] = jnp.where(key_at <= tok_at, 0.0, MASKED)
        acc_e[...] = jnp.zeros_like(acc_e)
        acc_o[...] = jnp.zeros_like(acc_o)
        acc_v[...] = jnp.zeros_like(acc_v)

    keys = (keys_e, keys_o)
    s_st, dp_st, p_st, accs = (s_e, s_o), (dp_e, dp_o), (p_e, p_o), (acc_e, acc_o)

    def stacked(ref, j, first, pitch, at, size):
        toks = pl.ds(j * sub, sub)
        return jnp.concatenate(
            [ref[toks, pl.ds(first + i * pitch + at, size)] for i in range(PAIRS)], axis=0
        )

    def queries(par, j, at=0, size=WIDTH):
        return stacked(q, j, par * (LATENT - HALF), 2 * LATENT, at, size)

    def grads(par, j, at=0, size=RANK):
        return stacked(do, j, par * RANK, 2 * RANK, at, size)

    def seen(j):
        return far_rows + (j + 1) * sub

    def score(par, j):
        n, cols = seen(j), pl.ds(j * stack, stack)
        out = mm(keys[par][:n, :], queries(par, j), NT)
        s = s_st[par]
        s[:least, cols] = out[:least]
        s[least:far_rows, cols] = out[least:far_rows] + far_bias[...]
        if j > 0:
            s[far_rows:n - sub, cols] = out[far_rows:n - sub]
        s[n - sub:n, cols] = out[n - sub:] + causal[...]

    def prob(par, j):
        n, cols = seen(j), pl.ds(j * stack, stack)
        dp_st[par][:n, cols] = mm(keys_e[:n, :RANK], grads(par, j), NT)

    def soft(par, j, at):
        lane = pl.ds(j * stack + at, LANES)
        out_lane = pl.ds((par * parts + j) * stack + at, LANES)
        s, dp, p_out = s_st[par], dp_st[par], p_st[par]
        chunks = pieces(seen(j), 64)

        def fold(x):
            return x.reshape(-1, 8, LANES)

        top = None
        for r, n in chunks:
            part = jnp.max(fold(s[pl.ds(r, n), lane]), axis=0)
            top = part if top is None else jnp.maximum(top, part)
        top = jnp.max(top, axis=0, keepdims=True)
        total = jnp.zeros((8, LANES), jnp.float32)
        delta = jnp.zeros((8, LANES), jnp.float32)
        for r, n in chunks:
            e = jnp.exp2((s[pl.ds(r, n), lane] - top) * EXP_SCALE)
            s[pl.ds(r, n), lane] = e
            total += jnp.sum(fold(e), axis=0)
            delta += jnp.sum(fold(e * dp[pl.ds(r, n), lane]), axis=0)
        inv = 1.0 / jnp.sum(total, axis=0, keepdims=True)
        delta = jnp.sum(delta, axis=0, keepdims=True) * inv
        for r, n in chunks:
            p = s[pl.ds(r, n), lane] * inv
            p_out[pl.ds(r, n), lane] = p.astype(jnp.bfloat16)
            ds[0, pl.ds(r, n), out_lane] = (p * (dp[pl.ds(r, n), lane] - delta)).astype(ds.dtype)

    def grad_keys(par, j, at, size):
        n = seen(j)
        cols = pl.ds(at, size)
        d = ds[0, :n, pl.ds((par * parts + j) * stack, stack)]
        accs[par][:n, cols] += mm(d, queries(par, j, at, size), NN)

    def grad_values(par, j, at, size):
        n = seen(j)
        p = p_st[par][:n, pl.ds(j * stack, stack)]
        acc_v[:n, pl.ds(at, size)] += mm(p, grads(par, j, at, size), NN)

    units = [(par, j) for par in range(2) for j in range(parts)]

    def jobs_of(i):
        first, second, third = [], [], []
        if i < len(units):
            first = [functools.partial(score, *units[i]), functools.partial(prob, *units[i])]
        if 0 <= i - 1 < len(units):
            second = [functools.partial(soft, *units[i - 1], at) for at in range(0, stack, LANES)]
        if 0 <= i - 2 < len(units):
            unit = units[i - 2]
            third = [functools.partial(grad_values, *unit, *c) for c in pieces(RANK, 256)]
            third += [functools.partial(grad_keys, *unit, *c) for c in pieces(WIDTH, 256)]
        jobs = [first, second, third]
        order = [(k / len(group), g, job) for g, group in enumerate(jobs) for k, job in enumerate(group)]
        return [job for _, _, job in sorted(order, key=lambda item: item[:2])]

    for i in range(len(units) + 2):
        for job in jobs_of(i):
            job()

    @pl.when(step == pl.num_programs(0) - 1)
    def _():
        shifted = pltpu.roll(acc_o[...], WIDTH - HALF, axis=1)
        acc_e[...] = (acc_e[...] + shifted) * SCALE
        acc_e[:, :RANK] += acc_v[...]
        part_rows = BLK // head_parts
        row, owner, second = slot_places(ancestors, owned)
        inner = mod(row, BLK)
        place = (owner * head_parts + div(inner, part_rows)) * CAP + second
        place = place * part_rows + mod(inner, part_rows)
        sel = one_hot(place, sent.shape[0])
        far = acc_e[:far_rows, :LATENT].astype(jnp.bfloat16)
        sent[...] = mm(sel, far, TN).astype(sent.dtype)
        own_rows = tok // head_parts
        for hop, out in enumerate(own_parts):
            part = lax.rem(lax.axis_index("head") + hop, head_parts)
            at = pl.multiple_of(far_rows + part * own_rows, 8)
            out[...] = acc_e[pl.ds(at, own_rows), :LATENT]


def attention(owned, head_parts, anc_count, ancestors, incoming, own, queries, d_out):
    tok = queries.shape[0]
    heads = queries.shape[1] // LATENT
    steps = heads // (2 * PAIRS)
    far_rows, rows = ANC * BLK, ANC * BLK + tok
    toks = PAIRS * tok
    stack = PAIRS * token_part(tok)
    bf16, f32 = jnp.bfloat16, jnp.float32

    def whole(i):
        return (0, 0)

    def along(i):
        return (0, i)

    own_part = (tok // head_parts, LATENT)
    return pl.pallas_call(
        functools.partial(attn_kernel, owned, head_parts),
        grid=(steps,),
        in_specs=[
            pl.BlockSpec(memory_space=pltpu.SMEM),
            pl.BlockSpec(ancestors.shape, whole),
            pl.BlockSpec(incoming.shape, whole),
            pl.BlockSpec(own.shape, whole),
            pl.BlockSpec((tok, 2 * PAIRS * LATENT), along),
            pl.BlockSpec((tok, 2 * PAIRS * RANK), along),
        ],
        out_specs=[
            pl.BlockSpec((1, rows, 2 * toks), lambda i: (i, 0, 0)),
            pl.BlockSpec((rows, WIDTH), whole),
            pl.BlockSpec((rows, WIDTH), whole),
            pl.BlockSpec(incoming.shape, whole),
        ] + [pl.BlockSpec(own_part, whole)] * head_parts,
        out_shape=[
            jax.ShapeDtypeStruct((steps, rows, 2 * toks), bf16),
            jax.ShapeDtypeStruct((rows, WIDTH), bf16),
            jax.ShapeDtypeStruct((rows, WIDTH), bf16),
            jax.ShapeDtypeStruct(incoming.shape, bf16),
        ] + [jax.ShapeDtypeStruct(own_part, f32)] * head_parts,
        scratch_shapes=[
            pltpu.VMEM((far_rows - LEAST_LIVE * BLK, stack), f32),
            pltpu.VMEM((token_part(tok), stack), f32),
            pltpu.VMEM((rows, toks), f32), pltpu.VMEM((rows, toks), f32),
            pltpu.VMEM((rows, toks), f32), pltpu.VMEM((rows, toks), f32),
            pltpu.VMEM((rows, toks), bf16), pltpu.VMEM((rows, toks), bf16),
            pltpu.VMEM((rows, WIDTH), f32), pltpu.VMEM((rows, WIDTH), f32),
            pltpu.VMEM((rows, RANK), f32),
        ],
        compiler_params=pltpu.CompilerParams(vmem_limit_bytes=48 * MIB),
        cost_estimate=pl.CostEstimate(
            flops=2 * tok * heads * rows * (2 * LATENT + 2 * RANK),
            bytes_accessed=2 * tok * heads * (LATENT + RANK + rows),
            transcendentals=tok * heads * rows,
        ),
        name="score_gradients",
    )(anc_count, ancestors, incoming, own, queries, d_out)


def query_kernel(keys_e, keys_o, ds, dq):
    tok = dq.shape[0]
    rows = ds.shape[1]
    sub = token_part(tok)
    parts = tok // sub
    stack = PAIRS * sub
    low = LATENT - HALF
    for j in range(parts):
        n = rows - tok + (j + 1) * sub
        even = mm(ds[0, :n, pl.ds(j * stack, stack)], keys_e[:n, :], TN) * SCALE
        odd = mm(ds[0, :n, pl.ds((parts + j) * stack, stack)], keys_o[:n, :], TN) * SCALE
        for i in range(PAIRS):
            at = i * 2 * LATENT
            part = slice(i * sub, (i + 1) * sub)
            toks = pl.ds(j * sub, sub)
            dq[toks, at:at + low] = even[part, :low].astype(dq.dtype)
            joint = even[part, low:] + odd[part, :2 * HALF]
            dq[toks, at + low:at + low + 2 * HALF] = joint.astype(dq.dtype)
            dq[toks, at + low + 2 * HALF:at + 2 * LATENT] = odd[part, 2 * HALF:].astype(dq.dtype)


def query_gradients(keys_e, keys_o, ds, queries):
    tok = queries.shape[0]
    heads = queries.shape[1] // LATENT
    steps, rows = ds.shape[0], ds.shape[1]
    return pl.pallas_call(
        query_kernel,
        grid=(steps,),
        in_specs=[
            pl.BlockSpec(keys_e.shape, lambda i: (0, 0)),
            pl.BlockSpec(keys_o.shape, lambda i: (0, 0)),
            pl.BlockSpec((1,) + ds.shape[1:], lambda i: (i, 0, 0)),
        ],
        out_specs=pl.BlockSpec((tok, 2 * PAIRS * LATENT), lambda i: (0, i)),
        out_shape=jax.ShapeDtypeStruct(queries.shape, queries.dtype),
        compiler_params=pltpu.CompilerParams(vmem_limit_bytes=32 * MIB),
        cost_estimate=pl.CostEstimate(
            flops=2 * tok * heads * rows * LATENT,
            bytes_accessed=2 * tok * heads * (LATENT + rows),
            transcendentals=0,
        ),
        name="query_gradients",
    )(keys_e, keys_o, ds)


def local(queries, d_out, branch_latent, trunk_latent, ancestors, anc_count):
    leafs = lax.axis_size("leaf")
    head_parts = lax.axis_size("head")
    owned = trunk_latent.shape[0]
    part_rows = BLK // head_parts

    outgoing = pick(ancestors, trunk_latent.reshape(owned * BLK, LATENT))
    incoming = lax.all_to_all(
        outgoing.reshape(leafs, CAP * BLK, LATENT), "leaf", split_axis=0, concat_axis=0, tiled=True
    ).reshape(leafs * CAP * BLK, LATENT)

    ds, keys_e, keys_o, sent, mine, *others = attention(
        owned, head_parts, anc_count, ancestors, incoming, branch_latent, queries, d_out
    )

    got = lax.all_to_all(
        sent.reshape(leafs * head_parts, CAP * part_rows, LATENT),
        ("leaf", "head"), split_axis=0, concat_axis=0, tiled=True,
    ).reshape(leafs * CAP * BLK, LATENT)
    theirs = []
    for hop, part in enumerate(others, 1):
        route = [(i, (i + hop) % head_parts) for i in range(head_parts)]
        theirs.append(lax.ppermute(part, "head", route))

    d_queries = query_gradients(keys_e, keys_o, ds, queries)
    d_branch, d_trunk = finish(ancestors, got, mine, theirs, owned, part_rows)
    return d_queries, d_branch, d_trunk


def solution(mesh):
    return jax.shard_map(
        local,
        mesh=mesh,
        in_specs=(
            P("leaf", "head"),
            P("leaf", "head"),
            P("leaf", None),
            P("leaf", None, None),
            P(),
            P(),
        ),
        out_specs=(P("leaf", "head"), P(("leaf", "head"), None), P("leaf", "head", None)),
        check_vma=False,
    )
```

profile of v0, /device:TPU:0, one launch (start us, length us, event | category | flops | bytes accessed | tf_op | source)
XLA Modules:
  0.0 83.7 jit_solution(1042302708141870661)
XLA Ops:
  0.6 2.0 %pick_blocks.1 = bf16[256,576]{1,0:T(8,128)(2,1)} custom-call(s32[16,32]{1,0:T(8,128)} %ancestors.5, bf16[128,576]{1,0:T(8,128)(2,1)} %bitcast.8), custom_call_target="tpu_custom_call" | custom-call | tf_op jit(solution)/shard_map/pick_blocks/pallas_call | solution.py:84
  2.6 18.5 %all_to_all.10 = bf16[16,16,576]{2,1,0:T(8,128)(2,1)S(1)} all-to-all(bf16[16,16,576]{2,1,0:T(8,128)(2,1)} %bitcast.7), channel_id=1, replica_groups=mesh['leaf'=16,'head'=2] {'leaf'}, dimensions={0} | all-to-all | bytes 589824 | tf_op jit(solution)/shard_map/all_to_all | solution.py:383
  21.1 0.0 copy-start.2
  21.1 0.7 copy-done.2
  21.8 0.0 copy-start.3
  21.8 0.9 %copy-done.3 = bf16[192,576]{1,0:T(8,128)(2,1)S(1)} copy-done((bf16[192,576]{1,0:T(8,128)(2,1)S(1)}, bf16[192,576]{1,0:T(8,128)(2,1)}, u32[]{:S(2)}) %copy-start.3) | copy-done | bytes 221208
  22.7 0.0 copy-start.4
  22.7 0.7 copy-done.4
  23.4 35.4 %score_gradients.1 = (bf16[8,448,1536]{2,1,0:T(8,128)(2,1)}, bf16[448,640]{1,0:T(8,128)(2,1)S(1)}, bf16[448,640]{1,0:T(8,128)(2,1)S(1)}, bf16[256,576]{1,0:T(8,1...) custom-call(s32[16]{0:T(128)S(1)} %copy-done.4, s32[16,32]{1,0:T(8,128)S(1)} %copy-done.2, ...), custom_call_target="tpu_custom_call" | custom-call | flops 23957864448 | bytes 37748736 | tf_op jit(solution)/shard_map/score_gradients/pallas_call | solution.py:289
  58.8 0.0 copy-start.1
  58.8 0.7 copy-done.1
  59.5 3.2 %all-to-all-start.1 = ((bf16[32,8,576]{2,1,0:T(8,128)(2,1)}), bf16[32,8,576]{2,1,0:T(8,128)(2,1)S(1)}, u32[]{:S(2)}, u32[]{:S(2)}) async-start(bf16[32,8,576]{2,1,0:T(8,128)(2,1)} %bitcast.3), calls=%async_computation.1 | async-start | bytes 655360 | tf_op jit(solution)/shard_map/all_to_all | solution.py:391
  62.7 1.8 %collective-permute-start = (f32[96,576]{1,0:T(8,128)S(1)}, f32[96,576]{1,0:T(8,128)S(1)}, u32[]{:S(2)}, u32[]{:S(2)}) collective-permute-start(f32[96,576]{1,0:T(8,128)S(1)} %get-tuple-element.16), channel_id=1, source_target_pairs={{0,1},{1,0},{2,3},{3,2},{4,5},{5,4},{6,7},{7,6},{8,9},{9,8},{10,11... | collective-permute-start | bytes 663560 | tf_op jit(solution)/shard_map/ppermute | solution.py:398
  64.5 0.0 copy-start
  64.5 4.1 %copy-done = bf16[8,448,1536]{2,1,0:T(8,128)(2,1)S(1)} copy-done((bf16[8,448,1536]{2,1,0:T(8,128)(2,1)S(1)}, bf16[8,448,1536]{2,1,0:T(8,128)(2,1)}, u32[]{:S(2)}) %copy-start) | copy-done | bytes 11010072
  68.6 12.1 %query_gradients.1 = bf16[192,36864]{1,0:T(8,128)(2,1)} custom-call(bf16[448,640]{1,0:T(8,128)(2,1)S(1)} %get-tuple-element.11.keys_e, bf16[448,640]{1,0:T(8,128)(2,1)S(1)} %get-tuple-element.12.keys_o, bf16[8,448,1536]{2,1,0:T(8,128)(2,1)S(1)} %copy-done), custom_call_target="tpu_custom_call" | custom-call | flops 6341787648 | bytes 25165824 | tf_op jit(solution)/shard_map/query_gradients/pallas_call | solution.py:356
  80.8 0.0 collective-permute-done.rest_0_
  80.8 0.0 copy-start.6
  80.8 0.0 all-to-all-done.1
  80.8 0.0 copy-start.5
  80.8 0.7 copy-done.6
  81.5 0.1 copy-done.5
  81.6 2.2 %sum_gradients.1 = (f32[96,576]{1,0:T(8,128)}, f32[16,4,576]{2,1,0:T(4,128)}) custom-call(s32[16,32]{1,0:T(8,128)} %ancestors.5, bf16[256,576]{1,0:T(8,128)(2,1)} %bitcast.6, f32[96,576]{1,0:T(8,128)} %copy-done.1, f32[96,576]{1,0:T(8,128)} %copy-done.6), custom_call_target="tpu_custom_call" | custom-call | tf_op jit(solution)/shard_map/sum_gradients/pallas_call | solution.py:107
Async XLA Ops:
  21.1 0.7 copy-start.2
  21.8 0.9 %copy-start.3 = (bf16[192,576]{1,0:T(8,128)(2,1)S(1)}, bf16[192,576]{1,0:T(8,128)(2,1)}, u32[]{:S(2)}) copy-start(bf16[192,576]{1,0:T(8,128)(2,1)} %own.1) | copy-start | bytes 663556
  22.7 0.7 copy-start.4
  58.8 0.7 copy-start.1
  59.5 21.3 %all-to-all-start.1 = ((bf16[32,8,576]{2,1,0:T(8,128)(2,1)}), bf16[32,8,576]{2,1,0:T(8,128)(2,1)S(1)}, u32[]{:S(2)}, u32[]{:S(2)}) async-start(bf16[32,8,576]{2,1,0:T(8,128)(2,1)} %bitcast.3), calls=%async_computation.1 | async-start | bytes 655360 | tf_op jit(solution)/shard_map/all_to_all | solution.py:391
  62.7 18.1 %collective-permute-start = (f32[96,576]{1,0:T(8,128)S(1)}, f32[96,576]{1,0:T(8,128)S(1)}, u32[]{:S(2)}, u32[]{:S(2)}) collective-permute-start(f32[96,576]{1,0:T(8,128)S(1)} %get-tuple-element.16), channel_id=1, source_target_pairs={{0,1},{1,0},{2,3},{3,2},{4,5},{5,4},{6,7},{7,6},{8,9},{9,8},{10,11... | collective-permute-start | bytes 663560 | tf_op jit(solution)/shard_map/ppermute | solution.py:398
  64.5 4.1 %copy-start = (bf16[8,448,1536]{2,1,0:T(8,128)(2,1)S(1)}, bf16[8,448,1536]{2,1,0:T(8,128)(2,1)}, u32[]{:S(2)}) copy-start(bf16[8,448,1536]{2,1,0:T(8,128)(2,1)} %get-tuple-element.13.ds) | copy-start | bytes 33030148
  80.8 0.7 copy-start.6
  80.8 0.8 copy-start.5
where the time goes:
time: 84.2 us; the launch traced here: 83.7 us
  Pallas kernels  51.7 us (61%)
  blocking collectives  18.5 us (22%)
  local copies, waits for them, and re-layouts  7.92 us (9%)
  starting transfers between devices  5.02 us (6%)
    pallas_call x1, Pallas kernels, attention(): pl.pallas_call(functools.partial(attn_kernel, owned, head_parts), grid=(s...  35.4 us
    all_to_all x1, blocking collectives, local(): lax.all_to_all(outgoing.reshape(leafs, CAP * BLK, LATENT), 'leaf', split_...  18.5 us
    pallas_call x1, Pallas kernels, query_gradients(): pl.pallas_call(query_kernel, grid=(steps,), in_specs=[pl.BlockSpec(keys_e...  12.1 us
    unnamed x14, local copies, waits for them, and re-layouts  7.92 us
    all_to_all x1, starting transfers between devices, local(): lax.all_to_all(sent.reshape(leafs * head_parts, CAP * part_rows, LATENT),...  3.18 us
    pallas_call x1, Pallas kernels, finish(): pl.pallas_call(finish_kernel, out_shape=[jax.ShapeDtypeStruct(mine.shape,...  2.17 us
    pallas_call x1, Pallas kernels, pick(): pl.pallas_call(pick_kernel, out_shape=jax.ShapeDtypeStruct((rows, LATENT)...  1.97 us
    ppermute x1, starting transfers between devices, local(): theirs.append(lax.ppermute(part, 'head', route))  1.83 us
  transfers between devices with their start and end apart: 2, of which 0 were waited for; matrix products, arithmetic and copies ran while one was open for 0% of the time, Pallas kernels for 14%

commit v1 on v0

--- a/solution.py
+++ b/solution.py
@@ -110,6 +110,7 @@
             jax.ShapeDtypeStruct(mine.shape, jnp.float32),
             jax.ShapeDtypeStruct((owned, part_rows, LATENT), jnp.float32),
         ],
+        compiler_params=pltpu.CompilerParams(vmem_limit_bytes=8 * MIB),
         name="sum_gradients",
     )(ancestors, got, mine, *theirs)
 
@@ -131,12 +132,12 @@
     owned, head_parts, anc_count, ancestors, incoming, own, q, do, ds, keys_e, keys_o, sent, *rest
 ):
     own_parts = rest[:head_parts]
-    far_bias, causal, s_e, s_o, dp_e, dp_o, p_e, p_o, acc_e, acc_o, acc_v = rest[head_parts:]
+    far_bias, causal, q_st, s, dp, p_low, acc_k, acc_v = rest[head_parts:]
     tok = q.shape[0]
     far_rows, rows = ANC * BLK, ANC * BLK + tok
     sub = token_part(tok)
     parts = tok // sub
-    stack = PAIRS * sub
+    stack = 2 * PAIRS * sub
     least = LEAST_LIVE * BLK
     step = pl.program_id(0)
 
@@ -155,46 +156,44 @@
         key_at = lax.broadcasted_iota(jnp.int32, (sub, stack), 0)
         tok_at = mod(lax.broadcasted_iota(jnp.int32, (sub, stack), 1), sub)
         causal[...] = jnp.where(key_at <= tok_at, 0.0, MASKED)
-        acc_e[...] = jnp.zeros_like(acc_e)
-        acc_o[...] = jnp.zeros_like(acc_o)
+        acc_k[...] = jnp.zeros_like(acc_k)
         acc_v[...] = jnp.zeros_like(acc_v)
-
-    keys = (keys_e, keys_o)
-    s_st, dp_st, p_st, accs = (s_e, s_o), (dp_e, dp_o), (p_e, p_o), (acc_e, acc_o)
-
-    def stacked(ref, j, first, pitch, at, size):
-        toks = pl.ds(j * sub, sub)
-        return jnp.concatenate(
-            [ref[toks, pl.ds(first + i * pitch + at, size)] for i in range(PAIRS)], axis=0
-        )
-
-    def queries(par, j, at=0, size=WIDTH):
-        return stacked(q, j, par * (LATENT - HALF), 2 * LATENT, at, size)
-
-    def grads(par, j, at=0, size=RANK):
-        return stacked(do, j, par * RANK, 2 * RANK, at, size)
 
     def seen(j):
         return far_rows + (j + 1) * sub
 
-    def score(par, j):
-        n, cols = seen(j), pl.ds(j * stack, stack)
-        out = mm(keys[par][:n, :], queries(par, j), NT)
-        s = s_st[par]
+    def lanes(j):
+        return pl.ds(j * stack, stack)
+
+    def fill(j):
+        toks = pl.ds(j * sub, sub)
+        for i in range(PAIRS):
+            at = i * 2 * LATENT
+            q_st[pl.ds(j * stack + i * sub, sub), :] = q[toks, at:at + WIDTH]
+            odd = q[toks, at + LATENT - HALF:at + 2 * LATENT]
+            odd = pltpu.roll(odd, WIDTH - HALF, axis=1)
+            q_st[pl.ds(j * stack + (PAIRS + i) * sub, sub), :] = odd
+
+    def grads(j):
+        toks = pl.ds(j * sub, sub)
+        heads = list(range(0, 2 * PAIRS, 2)) + list(range(1, 2 * PAIRS, 2))
+        return jnp.concatenate([do[toks, pl.ds(h * RANK, RANK)] for h in heads], axis=0)
+
+    def score(j):
+        n, cols = seen(j), lanes(j)
+        out = mm(keys_e[:n, :], q_st[cols, :], NT)
         s[:least, cols] = out[:least]
         s[least:far_rows, cols] = out[least:far_rows] + far_bias[...]
         if j > 0:
             s[far_rows:n - sub, cols] = out[far_rows:n - sub]
         s[n - sub:n, cols] = out[n - sub:] + causal[...]
 
-    def prob(par, j):
-        n, cols = seen(j), pl.ds(j * stack, stack)
-        dp_st[par][:n, cols] = mm(keys_e[:n, :RANK], grads(par, j), NT)
-
-    def soft(par, j, at):
+    def prob(j):
+        n = seen(j)
+        dp[:n, lanes(j)] = mm(keys_e[:n, :RANK], grads(j), NT)
+
+    def soft(j, at):
         lane = pl.ds(j * stack + at, LANES)
-        out_lane = pl.ds((par * parts + j) * stack + at, LANES)
-        s, dp, p_out = s_st[par], dp_st[par], p_st[par]
         chunks = pieces(seen(j), 64)
 
         def fold(x):
@@ -216,58 +215,51 @@
         delta = jnp.sum(delta, axis=0, keepdims=True) * inv
         for r, n in chunks:
             p = s[pl.ds(r, n), lane] * inv
-            p_out[pl.ds(r, n), lane] = p.astype(jnp.bfloat16)
-            ds[0, pl.ds(r, n), out_lane] = (p * (dp[pl.ds(r, n), lane] - delta)).astype(ds.dtype)
-
-    def grad_keys(par, j, at, size):
+            p_low[pl.ds(r, n), lane] = p.astype(jnp.bfloat16)
+            ds[0, pl.ds(r, n), lane] = (p * (dp[pl.ds(r, n), lane] - delta)).astype(ds.dtype)
+
+    def grad_values(j):
         n = seen(j)
-        cols = pl.ds(at, size)
-        d = ds[0, :n, pl.ds((par * parts + j) * stack, stack)]
-        accs[par][:n, cols] += mm(d, queries(par, j, at, size), NN)
-
-    def grad_values(par, j, at, size):
+        acc_v[:n, :] += mm(p_low[:n, lanes(j)], grads(j), NN)
+
+    def grad_keys(j):
         n = seen(j)
-        p = p_st[par][:n, pl.ds(j * stack, stack)]
-        acc_v[:n, pl.ds(at, size)] += mm(p, grads(par, j, at, size), NN)
-
-    units = [(par, j) for par in range(2) for j in range(parts)]
+        acc_k[:n, :] += mm(ds[0, :n, lanes(j)], q_st[lanes(j), :], NN)
 
     def jobs_of(i):
-        first, second, third = [], [], []
-        if i < len(units):
-            first = [functools.partial(score, *units[i]), functools.partial(prob, *units[i])]
-        if 0 <= i - 1 < len(units):
-            second = [functools.partial(soft, *units[i - 1], at) for at in range(0, stack, LANES)]
-        if 0 <= i - 2 < len(units):
-            unit = units[i - 2]
-            third = [functools.partial(grad_values, *unit, *c) for c in pieces(RANK, 256)]
-            third += [functools.partial(grad_keys, *unit, *c) for c in pieces(WIDTH, 256)]
-        jobs = [first, second, third]
-        order = [(k / len(group), g, job) for g, group in enumerate(jobs) for k, job in enumerate(group)]
+        groups = []
+        if i < parts:
+            groups.append([functools.partial(job, i) for job in (fill, score, prob)])
+        if 0 <= i - 1 < parts:
+            groups.append([functools.partial(soft, i - 1, at) for at in range(0, stack, LANES)])
+        if 0 <= i - 2 < parts:
+            groups.append([functools.partial(job, i - 2) for job in (grad_values, grad_keys)])
+        order = [
+            (k / len(group), g, job) for g, group in enumerate(groups) for k, job in enumerate(group)
+        ]
         return [job for _, _, job in sorted(order, key=lambda item: item[:2])]
 
-    for i in range(len(units) + 2):
+    for i in range(parts + 2):
         for job in jobs_of(i):
             job()
 
     @pl.when(step == pl.num_programs(0) - 1)
     def _():
-        shifted = pltpu.roll(acc_o[...], WIDTH - HALF, axis=1)
-        acc_e[...] = (acc_e[...] + shifted) * SCALE
-        acc_e[:, :RANK] += acc_v[...]
+        acc_k[...] = acc_k[...] * SCALE
+        acc_k[:, :RANK] += acc_v[...]
         part_rows = BLK // head_parts
         row, owner, second = slot_places(ancestors, owned)
         inner = mod(row, BLK)
         place = (owner * head_parts + div(inner, part_rows)) * CAP + second
         place = place * part_rows + mod(inner, part_rows)
         sel = one_hot(place, sent.shape[0])
-        far = acc_e[:far_rows, :LATENT].astype(jnp.bfloat16)
+        far = acc_k[:far_rows, :LATENT].astype(jnp.bfloat16)
         sent[...] = mm(sel, far, TN).astype(sent.dtype)
         own_rows = tok // head_parts
         for hop, out in enumerate(own_parts):
             part = lax.rem(lax.axis_index("head") + hop, head_parts)
             at = pl.multiple_of(far_rows + part * own_rows, 8)
-            out[...] = acc_e[pl.ds(at, own_rows), :LATENT]
+            out[...] = acc_k[pl.ds(at, own_rows), :LATENT]
 
 
 def attention(owned, head_parts, anc_count, ancestors, incoming, own, queries, d_out):
@@ -275,8 +267,8 @@
     heads = queries.shape[1] // LATENT
     steps = heads // (2 * PAIRS)
     far_rows, rows = ANC * BLK, ANC * BLK + tok
-    toks = PAIRS * tok
-    stack = PAIRS * token_part(tok)
+    toks = 2 * PAIRS * tok
+    stack = 2 * PAIRS * token_part(tok)
     bf16, f32 = jnp.bfloat16, jnp.float32
 
     def whole(i):
@@ -298,13 +290,13 @@
             pl.BlockSpec((tok, 2 * PAIRS * RANK), along),
         ],
         out_specs=[
-            pl.BlockSpec((1, rows, 2 * toks), lambda i: (i, 0, 0)),
+            pl.BlockSpec((1, rows, toks), lambda i: (i, 0, 0)),
             pl.BlockSpec((rows, WIDTH), whole),
             pl.BlockSpec((rows, WIDTH), whole),
             pl.BlockSpec(incoming.shape, whole),
         ] + [pl.BlockSpec(own_part, whole)] * head_parts,
         out_shape=[
-            jax.ShapeDtypeStruct((steps, rows, 2 * toks), bf16),
+            jax.ShapeDtypeStruct((steps, rows, toks), bf16),
             jax.ShapeDtypeStruct((rows, WIDTH), bf16),
             jax.ShapeDtypeStruct((rows, WIDTH), bf16),
             jax.ShapeDtypeStruct(incoming.shape, bf16),
@@ -312,13 +304,14 @@
         scratch_shapes=[
             pltpu.VMEM((far_rows - LEAST_LIVE * BLK, stack), f32),
             pltpu.VMEM((token_part(tok), stack), f32),
-            pltpu.VMEM((rows, toks), f32), pltpu.VMEM((rows, toks), f32),
-            pltpu.VMEM((rows, toks), f32), pltpu.VMEM((rows, toks), f32),
-            pltpu.VMEM((rows, toks), bf16), pltpu.VMEM((rows, toks), bf16),
-            pltpu.VMEM((rows, WIDTH), f32), pltpu.VMEM((rows, WIDTH), f32),
+            pltpu.VMEM((toks, WIDTH), bf16),
+            pltpu.VMEM((rows, toks), f32),
+            pltpu.VMEM((rows, toks), f32),
+            pltpu.VMEM((rows, toks), bf16),
+            pltpu.VMEM((rows, WIDTH), f32),
             pltpu.VMEM((rows, RANK), f32),
         ],
-        compiler_params=pltpu.CompilerParams(vmem_limit_bytes=48 * MIB),
+        compiler_params=pltpu.CompilerParams(vmem_limit_bytes=60 * MIB),
         cost_estimate=pl.CostEstimate(
             flops=2 * tok * heads * rows * (2 * LATENT + 2 * RANK),
             bytes_accessed=2 * tok * heads * (LATENT + RANK + rows),
@@ -337,8 +330,8 @@
     low = LATENT - HALF
     for j in range(parts):
         n = rows - tok + (j + 1) * sub
-        even = mm(ds[0, :n, pl.ds(j * stack, stack)], keys_e[:n, :], TN) * SCALE
-        odd = mm(ds[0, :n, pl.ds((parts + j) * stack, stack)], keys_o[:n, :], TN) * SCALE
+        even = mm(ds[0, :n, pl.ds(2 * j * stack, stack)], keys_e[:n, :], TN) * SCALE
+        odd = mm(ds[0, :n, pl.ds((2 * j + 1) * stack, stack)], keys_o[:n, :], TN) * SCALE
         for i in range(PAIRS):
             at = i * 2 * LATENT
             part = slice(i * sub, (i + 1) * sub)
@@ -363,7 +356,7 @@
         ],
         out_specs=pl.BlockSpec((tok, 2 * PAIRS * LATENT), lambda i: (0, i)),
         out_shape=jax.ShapeDtypeStruct(queries.shape, queries.dtype),
-        compiler_params=pltpu.CompilerParams(vmem_limit_bytes=32 * MIB),
+        compiler_params=pltpu.CompilerParams(vmem_limit_bytes=60 * MIB),
         cost_estimate=pl.CostEstimate(
             flops=2 * tok * heads * rows * LATENT,
             bytes_accessed=2 * tok * heads * (LATENT + rows),

time: 84.2 us -> 79.8 us (0.948)
  local copies, waits for them, and re-layouts: 7.92 us -> 0.01 us
  Pallas kernels: 51.7 us -> 55 us
    unnamed x14 -> x4, local copies, waits for them, and re-layouts: 7.92 us -> 0.01 us
    pallas_call x1, Pallas kernels: 12.1 us -> 15.9 us  [query_gradients(): pl.pallas_call(query_kernel, grid=(steps,), in_specs=[pl.BlockSpec(keys_e...]
    pallas_call x1, Pallas kernels: 2.17 us -> 1 us  [finish(): pl.pallas_call(finish_kernel, out_shape=[jax.ShapeDtypeStruct(mine.shape,...]
  transfers between devices with their start and end apart: 2 -> 2, of which waited for: 0 -> 0; matrix products, arithmetic and copies ran while one was open for 0% -> 0% of each run, Pallas kernels for 14% -> 20%
where the time goes in v1:
time: 79.8 us; the launch traced here: 79.2 us
  Pallas kernels  55 us (69%)
  blocking collectives  18.6 us (23%)
  starting transfers between devices  5.02 us (6%)
    pallas_call x1, Pallas kernels, attention(): pl.pallas_call(functools.partial(attn_kernel, owned, head_parts), grid=(s...  36.1 us
    all_to_all x1, blocking collectives, local(): lax.all_to_all(outgoing.reshape(leafs, CAP * BLK, LATENT), 'leaf', split_...  18.6 us
    pallas_call x1, Pallas kernels, query_gradients(): pl.pallas_call(query_kernel, grid=(steps,), in_specs=[pl.BlockSpec(keys_e...  15.9 us
    all_to_all x1, starting transfers between devices, local(): lax.all_to_all(sent.reshape(leafs * head_parts, CAP * part_rows, LATENT),...  3.18 us
    pallas_call x1, Pallas kernels, pick(): pl.pallas_call(pick_kernel, out_shape=jax.ShapeDtypeStruct((rows, LATENT)...  1.97 us
    ppermute x1, starting transfers between devices, local(): theirs.append(lax.ppermute(part, 'head', route))  1.83 us
  transfers between devices with their start and end apart: 2, of which 0 were waited for; matrix products, arithmetic and copies ran while one was open for 0% of the time, Pallas kernels for 20%

profile of v1, /device:TPU:0, one launch (start us, length us, event | category | flops | bytes accessed | tf_op | source)
XLA Modules:
  0.0 79.2 jit_solution(9494155635240488673)
XLA Ops:
  0.6 2.0 %pick_blocks.1 = bf16[256,576]{1,0:T(8,128)(2,1)} custom-call(s32[16,32]{1,0:T(8,128)} %ancestors.5, bf16[128,576]{1,0:T(8,128)(2,1)} %bitcast.9), custom_call_target="tpu_custom_call" | custom-call | tf_op jit(solution)/shard_map/pick_blocks/pallas_call | solution.py:84
  2.6 18.6 %all_to_all.10 = bf16[16,16,576]{2,1,0:T(8,128)(2,1)} all-to-all(bf16[16,16,576]{2,1,0:T(8,128)(2,1)} %bitcast.6), channel_id=1, replica_groups=mesh['leaf'=16,'head'=2] {'leaf'}, dimensions={0} | all-to-all | bytes 589824 | tf_op jit(solution)/shard_map/all_to_all | solution.py:376
  21.2 36.1 %score_gradients.1 = (bf16[8,448,1536]{2,1,0:T(8,128)(2,1)}, bf16[448,640]{1,0:T(8,128)(2,1)}, bf16[448,640]{1,0:T(8,128)(2,1)}, bf16[256,576]{1,0:T(8,128)(2,1)}, f32[96,576]{1,0:T(8,128)}, /*index=5*/f32[96,576]{1,0:T(8,128)}) custom-call(s32[16]{0:T(128)} %anc_count.1, s32[16,32]{1,0:T(8,128)} %ancestors.5, bf16[256,576]{1,0:T(8,128)(2,1)} %bitcast.8, ...), custom_call_target="tpu_custom_call" | custom-call | flops 23957864448 | bytes 37748736 | tf_op jit(solution)/shard_map/score_gradients/pallas_call | solution.py:281
  57.2 0.0 copy-start
  57.2 0.0 copy-start.1
  57.3 3.2 %all-to-all-start.1 = ((bf16[32,8,576]{2,1,0:T(8,128)(2,1)}), bf16[32,8,576]{2,1,0:T(8,128)(2,1)S(1)}, u32[]{:S(2)}, u32[]{:S(2)}) async-start(bf16[32,8,576]{2,1,0:T(8,128)(2,1)} %bitcast.7), calls=%async_computation.1 | async-start | bytes 655360 | tf_op jit(solution)/shard_map/all_to_all | solution.py:384
  60.4 1.8 %collective-permute-start = (f32[96,576]{1,0:T(8,128)}, f32[96,576]{1,0:T(8,128)S(1)}, u32[]{:S(2)}, u32[]{:S(2)}) collective-permute-start(f32[96,576]{1,0:T(8,128)} %get-tuple-element.16), channel_id=1, source_target_pairs={{0,1},{1,0},{2,3},{3,2},{4,5},{5,4},{6,7},{7,6},{8,9},{9,8},{10,11... | collective-permute-start | bytes 663560 | tf_op jit(solution)/shard_map/ppermute | solution.py:391
  62.3 15.9 %query_gradients.1 = bf16[192,36864]{1,0:T(8,128)(2,1)} custom-call(bf16[448,640]{1,0:T(8,128)(2,1)} %get-tuple-element.11.keys_e, bf16[448,640]{1,0:T(8,128)(2,1)} %get-tuple-element.12.keys_o, bf16[8,448,1536]{2,1,0:T(8,128)(2,1)} %get-tuple-element.13.ds), custom_call_target="tpu_custom_call" | custom-call | flops 6341787648 | bytes 25165824 | tf_op jit(solution)/shard_map/query_gradients/pallas_call | solution.py:349
  78.2 0.0 collective-permute-done.rest_0_
  78.2 0.0 all-to-all-done.1
  78.2 0.0 copy-done
  78.2 0.0 copy-done.1
  78.2 1.0 %sum_gradients.1 = (f32[96,576]{1,0:T(8,128)}, f32[16,4,576]{2,1,0:T(4,128)}) custom-call(s32[16,32]{1,0:T(8,128)S(1)} %copy-done.1, bf16[256,576]{1,0:T(8,128)(2,1)S(1)} %bitcast.5, f32[96,576]{1,0:T(8,128)S(1)} %copy-done, f32[96,576]{1,0:T(8,128)S(1)} %collective-permute-done.rest_0_), custom_call_target="tpu_custom_call" | custom-call | tf_op jit(solution)/shard_map/sum_gradients/pallas_call | solution.py:107
Async XLA Ops:
  57.2 21.0 %copy-start = (f32[96,576]{1,0:T(8,128)S(1)}, f32[96,576]{1,0:T(8,128)}, u32[]{:S(2)}) copy-start(f32[96,576]{1,0:T(8,128)} %get-tuple-element.15.mine) | copy-start | bytes 663556
  57.2 21.0 %copy-start.1 = (s32[16,32]{1,0:T(8,128)S(1)}, s32[16,32]{1,0:T(8,128)}, u32[]{:S(2)}) copy-start(s32[16,32]{1,0:T(8,128)} %ancestors.5) | copy-start | bytes 6148
  57.3 20.9 %all-to-all-start.1 = ((bf16[32,8,576]{2,1,0:T(8,128)(2,1)}), bf16[32,8,576]{2,1,0:T(8,128)(2,1)S(1)}, u32[]{:S(2)}, u32[]{:S(2)}) async-start(bf16[32,8,576]{2,1,0:T(8,128)(2,1)} %bitcast.7), calls=%async_computation.1 | async-start | bytes 655360 | tf_op jit(solution)/shard_map/all_to_all | solution.py:384
  60.4 17.8 %collective-permute-start = (f32[96,576]{1,0:T(8,128)}, f32[96,576]{1,0:T(8,128)S(1)}, u32[]{:S(2)}, u32[]{:S(2)}) collective-permute-start(f32[96,576]{1,0:T(8,128)} %get-tuple-element.16), channel_id=1, source_target_pairs={{0,1},{1,0},{2,3},{3,2},{4,5},{5,4},{6,7},{7,6},{8,9},{9,8},{10,11... | collective-permute-start | bytes 663560 | tf_op jit(solution)/shard_map/ppermute | solution.py:391

commit v2 on v1

--- a/solution.py
+++ b/solution.py
@@ -132,7 +132,7 @@
     owned, head_parts, anc_count, ancestors, incoming, own, q, do, ds, keys_e, keys_o, sent, *rest
 ):
     own_parts = rest[:head_parts]
-    far_bias, causal, q_st, s, dp, p_low, acc_k, acc_v = rest[head_parts:]
+    far_bias, causal, q_st, s, dp, p_low, tops, acc_k, acc_v = rest[head_parts:]
     tok = q.shape[0]
     far_rows, rows = ANC * BLK, ANC * BLK + tok
     sub = token_part(tok)
@@ -153,8 +153,8 @@
         live = anc_count[lax.axis_index("leaf")]
         slot = div(lax.broadcasted_iota(jnp.int32, far_bias.shape, 0) + least, BLK)
         far_bias[...] = jnp.where(slot < live, 0.0, MASKED)
-        key_at = lax.broadcasted_iota(jnp.int32, (sub, stack), 0)
-        tok_at = mod(lax.broadcasted_iota(jnp.int32, (sub, stack), 1), sub)
+        key_at = lax.broadcasted_iota(jnp.int32, causal.shape, 0)
+        tok_at = mod(lax.broadcasted_iota(jnp.int32, causal.shape, 1), sub)
         causal[...] = jnp.where(key_at <= tok_at, 0.0, MASKED)
         acc_k[...] = jnp.zeros_like(acc_k)
         acc_v[...] = jnp.zeros_like(acc_v)
@@ -174,68 +174,80 @@
             odd = pltpu.roll(odd, WIDTH - HALF, axis=1)
             q_st[pl.ds(j * stack + (PAIRS + i) * sub, sub), :] = odd
 
-    def grads(j):
+    heads = list(range(0, 2 * PAIRS, 2)) + list(range(1, 2 * PAIRS, 2))
+
+    def grads(j, first, count, at=0, size=RANK):
         toks = pl.ds(j * sub, sub)
-        heads = list(range(0, 2 * PAIRS, 2)) + list(range(1, 2 * PAIRS, 2))
-        return jnp.concatenate([do[toks, pl.ds(h * RANK, RANK)] for h in heads], axis=0)
-
-    def score(j):
-        n, cols = seen(j), lanes(j)
+        cols = [pl.ds(h * RANK + at, size) for h in heads[first:first + count]]
+        return jnp.concatenate([do[toks, c] for c in cols], axis=0)
+
+    def fold(x):
+        return x.reshape(-1, 8, x.shape[1])
+
+    def score(j, at):
+        n, cols = seen(j), pl.ds(j * stack + at, stack // 2)
         out = mm(keys_e[:n, :], q_st[cols, :], NT)
-        s[:least, cols] = out[:least]
-        s[least:far_rows, cols] = out[least:far_rows] + far_bias[...]
+        near = [(0, out[:least]), (least, out[least:far_rows] + far_bias[...])]
         if j > 0:
-            s[far_rows:n - sub, cols] = out[far_rows:n - sub]
-        s[n - sub:n, cols] = out[n - sub:] + causal[...]
-
-    def prob(j):
-        n = seen(j)
-        dp[:n, lanes(j)] = mm(keys_e[:n, :RANK], grads(j), NT)
-
-    def soft(j, at):
+            near.append((far_rows, out[far_rows:n - sub]))
+        near.append((n - sub, out[n - sub:] + causal[...]))
+        top = None
+        for r, part in near:
+            s[pl.ds(r, part.shape[0]), cols] = part
+            part = jnp.max(fold(part), axis=0)
+            top = part if top is None else jnp.maximum(top, part)
+        tops[:, cols] = top
+
+    def prob(j, at):
+        n, cols = seen(j), pl.ds(j * stack + at, stack // 2)
+        dp[:n, cols] = mm(keys_e[:n, :RANK], grads(j, at // sub, PAIRS), NT)
+
+    state = {}
+
+    def soft_sums(j, at):
         lane = pl.ds(j * stack + at, LANES)
-        chunks = pieces(seen(j), 64)
-
-        def fold(x):
-            return x.reshape(-1, 8, LANES)
-
-        top = None
-        for r, n in chunks:
-            part = jnp.max(fold(s[pl.ds(r, n), lane]), axis=0)
-            top = part if top is None else jnp.maximum(top, part)
-        top = jnp.max(top, axis=0, keepdims=True)
+        top = jnp.max(tops[:, lane], axis=0, keepdims=True)
         total = jnp.zeros((8, LANES), jnp.float32)
         delta = jnp.zeros((8, LANES), jnp.float32)
-        for r, n in chunks:
+        for r, n in pieces(seen(j), 64):
             e = jnp.exp2((s[pl.ds(r, n), lane] - top) * EXP_SCALE)
             s[pl.ds(r, n), lane] = e
             total += jnp.sum(fold(e), axis=0)
             delta += jnp.sum(fold(e * dp[pl.ds(r, n), lane]), axis=0)
         inv = 1.0 / jnp.sum(total, axis=0, keepdims=True)
-        delta = jnp.sum(delta, axis=0, keepdims=True) * inv
-        for r, n in chunks:
+        state[j, at] = inv, jnp.sum(delta, axis=0, keepdims=True) * inv
+
+    def soft_outs(j, at):
+        lane = pl.ds(j * stack + at, LANES)
+        inv, delta = state.pop((j, at))
+        for r, n in pieces(seen(j), 64):
             p = s[pl.ds(r, n), lane] * inv
             p_low[pl.ds(r, n), lane] = p.astype(jnp.bfloat16)
             ds[0, pl.ds(r, n), lane] = (p * (dp[pl.ds(r, n), lane] - delta)).astype(ds.dtype)
 
-    def grad_values(j):
-        n = seen(j)
-        acc_v[:n, :] += mm(p_low[:n, lanes(j)], grads(j), NN)
-
-    def grad_keys(j):
-        n = seen(j)
-        acc_k[:n, :] += mm(ds[0, :n, lanes(j)], q_st[lanes(j), :], NN)
+    def grad_values(j, at, size):
+        n, cols = seen(j), pl.ds(at, size)
+        acc_v[:n, cols] += mm(p_low[:n, lanes(j)], grads(j, 0, 2 * PAIRS, at, size), NN)
+
+    def grad_keys(j, at, size):
+        n, cols = seen(j), pl.ds(at, size)
+        acc_k[:n, cols] += mm(ds[0, :n, lanes(j)], q_st[lanes(j), cols], NN)
 
     def jobs_of(i):
-        groups = []
+        products, passes = [], []
         if i < parts:
-            groups.append([functools.partial(job, i) for job in (fill, score, prob)])
+            products += [functools.partial(fill, i)]
+            for at in (0, stack // 2):
+                products += [functools.partial(score, i, at), functools.partial(prob, i, at)]
+        if 0 <= i - 2 < parts:
+            products += [functools.partial(grad_values, i - 2, *c) for c in pieces(RANK, 256)]
+            products += [functools.partial(grad_keys, i - 2, *c) for c in pieces(WIDTH, 256)]
         if 0 <= i - 1 < parts:
-            groups.append([functools.partial(soft, i - 1, at) for at in range(0, stack, LANES)])
-        if 0 <= i - 2 < parts:
-            groups.append([functools.partial(job, i - 2) for job in (grad_values, grad_keys)])
+            for at in range(0, stack, LANES):
+                passes += [functools.partial(job, i - 1, at) for job in (soft_sums, soft_outs)]
         order = [
-            (k / len(group), g, job) for g, group in enumerate(groups) for k, job in enumerate(group)
+            (k / len(group), g, job)
+            for g, group in enumerate((products, passes)) for k, job in enumerate(group)
         ]
         return [job for _, _, job in sorted(order, key=lambda item: item[:2])]
 
@@ -302,16 +314,17 @@
             jax.ShapeDtypeStruct(incoming.shape, bf16),
         ] + [jax.ShapeDtypeStruct(own_part, f32)] * head_parts,
         scratch_shapes=[
-            pltpu.VMEM((far_rows - LEAST_LIVE * BLK, stack), f32),
-            pltpu.VMEM((token_part(tok), stack), f32),
+            pltpu.VMEM((far_rows - LEAST_LIVE * BLK, stack // 2), f32),
+            pltpu.VMEM((token_part(tok), stack // 2), f32),
             pltpu.VMEM((toks, WIDTH), bf16),
             pltpu.VMEM((rows, toks), f32),
             pltpu.VMEM((rows, toks), f32),
             pltpu.VMEM((rows, toks), bf16),
+            pltpu.VMEM((8, toks), f32),
             pltpu.VMEM((rows, WIDTH), f32),
             pltpu.VMEM((rows, RANK), f32),
         ],
-        compiler_params=pltpu.CompilerParams(vmem_limit_bytes=60 * MIB),
+        compiler_params=pltpu.CompilerParams(vmem_limit_bytes=36 * MIB),
         cost_estimate=pl.CostEstimate(
             flops=2 * tok * heads * rows * (2 * LATENT + 2 * RANK),
             bytes_accessed=2 * tok * heads * (LATENT + RANK + rows),
@@ -356,7 +369,7 @@
         ],
         out_specs=pl.BlockSpec((tok, 2 * PAIRS * LATENT), lambda i: (0, i)),
         out_shape=jax.ShapeDtypeStruct(queries.shape, queries.dtype),
-        compiler_params=pltpu.CompilerParams(vmem_limit_bytes=60 * MIB),
+        compiler_params=pltpu.CompilerParams(vmem_limit_bytes=16 * MIB),
         cost_estimate=pl.CostEstimate(
             flops=2 * tok * heads * rows * LATENT,
             bytes_accessed=2 * tok * heads * (LATENT + rows),

time: 79.8 us -> 85.7 us (1.074)
  local copies, waits for them, and re-layouts: 0.01 us -> 10.7 us
  Pallas kernels: 55 us -> 50.5 us
    unnamed x4 -> x12, local copies, waits for them, and re-layouts: 0.01 us -> 10.7 us
    pallas_call x1, Pallas kernels: 15.9 us -> 12.1 us  [query_gradients(): pl.pallas_call(query_kernel, grid=(steps,), in_specs=[pl.BlockSpec(keys_e...]
  transfers between devices with their start and end apart: 2 -> 2, of which waited for: 0 -> 0; matrix products, arithmetic and copies ran while one was open for 0% -> 0% of each run, Pallas kernels for 20% -> 14%
where the time goes in v2:
time: 85.7 us; the launch traced here: 85.3 us
  Pallas kernels  50.5 us (59%)
  blocking collectives  18.5 us (22%)
  local copies, waits for them, and re-layouts  10.7 us (12%)
  starting transfers between devices  5.01 us (6%)
    pallas_call x1, Pallas kernels, attention(): pl.pallas_call(functools.partial(attn_kernel, owned, head_parts), grid=(s...  35.4 us
    all_to_all x1, blocking collectives, local(): lax.all_to_all(outgoing.reshape(leafs, CAP * BLK, LATENT), 'leaf', split_...  18.5 us
    pallas_call x1, Pallas kernels, query_gradients(): pl.pallas_call(query_kernel, grid=(steps,), in_specs=[pl.BlockSpec(keys_e...  12.1 us
    unnamed x12, local copies, waits for them, and re-layouts  10.7 us
    all_to_all x1, starting transfers between devices, local(): lax.all_to_all(sent.reshape(leafs * head_parts, CAP * part_rows, LATENT),...  3.18 us
    pallas_call x1, Pallas kernels, pick(): pl.pallas_call(pick_kernel, out_shape=jax.ShapeDtypeStruct((rows, LATENT)...  1.97 us
    ppermute x1, starting transfers between devices, local(): theirs.append(lax.ppermute(part, 'head', route))  1.83 us
  transfers between devices with their start and end apart: 2, of which 0 were waited for; matrix products, arithmetic and copies ran while one was open for 0% of the time, Pallas kernels for 14%

profile of v2, /device:TPU:0, one launch (start us, length us, event | category | flops | bytes accessed | tf_op | source)
XLA Modules:
  0.0 85.3 jit_solution(6698725246368626433)
XLA Ops:
  0.6 2.0 %pick_blocks.1 = bf16[256,576]{1,0:T(8,128)(2,1)} custom-call(s32[16,32]{1,0:T(8,128)} %ancestors.5, bf16[128,576]{1,0:T(8,128)(2,1)} %bitcast.8), custom_call_target="tpu_custom_call" | custom-call | tf_op jit(solution)/shard_map/pick_blocks/pallas_call | solution.py:84
  2.6 18.5 %all_to_all.10 = bf16[16,16,576]{2,1,0:T(8,128)(2,1)S(1)} all-to-all(bf16[16,16,576]{2,1,0:T(8,128)(2,1)} %bitcast.7), channel_id=1, replica_groups=mesh['leaf'=16,'head'=2] {'leaf'}, dimensions={0} | all-to-all | bytes 589824 | tf_op jit(solution)/shard_map/all_to_all | solution.py:389
  21.1 0.0 copy-start.2
  21.1 0.7 copy-done.2
  21.8 0.0 copy-start.4
  21.8 0.9 %copy-done.4 = bf16[192,576]{1,0:T(8,128)(2,1)S(1)} copy-done((bf16[192,576]{1,0:T(8,128)(2,1)S(1)}, bf16[192,576]{1,0:T(8,128)(2,1)}, u32[]{:S(2)}) %copy-start.4) | copy-done | bytes 221208
  22.7 0.0 copy-start.5
  22.7 0.7 copy-done.5
  23.4 35.4 %score_gradients.1 = (bf16[8,448,1536]{2,1,0:T(8,128)(2,1)S(1)}, bf16[448,640]{1,0:T(8,128)(2,1)S(1)}, bf16[448,640]{1,0:T(8,128)(2,1)S(1)}, bf16[256,576]{1,0:T...) custom-call(s32[16]{0:T(128)S(1)} %copy-done.5, s32[16,32]{1,0:T(8,128)S(1)} %copy-done.2, ...), custom_call_target="tpu_custom_call" | custom-call | flops 23957864448 | bytes 37748736 | tf_op jit(solution)/shard_map/score_gradients/pallas_call | solution.py:293
  58.8 0.0 copy-start
  58.8 4.3 %copy-done = bf16[8,448,1536]{2,1,0:T(8,128)(2,1)} copy-done((bf16[8,448,1536]{2,1,0:T(8,128)(2,1)}, bf16[8,448,1536]{2,1,0:T(8,128)(2,1)S(1)}, u32[]{:S(2)}) %copy-start) | copy-done | bytes 11010072
  63.0 0.0 copy-start.3
  63.0 3.2 %all-to-all-start.1 = ((bf16[32,8,576]{2,1,0:T(8,128)(2,1)}), bf16[32,8,576]{2,1,0:T(8,128)(2,1)S(1)}, u32[]{:S(2)}, u32[]{:S(2)}) async-start(bf16[32,8,576]{2,1,0:T(8,128)(2,1)} %bitcast.3), calls=%async_computation.1 | async-start | bytes 655360 | tf_op jit(solution)/shard_map/all_to_all | solution.py:397
  66.2 1.8 %collective-permute-start = (f32[96,576]{1,0:T(8,128)S(1)}, f32[96,576]{1,0:T(8,128)S(1)}, u32[]{:S(2)}, u32[]{:S(2)}) collective-permute-start(f32[96,576]{1,0:T(8,128)S(1)} %get-tuple-element.16), channel_id=1, source_target_pairs={{0,1},{1,0},{2,3},{3,2},{4,5},{5,4},{6,7},{7,6},{8,9},{9,8},{10,11... | collective-permute-start | bytes 663560 | tf_op jit(solution)/shard_map/ppermute | solution.py:404
  68.0 0.0 copy-start.1
  68.1 4.1 %copy-done.1 = bf16[8,448,1536]{2,1,0:T(8,128)(2,1)S(1)} copy-done((bf16[8,448,1536]{2,1,0:T(8,128)(2,1)S(1)}, bf16[8,448,1536]{2,1,0:T(8,128)(2,1)}, u32[]{:S(2)}) %copy-start.1) | copy-done | bytes 11010072
  72.2 12.1 %query_gradients.1 = bf16[192,36864]{1,0:T(8,128)(2,1)} custom-call(bf16[448,640]{1,0:T(8,128)(2,1)S(1)} %get-tuple-element.11.keys_e, bf16[448,640]{1,0:T(8,128)(2,1)S(1)} %get-tuple-element.12.keys_o, bf16[8,448,1536]{2,1,0:T(8,128)(2,1)S(1)} %copy-done.1), custom_call_target="tpu_custom_call" | custom-call | flops 6341787648 | bytes 25165824 | tf_op jit(solution)/shard_map/query_gradients/pallas_call | solution.py:362
  84.3 0.0 collective-permute-done.rest_0_
  84.3 0.0 all-to-all-done.1
  84.3 0.0 copy-done.3
  84.3 1.0 %sum_gradients.1 = (f32[96,576]{1,0:T(8,128)}, f32[16,4,576]{2,1,0:T(4,128)}) custom-call(s32[16,32]{1,0:T(8,128)S(1)} %copy-done.3, bf16[256,576]{1,0:T(8,128)(2,1)S(1)} %bitcast.5, f32[96,576]{1,0:T(8,128)S(1)} %get-tuple-element.15.mine, f32[96,576]{1,0:T(8,128)S(1)} %collective-permute-done.rest_0_), custom_call_target="tpu_custom_call" | custom-call | tf_op jit(solution)/shard_map/sum_gradients/pallas_call | solution.py:107
Async XLA Ops:
  21.1 0.7 copy-start.2
  21.8 0.9 %copy-start.4 = (bf16[192,576]{1,0:T(8,128)(2,1)S(1)}, bf16[192,576]{1,0:T(8,128)(2,1)}, u32[]{:S(2)}) copy-start(bf16[192,576]{1,0:T(8,128)(2,1)} %own.1) | copy-start | bytes 663556
  22.7 0.7 copy-start.5
  58.8 4.3 %copy-start = (bf16[8,448,1536]{2,1,0:T(8,128)(2,1)}, bf16[8,448,1536]{2,1,0:T(8,128)(2,1)S(1)}, u32[]{:S(2)}) copy-start(bf16[8,448,1536]{2,1,0:T(8,128)(2,1)S(1)} %get-tuple-element.13.ds) | copy-start | bytes 33030148
  63.0 21.3 %copy-start.3 = (s32[16,32]{1,0:T(8,128)S(1)}, s32[16,32]{1,0:T(8,128)}, u32[]{:S(2)}) copy-start(s32[16,32]{1,0:T(8,128)} %ancestors.5) | copy-start | bytes 6148
  63.0 21.3 %all-to-all-start.1 = ((bf16[32,8,576]{2,1,0:T(8,128)(2,1)}), bf16[32,8,576]{2,1,0:T(8,128)(2,1)S(1)}, u32[]{:S(2)}, u32[]{:S(2)}) async-start(bf16[32,8,576]{2,1,0:T(8,128)(2,1)} %bitcast.3), calls=%async_computation.1 | async-start | bytes 655360 | tf_op jit(solution)/shard_map/all_to_all | solution.py:397
  66.2 18.1 %collective-permute-start = (f32[96,576]{1,0:T(8,128)S(1)}, f32[96,576]{1,0:T(8,128)S(1)}, u32[]{:S(2)}, u32[]{:S(2)}) collective-permute-start(f32[96,576]{1,0:T(8,128)S(1)} %get-tuple-element.16), channel_id=1, source_target_pairs={{0,1},{1,0},{2,3},{3,2},{4,5},{5,4},{6,7},{7,6},{8,9},{9,8},{10,11... | collective-permute-start | bytes 663560 | tf_op jit(solution)/shard_map/ppermute | solution.py:404
  68.0 4.1 %copy-start.1 = (bf16[8,448,1536]{2,1,0:T(8,128)(2,1)S(1)}, bf16[8,448,1536]{2,1,0:T(8,128)(2,1)}, u32[]{:S(2)}) copy-start(bf16[8,448,1536]{2,1,0:T(8,128)(2,1)} %copy-done) | copy-start | bytes 33030148

commit v3 on v1

v3 whole, which is shorter than its diff:
```python
import functools
import math

import jax
import jax.numpy as jnp
from jax import lax
from jax.experimental import pallas as pl
from jax.experimental.pallas import tpu as pltpu
from jax.sharding import PartitionSpec as P

RANK = 512
QK_HEAD = 192
LATENT = 576
BLK = 8
CAP = 2
ANC = 32
LANES = 128
WIDTH = 640
HALF = WIDTH - LATENT
PAIRS = 4
MASKED = -1e30
FAR_OFF = 1 << 20
SCALE = float(QK_HEAD) ** -0.5
EXP_SCALE = SCALE * math.log2(math.e)
MIB = 1024 * 1024
NT = (((1,), (1,)), ((), ()))
NN = (((1,), (0,)), ((), ()))
TN = (((0,), (0,)), ((), ()))


def mm(a, b, dims):
    return lax.dot_general(a, b, dims, preferred_element_type=jnp.float32)


def pieces(total, size):
    return [(at, min(size, total - at)) for at in range(0, total, size)]


def div(x, n):
    return x >> (n.bit_length() - 1) if n & (n - 1) == 0 else lax.div(x, jnp.full_like(x, n))


def mod(x, n):
    return x - div(x, n) * n


def column(rows):
    return lax.broadcasted_iota(jnp.int32, (rows, 1), 0)


def one_hot(place, size):
    lane = lax.broadcasted_iota(jnp.int32, (place.shape[0], size), 1)
    return jnp.where(lane == place, 1.0, 0.0).astype(jnp.bfloat16)


def token_part(tok):
    return 64 if tok % 64 == 0 else tok


def listed_blocks(ancestors, owned, second):
    leafs = ancestors.shape[0]
    rows = leafs * CAP * BLK
    named = ancestors[...].astype(jnp.float32)
    named = jnp.broadcast_to(named[:, None, :], (leafs, CAP * BLK, ANC)).reshape(rows, ANC)
    first = lax.axis_index("leaf") * owned
    low_end = first.astype(jnp.float32)
    mine = (named >= low_end) & (named < low_end + owned)
    low = jnp.min(jnp.where(mine, named, float(FAR_OFF)), axis=1, keepdims=True)
    high = jnp.max(jnp.where(mine, named, -1.0), axis=1, keepdims=True)
    return jnp.where(second, high, low).astype(jnp.int32) - first


def pick_kernel(ancestors, trunk, out):
    owned = trunk.shape[0] // BLK
    row = column(out.shape[0])
    block = listed_blocks(ancestors, owned, mod(div(row, BLK), CAP) == 1)
    sel = one_hot(block * BLK + mod(row, BLK), trunk.shape[0])
    out[...] = mm(sel, trunk[...], NN).astype(out.dtype)


def pick(ancestors, trunk):
    rows = ancestors.shape[0] * CAP * BLK
    return pl.pallas_call(
        pick_kernel,
        out_shape=jax.ShapeDtypeStruct((rows, LATENT), trunk.dtype),
        name="pick_blocks",
    )(ancestors, trunk)


def finish_kernel(ancestors, got, mine, *rest):
    theirs, (d_branch, d_trunk) = rest[:-2], rest[-2:]
    owned, part_rows = d_trunk.shape[0], d_trunk.shape[1]
    row = column(got.shape[0])
    block = listed_blocks(ancestors, owned, mod(div(row, part_rows), CAP) == 1)
    sel = one_hot(block * part_rows + mod(row, part_rows), owned * part_rows)
    total = mm(sel, got[...], TN)
    for b in range(owned):
        d_trunk[b] = total[b * part_rows:(b + 1) * part_rows]
    own = mine[...]
    for other in theirs:
        own = own + other[...]
    d_branch[...] = own


def finish(ancestors, got, mine, theirs, owned, part_rows):
    return pl.pallas_call(
        finish_kernel,
        out_shape=[
            jax.ShapeDtypeStruct(mine.shape, jnp.float32),
            jax.ShapeDtypeStruct((owned, part_rows, LATENT), jnp.float32),
        ],
        compiler_params=pltpu.CompilerParams(vmem_limit_bytes=8 * MIB),
        name="sum_gradients",
    )(ancestors, got, mine, *theirs)


def slot_places(ancestors, owned):
    row = column(ANC * BLK)
    mine = ancestors[pl.ds(lax.axis_index("leaf"), 1), :].astype(jnp.float32)
    mine = jnp.broadcast_to(mine, (ANC * BLK, ANC))
    lane = lax.broadcasted_iota(jnp.int32, (ANC * BLK, ANC), 1)
    block = jnp.max(jnp.where(lane == div(row, BLK), mine, -1.0), axis=1, keepdims=True)
    owner = div(block.astype(jnp.int32), owned)
    low_end = (owner * owned).astype(jnp.float32)
    below = (mine >= low_end) & (mine < block)
    second = jnp.max(jnp.where(below, 1.0, 0.0), axis=1, keepdims=True).astype(jnp.int32)
    return row, owner, second


def attn_kernel(
    owned, head_parts, ahead, anc_count, ancestors, incoming, own, q, do, dq, ds, keys_e, keys_o, sent,
    *rest
):
    own_parts = rest[:head_parts]
    scratch = rest[head_parts:]
    bias, cols_e, cols_o, s_e, s_o, dp_e, dp_o, p_e, p_o, d_e, d_o, acc_e, acc_o, acc_v = scratch
    tok = q.shape[0]
    far_rows, rows = ANC * BLK, ANC * BLK + tok
    lanes = keys_e.shape[0]
    sub = token_part(tok)
    parts = tok // sub
    step = pl.program_id(0)

    @pl.when(step == 0)
    def _():
        row, owner, second = slot_places(ancestors, owned)
        sel = one_hot((owner * CAP + second) * BLK + mod(row, BLK), incoming.shape[0])
        far = mm(sel, incoming[...], NN)
        joined = jnp.concatenate([far, own[...].astype(jnp.float32)], axis=0)
        padded = jnp.concatenate([joined, jnp.zeros((rows, HALF), jnp.float32)], axis=1)
        if lanes > rows:
            padded = jnp.concatenate([padded, jnp.zeros((lanes - rows, WIDTH), jnp.float32)], axis=0)
        keys_e[...] = padded.astype(jnp.bfloat16)
        cols_e[...] = padded.T.astype(jnp.bfloat16)
        moved = pltpu.roll(padded, HALF, axis=1)
        keys_o[...] = moved.astype(jnp.bfloat16)
        cols_o[...] = moved.T.astype(jnp.bfloat16)
        live = anc_count[lax.axis_index("leaf")]
        key_at = lax.broadcasted_iota(jnp.int32, bias.shape, 1)
        tok_at = lax.broadcasted_iota(jnp.int32, bias.shape, 0)
        far_ok = (key_at < far_rows) & (key_at < live * BLK)
        own_ok = (key_at >= far_rows) & (key_at - far_rows <= tok_at)
        bias[...] = jnp.where(far_ok | own_ok, 0.0, MASKED)
        acc_e[...] = jnp.zeros_like(acc_e)
        acc_o[...] = jnp.zeros_like(acc_o)
        acc_v[...] = jnp.zeros_like(acc_v)

    keys, cols = (keys_e, keys_o), (cols_e, cols_o)
    s_st, dp_st, p_st, d_st, accs = (s_e, s_o), (dp_e, dp_o), (p_e, p_o), (d_e, d_o), (acc_e, acc_o)

    def seen(j):
        return far_rows + (j + 1) * sub

    def seen_lanes(j):
        return -(-seen(j) // LANES) * LANES

    def head_queries(par, pair, toks):
        return q[toks, pl.ds(pair * 2 * LATENT + par * (LATENT - HALF), WIDTH)]

    def head_grads(par, pair, toks):
        return do[toks, pl.ds((2 * pair + par) * RANK, RANK)]

    def stacked(of, par, toks):
        return jnp.concatenate([of(par, pair, toks) for pair in range(PAIRS)], axis=0)

    every = slice(0, tok)

    def put(to, out, at, plus=None):
        size = out.shape[1]
        for pair in range(PAIRS):
            for j in range(parts):
                n = min(size, seen_lanes(j) - at)
                if n > 0:
                    r = pair * tok + j * sub
                    kept = out[r:r + sub, :n]
                    if plus is not None:
                        kept = kept + plus[j * sub:(j + 1) * sub, at:at + n]
                    to[r:r + sub, at:at + n] = kept

    def score(par, at, size):
        out = mm(stacked(head_queries, par, every), cols[par][:, at:at + size], NN)
        put(s_st[par], out, at, bias)

    def prob(par, at, size):
        out = mm(stacked(head_grads, par, every), cols_e[:RANK, at:at + size], NN)
        put(dp_st[par], out, at)

    def soft(par, pair, j, half):
        n, size = seen_lanes(j), sub // 2
        block = pl.ds(pair * tok + j * sub + half * size, size)
        s, dp = s_st[par][block, :n], dp_st[par][block, :n]
        top = jnp.max(s, axis=1, keepdims=True)
        e = jnp.exp2((s - top) * EXP_SCALE)
        inv = 1.0 / jnp.sum(e, axis=1, keepdims=True)
        delta = jnp.sum(e * dp, axis=1, keepdims=True) * inv
        p = e * inv
        p_st[par][block, :n] = p.astype(jnp.bfloat16)
        d_st[par][block, :n] = (p * (dp - delta)).astype(jnp.bfloat16)
        if n < lanes:
            d_st[par][block, n:] = jnp.zeros((size, lanes - n), jnp.bfloat16)

    def turned(ref, j):
        blocks = [ref[pl.ds(pair * tok + j * sub, sub), :seen_lanes(j)] for pair in range(PAIRS)]
        return jnp.concatenate(blocks, axis=0).T[:seen(j)]

    def grad_values(par, j):
        toks = pl.ds(j * sub, sub)
        acc_v[:seen(j), :] += mm(turned(p_st[par], j), stacked(head_grads, par, toks), NN)

    def grad_keys(par, j):
        toks = pl.ds(j * sub, sub)
        accs[par][:seen(j), :] += mm(turned(d_st[par], j), stacked(head_queries, par, toks), NN)

    def scores(par):
        jobs = []
        for piece in pieces(lanes, 256):
            jobs += [functools.partial(score, par, *piece), functools.partial(prob, par, *piece)]
        return jobs

    def softs(par):
        blocks = [(pair, j, half) for pair in range(PAIRS) for j in range(parts) for half in range(2)]
        return [functools.partial(soft, par, *block) for block in blocks]

    def grads(par):
        jobs = []
        for j in range(parts):
            jobs += [functools.partial(grad_values, par, j), functools.partial(grad_keys, par, j)]
        return jobs

    def together(*groups):
        order = [
            (k / len(group), g, job) for g, group in enumerate(groups) for k, job in enumerate(group)
        ]
        for _, _, job in sorted(order, key=lambda item: item[:2]):
            job()

    together(scores(0))
    together(scores(1), softs(0))
    together(grads(0), softs(1))
    together(grads(1))

    @pl.when(step < ahead)
    def _():
        put_queries(dq, d_e[...], d_o[...], keys_e[...], keys_o[...])

    @pl.when(step >= ahead)
    def _():
        ds[0, 0] = d_e[...]
        ds[0, 1] = d_o[...]

    @pl.when(step == pl.num_programs(0) - 1)
    def _():
        shifted = pltpu.roll(acc_o[...], WIDTH - HALF, axis=1)
        acc_e[...] = (acc_e[...] + shifted) * SCALE
        acc_e[:, :RANK] += acc_v[...]
        part_rows = BLK // head_parts
        row, owner, second = slot_places(ancestors, owned)
        inner = mod(row, BLK)
        place = (owner * head_parts + div(inner, part_rows)) * CAP + second
        place = place * part_rows + mod(inner, part_rows)
        sel = one_hot(place, sent.shape[0])
        far = acc_e[:far_rows, :LATENT].astype(jnp.bfloat16)
        sent[...] = mm(sel, far, TN).astype(sent.dtype)
        own_rows = tok // head_parts
        for hop, out in enumerate(own_parts):
            part = lax.rem(lax.axis_index("head") + hop, head_parts)
            at = pl.multiple_of(far_rows + part * own_rows, 8)
            out[...] = acc_e[pl.ds(at, own_rows), :LATENT]


def put_queries(dq, even, odd, keys_e, keys_o):
    tok = dq.shape[0]
    low = LATENT - HALF
    even = mm(even, keys_e, NN) * SCALE
    odd = mm(odd, keys_o, NN) * SCALE
    for pair in range(PAIRS):
        at, part = pair * 2 * LATENT, slice(pair * tok, (pair + 1) * tok)
        dq[:, at:at + low] = even[part, :low].astype(dq.dtype)
        joint = even[part, low:] + odd[part, :2 * HALF]
        dq[:, at + low:at + low + 2 * HALF] = joint.astype(dq.dtype)
        dq[:, at + low + 2 * HALF:at + 2 * LATENT] = odd[part, 2 * HALF:].astype(dq.dtype)


def steps_ahead(steps):
    return steps * 3 // 8


def attention(owned, head_parts, anc_count, ancestors, incoming, own, queries, d_out):
    tok = queries.shape[0]
    heads = queries.shape[1] // LATENT
    steps = heads // (2 * PAIRS)
    ahead = steps_ahead(steps)
    far_rows, rows = ANC * BLK, ANC * BLK + tok
    lanes = -(-rows // LANES) * LANES
    toks = PAIRS * tok
    bf16, f32 = jnp.bfloat16, jnp.float32

    def whole(i):
        return (0, 0)

    def along(i):
        return (0, i)

    own_part = (tok // head_parts, LATENT)
    pair_of = lambda shape, dtype: [pltpu.VMEM(shape, dtype)] * 2
    return pl.pallas_call(
        functools.partial(attn_kernel, owned, head_parts, ahead),
        grid=(steps,),
        in_specs=[
            pl.BlockSpec(memory_space=pltpu.SMEM),
            pl.BlockSpec(ancestors.shape, whole),
            pl.BlockSpec(incoming.shape, whole),
            pl.BlockSpec(own.shape, whole),
            pl.BlockSpec((tok, 2 * PAIRS * LATENT), along),
            pl.BlockSpec((tok, 2 * PAIRS * RANK), along),
        ],
        out_specs=[
            pl.BlockSpec(
                (tok, 2 * PAIRS * LATENT), lambda i: (0, jnp.minimum(i, max(ahead - 1, 0)))
            ),
            pl.BlockSpec((1, 2, toks, lanes), lambda i: (jnp.maximum(i - ahead, 0), 0, 0, 0)),
            pl.BlockSpec((lanes, WIDTH), whole),
            pl.BlockSpec((lanes, WIDTH), whole),
            pl.BlockSpec(incoming.shape, whole),
        ] + [pl.BlockSpec(own_part, whole)] * head_parts,
        out_shape=[
            jax.ShapeDtypeStruct(queries.shape, bf16),
            jax.ShapeDtypeStruct((steps - ahead, 2, toks, lanes), bf16),
            jax.ShapeDtypeStruct((lanes, WIDTH), bf16),
            jax.ShapeDtypeStruct((lanes, WIDTH), bf16),
            jax.ShapeDtypeStruct(incoming.shape, bf16),
        ] + [jax.ShapeDtypeStruct(own_part, f32)] * head_parts,
        scratch_shapes=[pltpu.VMEM((tok, lanes), f32)]
        + pair_of((WIDTH, lanes), bf16)
        + pair_of((toks, lanes), f32)
        + pair_of((toks, lanes), f32)
        + pair_of((toks, lanes), bf16)
        + pair_of((toks, lanes), bf16)
        + pair_of((rows, WIDTH), f32)
        + [pltpu.VMEM((rows, RANK), f32)],
        compiler_params=pltpu.CompilerParams(vmem_limit_bytes=60 * MIB),
        cost_estimate=pl.CostEstimate(
            flops=2 * tok * heads * rows * (2 * LATENT + 2 * RANK),
            bytes_accessed=2 * tok * heads * (LATENT + RANK + rows),
            transcendentals=tok * heads * rows,
        ),
        name="score_gradients",
    )(anc_count, ancestors, incoming, own, queries, d_out)


def query_kernel(keys_e, keys_o, ds, started, dq):
    put_queries(dq, ds[0, 0], ds[0, 1], keys_e[...], keys_o[...])


def query_gradients(keys_e, keys_o, ds, started):
    tok = started.shape[0]
    steps = ds.shape[0]
    ahead = started.shape[1] // (2 * PAIRS * LATENT) - steps
    rows = ds.shape[3]
    return pl.pallas_call(
        query_kernel,
        grid=(steps,),
        in_specs=[
            pl.BlockSpec(keys_e.shape, lambda i: (0, 0)),
            pl.BlockSpec(keys_o.shape, lambda i: (0, 0)),
            pl.BlockSpec((1,) + ds.shape[1:], lambda i: (i, 0, 0, 0)),
            pl.BlockSpec(memory_space=pl.ANY),
        ],
        out_specs=pl.BlockSpec((tok, 2 * PAIRS * LATENT), lambda i: (0, i + ahead)),
        out_shape=jax.ShapeDtypeStruct(started.shape, started.dtype),
        input_output_aliases={3: 0},
        compiler_params=pltpu.CompilerParams(vmem_limit_bytes=60 * MIB),
        cost_estimate=pl.CostEstimate(
            flops=4 * tok * steps * PAIRS * rows * LATENT,
            bytes_accessed=4 * tok * steps * PAIRS * (LATENT + rows),
            transcendentals=0,
        ),
        name="query_gradients",
    )(keys_e, keys_o, ds, started)


def local(queries, d_out, branch_latent, trunk_latent, ancestors, anc_count):
    leafs = lax.axis_size("leaf")
    head_parts = lax.axis_size("head")
    owned = trunk_latent.shape[0]
    part_rows = BLK // head_parts

    outgoing = pick(ancestors, trunk_latent.reshape(owned * BLK, LATENT))
    incoming = lax.all_to_all(
        outgoing.reshape(leafs, CAP * BLK, LATENT), "leaf", split_axis=0, concat_axis=0, tiled=True
    ).reshape(leafs * CAP * BLK, LATENT)

    started, ds, keys_e, keys_o, sent, mine, *others = attention(
        owned, head_parts, anc_count, ancestors, incoming, branch_latent, queries, d_out
    )

    got = lax.all_to_all(
        sent.reshape(leafs * head_parts, CAP * part_rows, LATENT),
        ("leaf", "head"), split_axis=0, concat_axis=0, tiled=True,
    ).reshape(leafs * CAP * BLK, LATENT)
    theirs = []
    for hop, part in enumerate(others, 1):
        route = [(i, (i + hop) % head_parts) for i in range(head_parts)]
        theirs.append(lax.ppermute(part, "head", route))

    d_queries = query_gradients(keys_e, keys_o, ds, started)
    d_branch, d_trunk = finish(ancestors, got, mine, theirs, owned, part_rows)
    return d_queries, d_branch, d_trunk


def solution(mesh):
    return jax.shard_map(
        local,
        mesh=mesh,
        in_specs=(
            P("leaf", "head"),
            P("leaf", "head"),
            P("leaf", None),
            P("leaf", None, None),
            P(),
            P(),
        ),
        out_specs=(P("leaf", "head"), P(("leaf", "head"), None), P("leaf", "head", None)),
        check_vma=False,
    )
```

time: 79.8 us -> 84.6 us (1.060)
  Pallas kernels: 55 us -> 59.9 us
    pallas_call x1, Pallas kernels: 36.1 us -> 45.7 us  [attention(): pl.pallas_call(functools.partial(attn_kernel, owned, head_parts, ahead),...]
    pallas_call x1, Pallas kernels: 15.9 us -> 11.3 us  [query_gradients(): pl.pallas_call(query_kernel, grid=(steps,), in_specs=[pl.BlockSpec(keys_e...]
  transfers between devices with their start and end apart: 2 -> 2, of which waited for: 0 -> 0; matrix products, arithmetic and copies ran while one was open for 0% -> 0% of each run, Pallas kernels for 20% -> 13%
where the time goes in v3:
time: 84.6 us; the launch traced here: 84.2 us
  Pallas kernels  59.9 us (71%)
  blocking collectives  18.6 us (22%)
  starting transfers between devices  5.02 us (6%)
    pallas_call x1, Pallas kernels, attention(): pl.pallas_call(functools.partial(attn_kernel, owned, head_parts, ahead),...  45.7 us
    all_to_all x1, blocking collectives, local(): lax.all_to_all(outgoing.reshape(leafs, CAP * BLK, LATENT), 'leaf', split_...  18.6 us
    pallas_call x1, Pallas kernels, query_gradients(): pl.pallas_call(query_kernel, grid=(steps,), in_specs=[pl.BlockSpec(keys_e...  11.3 us
    all_to_all x1, starting transfers between devices, local(): lax.all_to_all(sent.reshape(leafs * head_parts, CAP * part_rows, LATENT),...  3.19 us
    pallas_call x1, Pallas kernels, pick(): pl.pallas_call(pick_kernel, out_shape=jax.ShapeDtypeStruct((rows, LATENT)...  1.97 us
    ppermute x1, starting transfers between devices, local(): theirs.append(lax.ppermute(part, 'head', route))  1.83 us
  transfers between devices with their start and end apart: 2, of which 0 were waited for; matrix products, arithmetic and copies ran while one was open for 0% of the time, Pallas kernels for 13%

profile of v3, /device:TPU:0, one launch (start us, length us, event | category | flops | bytes accessed | tf_op | source)
XLA Modules:
  0.0 84.2 jit_solution(7797545828156456216)
XLA Ops:
  0.6 2.0 %pick_blocks.1 = bf16[256,576]{1,0:T(8,128)(2,1)} custom-call(s32[16,32]{1,0:T(8,128)} %ancestors.5, bf16[128,576]{1,0:T(8,128)(2,1)} %bitcast.9), custom_call_target="tpu_custom_call" | custom-call | tf_op jit(solution)/shard_map/pick_blocks/pallas_call | solution.py:83
  2.6 18.6 %all_to_all.10 = bf16[16,16,576]{2,1,0:T(8,128)(2,1)} all-to-all(bf16[16,16,576]{2,1,0:T(8,128)(2,1)} %bitcast.6), channel_id=1, replica_groups=mesh['leaf'=16,'head'=2] {'leaf'}, dimensions={0} | all-to-all | bytes 589824 | tf_op jit(solution)/shard_map/all_to_all | solution.py:409
  21.2 45.7 %score_gradients.1 = (bf16[192,36864]{1,0:T(8,128)(2,1)}, bf16[5,2,768,512]{3,2,1,0:T(8,128)(2,1)}, bf16[512,640]{1,0:T(8,128)(2,1)}, bf16[512,640]{1,0:T(8,128)...) custom-call(s32[16]{0:T(128)} %anc_count.1, s32[16,32]{1,0:T(8,128)} %ancestors.5, ...), custom_call_target="tpu_custom_call" | custom-call | flops 23957864448 | bytes 37748736 | tf_op jit(solution)/shard_map/score_gradients/pallas_call | solution.py:326
  66.8 3.2 %all-to-all-start.1 = ((bf16[32,8,576]{2,1,0:T(8,128)(2,1)}), bf16[32,8,576]{2,1,0:T(8,128)(2,1)S(1)}, u32[]{:S(2)}, u32[]{:S(2)}) async-start(bf16[32,8,576]{2,1,0:T(8,128)(2,1)} %bitcast.7), calls=%async_computation.1 | async-start | bytes 655360 | tf_op jit(solution)/shard_map/all_to_all | solution.py:417
  70.0 1.8 %collective-permute-start = (f32[96,576]{1,0:T(8,128)}, f32[96,576]{1,0:T(8,128)S(1)}, u32[]{:S(2)}, u32[]{:S(2)}) collective-permute-start(f32[96,576]{1,0:T(8,128)} %get-tuple-element.18), channel_id=1, source_target_pairs={{0,1},{1,0},{2,3},{3,2},{4,5},{5,4},{6,7},{7,6},{8,9},{9,8},{10,11... | collective-permute-start | bytes 663560 | tf_op jit(solution)/shard_map/ppermute | solution.py:424
  71.9 0.0 copy-start
  71.9 0.0 copy-start.1
  71.9 11.3 %query_gradients.1 = bf16[192,36864]{1,0:T(8,128)(2,1)} custom-call(bf16[512,640]{1,0:T(8,128)(2,1)} %get-tuple-element.12.keys_e, bf16[512,640]{1,0:T(8,128)(2,1)} %get-tuple-element.13.keys_o, bf16[5,2,768,512]{3,2,1,0:T(8,128)(2,1)} %get-tuple-element.14.ds, bf16[192,36864]{1,0:T(8,128)(2,1)} %get-tuple-element.15.started), custom_call_target="tpu_custom_call", output_to_operand_aliasing={{}: (3, {})} | custom-call | flops 4529848320 | bytes 16711680 | tf_op jit(solution)/shard_map/query_gradients/pallas_call | solution.py:380
  83.2 0.0 collective-permute-done.rest_0_
  83.2 0.0 all-to-all-done.1
  83.2 0.0 copy-done
  83.2 0.0 copy-done.1
  83.2 1.0 %sum_gradients.1 = (f32[96,576]{1,0:T(8,128)}, f32[16,4,576]{2,1,0:T(4,128)}) custom-call(s32[16,32]{1,0:T(8,128)S(1)} %copy-done.1, bf16[256,576]{1,0:T(8,128)(2,1)S(1)} %bitcast.5, f32[96,576]{1,0:T(8,128)S(1)} %copy-done, f32[96,576]{1,0:T(8,128)S(1)} %collective-permute-done.rest_0_), custom_call_target="tpu_custom_call" | custom-call | tf_op jit(solution)/shard_map/sum_gradients/pallas_call | solution.py:106
Async XLA Ops:
  66.8 16.4 %all-to-all-start.1 = ((bf16[32,8,576]{2,1,0:T(8,128)(2,1)}), bf16[32,8,576]{2,1,0:T(8,128)(2,1)S(1)}, u32[]{:S(2)}, u32[]{:S(2)}) async-start(bf16[32,8,576]{2,1,0:T(8,128)(2,1)} %bitcast.7), calls=%async_computation.1 | async-start | bytes 655360 | tf_op jit(solution)/shard_map/all_to_all | solution.py:417
  70.0 13.2 %collective-permute-start = (f32[96,576]{1,0:T(8,128)}, f32[96,576]{1,0:T(8,128)S(1)}, u32[]{:S(2)}, u32[]{:S(2)}) collective-permute-start(f32[96,576]{1,0:T(8,128)} %get-tuple-element.18), channel_id=1, source_target_pairs={{0,1},{1,0},{2,3},{3,2},{4,5},{5,4},{6,7},{7,6},{8,9},{9,8},{10,11... | collective-permute-start | bytes 663560 | tf_op jit(solution)/shard_map/ppermute | solution.py:424
  71.9 11.3 %copy-start = (f32[96,576]{1,0:T(8,128)S(1)}, f32[96,576]{1,0:T(8,128)}, u32[]{:S(2)}) copy-start(f32[96,576]{1,0:T(8,128)} %get-tuple-element.17.mine) | copy-start | bytes 663556
  71.9 11.3 %copy-start.1 = (s32[16,32]{1,0:T(8,128)S(1)}, s32[16,32]{1,0:T(8,128)}, u32[]{:S(2)}) copy-start(s32[16,32]{1,0:T(8,128)} %ancestors.5) | copy-start | bytes 6148

commit v4 on v2

--- a/solution.py
+++ b/solution.py
@@ -129,7 +129,8 @@
 
 
 def attn_kernel(
-    owned, head_parts, anc_count, ancestors, incoming, own, q, do, ds, keys_e, keys_o, sent, *rest
+    owned, head_parts, ahead, anc_count, ancestors, incoming, own, q, do, dq, ds, keys_e, keys_o, sent,
+    *rest
 ):
     own_parts = rest[:head_parts]
     far_bias, causal, q_st, s, dp, p_low, tops, acc_k, acc_v = rest[head_parts:]
@@ -186,7 +187,7 @@
 
     def score(j, at):
         n, cols = seen(j), pl.ds(j * stack + at, stack // 2)
-        out = mm(keys_e[:n, :], q_st[cols, :], NT)
+        out = mm(keys_e[:n, :], q_st[cols, :].T, NN)
         near = [(0, out[:least]), (least, out[least:far_rows] + far_bias[...])]
         if j > 0:
             near.append((far_rows, out[far_rows:n - sub]))
@@ -200,7 +201,7 @@
 
     def prob(j, at):
         n, cols = seen(j), pl.ds(j * stack + at, stack // 2)
-        dp[:n, cols] = mm(keys_e[:n, :RANK], grads(j, at // sub, PAIRS), NT)
+        dp[:n, cols] = mm(keys_e[:n, :RANK], grads(j, at // sub, PAIRS).T, NN)
 
     state = {}
 
@@ -255,6 +256,10 @@
         for job in jobs_of(i):
             job()
 
+    @pl.when(step < ahead)
+    def _():
+        put_queries(dq, ds, keys_e, keys_o)
+
     @pl.when(step == pl.num_programs(0) - 1)
     def _():
         acc_k[...] = acc_k[...] * SCALE
@@ -274,10 +279,15 @@
             out[...] = acc_k[pl.ds(at, own_rows), :LATENT]
 
 
+def steps_ahead(steps):
+    return steps * 3 // 8
+
+
 def attention(owned, head_parts, anc_count, ancestors, incoming, own, queries, d_out):
     tok = queries.shape[0]
     heads = queries.shape[1] // LATENT
     steps = heads // (2 * PAIRS)
+    ahead = steps_ahead(steps)
     far_rows, rows = ANC * BLK, ANC * BLK + tok
     toks = 2 * PAIRS * tok
     stack = 2 * PAIRS * token_part(tok)
@@ -291,7 +301,7 @@
 
     own_part = (tok // head_parts, LATENT)
     return pl.pallas_call(
-        functools.partial(attn_kernel, owned, head_parts),
+        functools.partial(attn_kernel, owned, head_parts, ahead),
         grid=(steps,),
         in_specs=[
             pl.BlockSpec(memory_space=pltpu.SMEM),
@@ -302,13 +312,17 @@
             pl.BlockSpec((tok, 2 * PAIRS * RANK), along),
         ],
         out_specs=[
-            pl.BlockSpec((1, rows, toks), lambda i: (i, 0, 0)),
+            pl.BlockSpec(
+                (tok, 2 * PAIRS * LATENT), lambda i: (0, jnp.minimum(i, max(ahead - 1, 0)))
+            ),
+            pl.BlockSpec((1, rows, toks), lambda i: (jnp.maximum(i - ahead, 0), 0, 0)),
             pl.BlockSpec((rows, WIDTH), whole),
             pl.BlockSpec((rows, WIDTH), whole),
             pl.BlockSpec(incoming.shape, whole),
         ] + [pl.BlockSpec(own_part, whole)] * head_parts,
         out_shape=[
-            jax.ShapeDtypeStruct((steps, rows, toks), bf16),
+            jax.ShapeDtypeStruct(queries.shape, bf16),
+            jax.ShapeDtypeStruct((steps - ahead, rows, toks), bf16),
             jax.ShapeDtypeStruct((rows, WIDTH), bf16),
             jax.ShapeDtypeStruct((rows, WIDTH), bf16),
             jax.ShapeDtypeStruct(incoming.shape, bf16),
@@ -324,7 +338,7 @@
             pltpu.VMEM((rows, WIDTH), f32),
             pltpu.VMEM((rows, RANK), f32),
         ],
-        compiler_params=pltpu.CompilerParams(vmem_limit_bytes=36 * MIB),
+        compiler_params=pltpu.CompilerParams(vmem_limit_bytes=60 * MIB),
         cost_estimate=pl.CostEstimate(
             flops=2 * tok * heads * rows * (2 * LATENT + 2 * RANK),
             bytes_accessed=2 * tok * heads * (LATENT + RANK + rows),
@@ -334,14 +348,13 @@
     )(anc_count, ancestors, incoming, own, queries, d_out)
 
 
-def query_kernel(keys_e, keys_o, ds, dq):
+def put_queries(dq, ds, keys_e, keys_o):
     tok = dq.shape[0]
     rows = ds.shape[1]
     sub = token_part(tok)
-    parts = tok // sub
     stack = PAIRS * sub
     low = LATENT - HALF
-    for j in range(parts):
+    for j in range(tok // sub):
         n = rows - tok + (j + 1) * sub
         even = mm(ds[0, :n, pl.ds(2 * j * stack, stack)], keys_e[:n, :], TN) * SCALE
         odd = mm(ds[0, :n, pl.ds((2 * j + 1) * stack, stack)], keys_o[:n, :], TN) * SCALE
@@ -355,10 +368,15 @@
             dq[toks, at + low + 2 * HALF:at + 2 * LATENT] = odd[part, 2 * HALF:].astype(dq.dtype)
 
 
-def query_gradients(keys_e, keys_o, ds, queries):
-    tok = queries.shape[0]
-    heads = queries.shape[1] // LATENT
-    steps, rows = ds.shape[0], ds.shape[1]
+def query_kernel(keys_e, keys_o, ds, started, dq):
+    put_queries(dq, ds, keys_e, keys_o)
+
+
+def query_gradients(keys_e, keys_o, ds, started):
+    tok = started.shape[0]
+    steps = ds.shape[0]
+    ahead = started.shape[1] // (2 * PAIRS * LATENT) - steps
+    rows = ds.shape[1]
     return pl.pallas_call(
         query_kernel,
         grid=(steps,),
@@ -366,17 +384,19 @@
             pl.BlockSpec(keys_e.shape, lambda i: (0, 0)),
             pl.BlockSpec(keys_o.shape, lambda i: (0, 0)),
             pl.BlockSpec((1,) + ds.shape[1:], lambda i: (i, 0, 0)),
+            pl.BlockSpec(memory_space=pl.ANY),
         ],
-        out_specs=pl.BlockSpec((tok, 2 * PAIRS * LATENT), lambda i: (0, i)),
-        out_shape=jax.ShapeDtypeStruct(queries.shape, queries.dtype),
-        compiler_params=pltpu.CompilerParams(vmem_limit_bytes=16 * MIB),
+        out_specs=pl.BlockSpec((tok, 2 * PAIRS * LATENT), lambda i: (0, i + ahead)),
+        out_shape=jax.ShapeDtypeStruct(started.shape, started.dtype),
+        input_output_aliases={3: 0},
+        compiler_params=pltpu.CompilerParams(vmem_limit_bytes=60 * MIB),
         cost_estimate=pl.CostEstimate(
-            flops=2 * tok * heads * rows * LATENT,
-            bytes_accessed=2 * tok * heads * (LATENT + rows),
+            flops=4 * tok * steps * PAIRS * rows * LATENT,
+            bytes_accessed=4 * tok * steps * PAIRS * (LATENT + rows),
             transcendentals=0,
         ),
         name="query_gradients",
-    )(keys_e, keys_o, ds)
+    )(keys_e, keys_o, ds, started)
 
 
 def local(queries, d_out, branch_latent, trunk_latent, ancestors, anc_count):
@@ -390,7 +410,7 @@
         outgoing.reshape(leafs, CAP * BLK, LATENT), "leaf", split_axis=0, concat_axis=0, tiled=True
     ).reshape(leafs * CAP * BLK, LATENT)
 
-    ds, keys_e, keys_o, sent, mine, *others = attention(
+    started, ds, keys_e, keys_o, sent, mine, *others = attention(
         owned, head_parts, anc_count, ancestors, incoming, branch_latent, queries, d_out
     )
 
@@ -403,7 +423,7 @@
         route = [(i, (i + hop) % head_parts) for i in range(head_parts)]
         theirs.append(lax.ppermute(part, "head", route))
 
-    d_queries = query_gradients(keys_e, keys_o, ds, queries)
+    d_queries = query_gradients(keys_e, keys_o, ds, started)
     d_branch, d_trunk = finish(ancestors, got, mine, theirs, owned, part_rows)
     return d_queries, d_branch, d_trunk
 

time: 85.7 us -> 79.2 us (0.924)
  local copies, waits for them, and re-layouts: 10.7 us -> 0.01 us
  Pallas kernels: 50.5 us -> 54.5 us
    unnamed x12 -> x4, local copies, waits for them, and re-layouts: 10.7 us -> 0.01 us
    pallas_call x1, Pallas kernels: 35.4 us -> 40.6 us  [attention(): pl.pallas_call(functools.partial(attn_kernel, owned, head_parts, ahead),...]
    pallas_call x1, Pallas kernels: 12.1 us -> 11 us  [query_gradients(): pl.pallas_call(query_kernel, grid=(steps,), in_specs=[pl.BlockSpec(keys_e...]
where the time goes in v4:
time: 79.2 us; the launch traced here: 78.7 us
  Pallas kernels  54.5 us (69%)
  blocking collectives  18.6 us (23%)
  starting transfers between devices  5.02 us (6%)
    pallas_call x1, Pallas kernels, attention(): pl.pallas_call(functools.partial(attn_kernel, owned, head_parts, ahead),...  40.6 us
    all_to_all x1, blocking collectives, local(): lax.all_to_all(outgoing.reshape(leafs, CAP * BLK, LATENT), 'leaf', split_...  18.6 us
    pallas_call x1, Pallas kernels, query_gradients(): pl.pallas_call(query_kernel, grid=(steps,), in_specs=[pl.BlockSpec(keys_e...  11 us
    all_to_all x1, starting transfers between devices, local(): lax.all_to_all(sent.reshape(leafs * head_parts, CAP * part_rows, LATENT),...  3.18 us
    pallas_call x1, Pallas kernels, pick(): pl.pallas_call(pick_kernel, out_shape=jax.ShapeDtypeStruct((rows, LATENT)...  1.97 us
    ppermute x1, starting transfers between devices, local(): theirs.append(lax.ppermute(part, 'head', route))  1.83 us
  transfers between devices with their start and end apart: 2, of which 0 were waited for; matrix products, arithmetic and copies ran while one was open for 0% of the time, Pallas kernels for 14%

profile of v4, /device:TPU:0, one launch (start us, length us, event | category | flops | bytes accessed | tf_op | source)
XLA Modules:
  0.0 78.7 jit_solution(4518718042493935281)
XLA Ops:
  0.6 2.0 %pick_blocks.1 = bf16[256,576]{1,0:T(8,128)(2,1)} custom-call(s32[16,32]{1,0:T(8,128)} %ancestors.5, bf16[128,576]{1,0:T(8,128)(2,1)} %bitcast.9), custom_call_target="tpu_custom_call" | custom-call | tf_op jit(solution)/shard_map/pick_blocks/pallas_call | solution.py:84
  2.6 18.6 %all_to_all.10 = bf16[16,16,576]{2,1,0:T(8,128)(2,1)} all-to-all(bf16[16,16,576]{2,1,0:T(8,128)(2,1)} %bitcast.6), channel_id=1, replica_groups=mesh['leaf'=16,'head'=2] {'leaf'}, dimensions={0} | all-to-all | bytes 589824 | tf_op jit(solution)/shard_map/all_to_all | solution.py:409
  21.2 40.6 %score_gradients.1 = (bf16[192,36864]{1,0:T(8,128)(2,1)}, bf16[5,448,1536]{2,1,0:T(8,128)(2,1)}, bf16[448,640]{1,0:T(8,128)(2,1)}, bf16[448,640]{1,0:T(8,128)(2,...) custom-call(s32[16]{0:T(128)} %anc_count.1, s32[16,32]{1,0:T(8,128)} %ancestors.5, ...), custom_call_target="tpu_custom_call" | custom-call | flops 23957864448 | bytes 37748736 | tf_op jit(solution)/shard_map/score_gradients/pallas_call | solution.py:303
  61.7 3.2 %all-to-all-start.1 = ((bf16[32,8,576]{2,1,0:T(8,128)(2,1)}), bf16[32,8,576]{2,1,0:T(8,128)(2,1)S(1)}, u32[]{:S(2)}, u32[]{:S(2)}) async-start(bf16[32,8,576]{2,1,0:T(8,128)(2,1)} %bitcast.7), calls=%async_computation.1 | async-start | bytes 655360 | tf_op jit(solution)/shard_map/all_to_all | solution.py:417
  64.9 1.8 %collective-permute-start = (f32[96,576]{1,0:T(8,128)}, f32[96,576]{1,0:T(8,128)S(1)}, u32[]{:S(2)}, u32[]{:S(2)}) collective-permute-start(f32[96,576]{1,0:T(8,128)} %get-tuple-element.18), channel_id=1, source_target_pairs={{0,1},{1,0},{2,3},{3,2},{4,5},{5,4},{6,7},{7,6},{8,9},{9,8},{10,11... | collective-permute-start | bytes 663560 | tf_op jit(solution)/shard_map/ppermute | solution.py:424
  66.8 0.0 copy-start
  66.8 0.0 copy-start.1
  66.8 11.0 %query_gradients.1 = bf16[192,36864]{1,0:T(8,128)(2,1)} custom-call(bf16[448,640]{1,0:T(8,128)(2,1)} %get-tuple-element.12.keys_e, bf16[448,640]{1,0:T(8,128)(2,1)} %get-tuple-element.13.keys_o, bf16[5,448,1536]{2,1,0:T(8,128)(2,1)} %get-tuple-element.14.ds, bf16[192,36864]{1,0:T(8,128)(2,1)} %get-tuple-element.15.started), custom_call_target="tpu_custom_call", output_to_operand_aliasing={{}: (3, {})} | custom-call | flops 3963617280 | bytes 15728640 | tf_op jit(solution)/shard_map/query_gradients/pallas_call | solution.py:380
  77.7 0.0 collective-permute-done.rest_0_
  77.7 0.0 all-to-all-done.1
  77.7 0.0 copy-done
  77.7 0.0 copy-done.1
  77.8 1.0 %sum_gradients.1 = (f32[96,576]{1,0:T(8,128)}, f32[16,4,576]{2,1,0:T(4,128)}) custom-call(s32[16,32]{1,0:T(8,128)S(1)} %copy-done.1, bf16[256,576]{1,0:T(8,128)(2,1)S(1)} %bitcast.5, f32[96,576]{1,0:T(8,128)S(1)} %copy-done, f32[96,576]{1,0:T(8,128)S(1)} %collective-permute-done.rest_0_), custom_call_target="tpu_custom_call" | custom-call | tf_op jit(solution)/shard_map/sum_gradients/pallas_call | solution.py:107
Async XLA Ops:
  61.7 16.0 %all-to-all-start.1 = ((bf16[32,8,576]{2,1,0:T(8,128)(2,1)}), bf16[32,8,576]{2,1,0:T(8,128)(2,1)S(1)}, u32[]{:S(2)}, u32[]{:S(2)}) async-start(bf16[32,8,576]{2,1,0:T(8,128)(2,1)} %bitcast.7), calls=%async_computation.1 | async-start | bytes 655360 | tf_op jit(solution)/shard_map/all_to_all | solution.py:417
  64.9 12.8 %collective-permute-start = (f32[96,576]{1,0:T(8,128)}, f32[96,576]{1,0:T(8,128)S(1)}, u32[]{:S(2)}, u32[]{:S(2)}) collective-permute-start(f32[96,576]{1,0:T(8,128)} %get-tuple-element.18), channel_id=1, source_target_pairs={{0,1},{1,0},{2,3},{3,2},{4,5},{5,4},{6,7},{7,6},{8,9},{9,8},{10,11... | collective-permute-start | bytes 663560 | tf_op jit(solution)/shard_map/ppermute | solution.py:424
  66.8 11.0 %copy-start = (f32[96,576]{1,0:T(8,128)S(1)}, f32[96,576]{1,0:T(8,128)}, u32[]{:S(2)}) copy-start(f32[96,576]{1,0:T(8,128)} %get-tuple-element.17.mine) | copy-start | bytes 663556
  66.8 11.0 %copy-start.1 = (s32[16,32]{1,0:T(8,128)S(1)}, s32[16,32]{1,0:T(8,128)}, u32[]{:S(2)}) copy-start(s32[16,32]{1,0:T(8,128)} %ancestors.5) | copy-start | bytes 6148

commit v5 on v4

--- a/solution.py
+++ b/solution.py
@@ -133,7 +133,8 @@
     *rest
 ):
     own_parts = rest[:head_parts]
-    far_bias, causal, q_st, s, dp, p_low, tops, acc_k, acc_v = rest[head_parts:]
+    scratch = rest[head_parts:]
+    k_e, k_o, far_bias, causal, q_st, do_st, s, dp, p_low, d_low, tops, acc_k, acc_v = scratch
     tok = q.shape[0]
     far_rows, rows = ANC * BLK, ANC * BLK + tok
     sub = token_part(tok)
@@ -149,8 +150,10 @@
         far = mm(sel, incoming[...], NN)
         joined = jnp.concatenate([far, own[...].astype(jnp.float32)], axis=0)
         padded = jnp.concatenate([joined, jnp.zeros((rows, HALF), jnp.float32)], axis=1)
-        keys_e[...] = padded.astype(jnp.bfloat16)
-        keys_o[...] = pltpu.roll(padded, HALF, axis=1).astype(jnp.bfloat16)
+        k_e[...] = padded.astype(jnp.bfloat16)
+        k_o[...] = pltpu.roll(padded, HALF, axis=1).astype(jnp.bfloat16)
+        keys_e[...] = k_e[...]
+        keys_o[...] = k_o[...]
         live = anc_count[lax.axis_index("leaf")]
         slot = div(lax.broadcasted_iota(jnp.int32, far_bias.shape, 0) + least, BLK)
         far_bias[...] = jnp.where(slot < live, 0.0, MASKED)
@@ -174,20 +177,16 @@
             odd = q[toks, at + LATENT - HALF:at + 2 * LATENT]
             odd = pltpu.roll(odd, WIDTH - HALF, axis=1)
             q_st[pl.ds(j * stack + (PAIRS + i) * sub, sub), :] = odd
-
-    heads = list(range(0, 2 * PAIRS, 2)) + list(range(1, 2 * PAIRS, 2))
-
-    def grads(j, first, count, at=0, size=RANK):
-        toks = pl.ds(j * sub, sub)
-        cols = [pl.ds(h * RANK + at, size) for h in heads[first:first + count]]
-        return jnp.concatenate([do[toks, c] for c in cols], axis=0)
+            for par in range(2):
+                block = do[toks, pl.ds((2 * i + par) * RANK, RANK)]
+                do_st[pl.ds(j * stack + (par * PAIRS + i) * sub, sub), :] = block
 
     def fold(x):
         return x.reshape(-1, 8, x.shape[1])
 
     def score(j, at):
         n, cols = seen(j), pl.ds(j * stack + at, stack // 2)
-        out = mm(keys_e[:n, :], q_st[cols, :].T, NN)
+        out = mm(k_e[:n, :], q_st[cols, :], NT)
         near = [(0, out[:least]), (least, out[least:far_rows] + far_bias[...])]
         if j > 0:
             near.append((far_rows, out[far_rows:n - sub]))
@@ -201,7 +200,7 @@
 
     def prob(j, at):
         n, cols = seen(j), pl.ds(j * stack + at, stack // 2)
-        dp[:n, cols] = mm(keys_e[:n, :RANK], grads(j, at // sub, PAIRS).T, NN)
+        dp[:n, cols] = mm(k_e[:n, :RANK], do_st[cols, :], NT)
 
     state = {}
 
@@ -224,15 +223,15 @@
         for r, n in pieces(seen(j), 64):
             p = s[pl.ds(r, n), lane] * inv
             p_low[pl.ds(r, n), lane] = p.astype(jnp.bfloat16)
-            ds[0, pl.ds(r, n), lane] = (p * (dp[pl.ds(r, n), lane] - delta)).astype(ds.dtype)
+            d_low[pl.ds(r, n), lane] = (p * (dp[pl.ds(r, n), lane] - delta)).astype(ds.dtype)
 
     def grad_values(j, at, size):
         n, cols = seen(j), pl.ds(at, size)
-        acc_v[:n, cols] += mm(p_low[:n, lanes(j)], grads(j, 0, 2 * PAIRS, at, size), NN)
+        acc_v[:n, cols] += mm(p_low[:n, lanes(j)], do_st[lanes(j), cols], NN)
 
     def grad_keys(j, at, size):
         n, cols = seen(j), pl.ds(at, size)
-        acc_k[:n, cols] += mm(ds[0, :n, lanes(j)], q_st[lanes(j), cols], NN)
+        acc_k[:n, cols] += mm(d_low[:n, lanes(j)], q_st[lanes(j), cols], NN)
 
     def jobs_of(i):
         products, passes = [], []
@@ -258,7 +257,12 @@
 
     @pl.when(step < ahead)
     def _():
-        put_queries(dq, ds, keys_e, keys_o)
+        put_queries(dq, d_low, k_e, k_o)
+
+    @pl.when(step >= ahead)
+    def _():
+        for j in range(parts):
+            ds[0, :seen(j), lanes(j)] = d_low[:seen(j), lanes(j)]
 
     @pl.when(step == pl.num_programs(0) - 1)
     def _():
@@ -328,11 +332,15 @@
             jax.ShapeDtypeStruct(incoming.shape, bf16),
         ] + [jax.ShapeDtypeStruct(own_part, f32)] * head_parts,
         scratch_shapes=[
+            pltpu.VMEM((rows, WIDTH), bf16),
+            pltpu.VMEM((rows, WIDTH), bf16),
             pltpu.VMEM((far_rows - LEAST_LIVE * BLK, stack // 2), f32),
             pltpu.VMEM((token_part(tok), stack // 2), f32),
             pltpu.VMEM((toks, WIDTH), bf16),
+            pltpu.VMEM((toks, RANK), bf16),
             pltpu.VMEM((rows, toks), f32),
             pltpu.VMEM((rows, toks), f32),
+            pltpu.VMEM((rows, toks), bf16),
             pltpu.VMEM((rows, toks), bf16),
             pltpu.VMEM((8, toks), f32),
             pltpu.VMEM((rows, WIDTH), f32),
@@ -350,14 +358,14 @@
 
 def put_queries(dq, ds, keys_e, keys_o):
     tok = dq.shape[0]
-    rows = ds.shape[1]
+    rows = ds.shape[0]
     sub = token_part(tok)
     stack = PAIRS * sub
     low = LATENT - HALF
     for j in range(tok // sub):
         n = rows - tok + (j + 1) * sub
-        even = mm(ds[0, :n, pl.ds(2 * j * stack, stack)], keys_e[:n, :], TN) * SCALE
-        odd = mm(ds[0, :n, pl.ds((2 * j + 1) * stack, stack)], keys_o[:n, :], TN) * SCALE
+        even = mm(ds[:n, pl.ds(2 * j * stack, stack)], keys_e[:n, :], TN) * SCALE
+        odd = mm(ds[:n, pl.ds((2 * j + 1) * stack, stack)], keys_o[:n, :], TN) * SCALE
         for i in range(PAIRS):
             at = i * 2 * LATENT
             part = slice(i * sub, (i + 1) * sub)
@@ -369,7 +377,7 @@
 
 
 def query_kernel(keys_e, keys_o, ds, started, dq):
-    put_queries(dq, ds, keys_e, keys_o)
+    put_queries(dq, ds.at[0], keys_e, keys_o)
 
 
 def query_gradients(keys_e, keys_o, ds, started):

time: 79.2 us -> 79.6 us (level)
  no operation moved by 1% of the time
where the time goes in v5:
time: 79.6 us; the launch traced here: 79.2 us
  Pallas kernels  54.9 us (69%)
  blocking collectives  18.6 us (23%)
  starting transfers between devices  5.01 us (6%)
    pallas_call x1, Pallas kernels, attention(): pl.pallas_call(functools.partial(attn_kernel, owned, head_parts, ahead),...  41 us
    all_to_all x1, blocking collectives, local(): lax.all_to_all(outgoing.reshape(leafs, CAP * BLK, LATENT), 'leaf', split_...  18.6 us
    pallas_call x1, Pallas kernels, query_gradients(): pl.pallas_call(query_kernel, grid=(steps,), in_specs=[pl.BlockSpec(keys_e...  11 us
    all_to_all x1, starting transfers between devices, local(): lax.all_to_all(sent.reshape(leafs * head_parts, CAP * part_rows, LATENT),...  3.18 us
    pallas_call x1, Pallas kernels, pick(): pl.pallas_call(pick_kernel, out_shape=jax.ShapeDtypeStruct((rows, LATENT)...  1.97 us
    ppermute x1, starting transfers between devices, local(): theirs.append(lax.ppermute(part, 'head', route))  1.83 us
  transfers between devices with their start and end apart: 2, of which 0 were waited for; matrix products, arithmetic and copies ran while one was open for 0% of the time, Pallas kernels for 14%

profile of v5, /device:TPU:0, one launch (start us, length us, event | category | flops | bytes accessed | tf_op | source)
XLA Modules:
  0.0 79.2 jit_solution(4002863976049588582)
XLA Ops:
  0.6 2.0 %pick_blocks.1 = bf16[256,576]{1,0:T(8,128)(2,1)} custom-call(s32[16,32]{1,0:T(8,128)} %ancestors.5, bf16[128,576]{1,0:T(8,128)(2,1)} %bitcast.9), custom_call_target="tpu_custom_call" | custom-call | tf_op jit(solution)/shard_map/pick_blocks/pallas_call | solution.py:84
  2.6 18.6 %all_to_all.10 = bf16[16,16,576]{2,1,0:T(8,128)(2,1)} all-to-all(bf16[16,16,576]{2,1,0:T(8,128)(2,1)} %bitcast.6), channel_id=1, replica_groups=mesh['leaf'=16,'head'=2] {'leaf'}, dimensions={0} | all-to-all | bytes 589824 | tf_op jit(solution)/shard_map/all_to_all | solution.py:417
  21.2 41.0 %score_gradients.1 = (bf16[192,36864]{1,0:T(8,128)(2,1)}, bf16[5,448,1536]{2,1,0:T(8,128)(2,1)}, bf16[448,640]{1,0:T(8,128)(2,1)}, bf16[448,640]{1,0:T(8,128)(2,...) custom-call(s32[16]{0:T(128)} %anc_count.1, s32[16,32]{1,0:T(8,128)} %ancestors.5, ...), custom_call_target="tpu_custom_call" | custom-call | flops 23957864448 | bytes 37748736 | tf_op jit(solution)/shard_map/score_gradients/pallas_call | solution.py:307
  62.2 3.2 %all-to-all-start.1 = ((bf16[32,8,576]{2,1,0:T(8,128)(2,1)}), bf16[32,8,576]{2,1,0:T(8,128)(2,1)S(1)}, u32[]{:S(2)}, u32[]{:S(2)}) async-start(bf16[32,8,576]{2,1,0:T(8,128)(2,1)} %bitcast.7), calls=%async_computation.1 | async-start | bytes 655360 | tf_op jit(solution)/shard_map/all_to_all | solution.py:425
  65.4 1.8 %collective-permute-start = (f32[96,576]{1,0:T(8,128)}, f32[96,576]{1,0:T(8,128)S(1)}, u32[]{:S(2)}, u32[]{:S(2)}) collective-permute-start(f32[96,576]{1,0:T(8,128)} %get-tuple-element.18), channel_id=1, source_target_pairs={{0,1},{1,0},{2,3},{3,2},{4,5},{5,4},{6,7},{7,6},{8,9},{9,8},{10,11... | collective-permute-start | bytes 663560 | tf_op jit(solution)/shard_map/ppermute | solution.py:432
  67.2 0.0 copy-start
  67.2 0.0 copy-start.1
  67.2 11.0 %query_gradients.1 = bf16[192,36864]{1,0:T(8,128)(2,1)} custom-call(bf16[448,640]{1,0:T(8,128)(2,1)} %get-tuple-element.12.keys_e, bf16[448,640]{1,0:T(8,128)(2,1)} %get-tuple-element.13.keys_o, bf16[5,448,1536]{2,1,0:T(8,128)(2,1)} %get-tuple-element.14.ds, bf16[192,36864]{1,0:T(8,128)(2,1)} %get-tuple-element.15.started), custom_call_target="tpu_custom_call", output_to_operand_aliasing={{}: (3, {})} | custom-call | flops 3963617280 | bytes 15728640 | tf_op jit(solution)/shard_map/query_gradients/pallas_call | solution.py:388
  78.2 0.0 collective-permute-done.rest_0_
  78.2 0.0 all-to-all-done.1
  78.2 0.0 copy-done
  78.2 0.0 copy-done.1
  78.2 1.0 %sum_gradients.1 = (f32[96,576]{1,0:T(8,128)}, f32[16,4,576]{2,1,0:T(4,128)}) custom-call(s32[16,32]{1,0:T(8,128)S(1)} %copy-done.1, bf16[256,576]{1,0:T(8,128)(2,1)S(1)} %bitcast.5, f32[96,576]{1,0:T(8,128)S(1)} %copy-done, f32[96,576]{1,0:T(8,128)S(1)} %collective-permute-done.rest_0_), custom_call_target="tpu_custom_call" | custom-call | tf_op jit(solution)/shard_map/sum_gradients/pallas_call | solution.py:107
Async XLA Ops:
  62.2 16.0 %all-to-all-start.1 = ((bf16[32,8,576]{2,1,0:T(8,128)(2,1)}), bf16[32,8,576]{2,1,0:T(8,128)(2,1)S(1)}, u32[]{:S(2)}, u32[]{:S(2)}) async-start(bf16[32,8,576]{2,1,0:T(8,128)(2,1)} %bitcast.7), calls=%async_computation.1 | async-start | bytes 655360 | tf_op jit(solution)/shard_map/all_to_all | solution.py:425
  65.4 12.8 %collective-permute-start = (f32[96,576]{1,0:T(8,128)}, f32[96,576]{1,0:T(8,128)S(1)}, u32[]{:S(2)}, u32[]{:S(2)}) collective-permute-start(f32[96,576]{1,0:T(8,128)} %get-tuple-element.18), channel_id=1, source_target_pairs={{0,1},{1,0},{2,3},{3,2},{4,5},{5,4},{6,7},{7,6},{8,9},{9,8},{10,11... | collective-permute-start | bytes 663560 | tf_op jit(solution)/shard_map/ppermute | solution.py:432
  67.2 11.0 %copy-start = (f32[96,576]{1,0:T(8,128)S(1)}, f32[96,576]{1,0:T(8,128)}, u32[]{:S(2)}) copy-start(f32[96,576]{1,0:T(8,128)} %get-tuple-element.17.mine) | copy-start | bytes 663556
  67.2 11.0 %copy-start.1 = (s32[16,32]{1,0:T(8,128)S(1)}, s32[16,32]{1,0:T(8,128)}, u32[]{:S(2)}) copy-start(s32[16,32]{1,0:T(8,128)} %ancestors.5) | copy-start | bytes 6148

commit v6 on v5

--- a/solution.py
+++ b/solution.py
@@ -54,6 +54,17 @@
     return jnp.where(lane == place, 1.0, 0.0).astype(jnp.bfloat16)
 
 
+def build_keys(k_e, k_o, ancestors, incoming, own, owned):
+    rows = k_e.shape[0]
+    row, owner, second = slot_places(ancestors, owned)
+    sel = one_hot((owner * CAP + second) * BLK + mod(row, BLK), incoming.shape[0])
+    far = mm(sel, incoming[...], NN)
+    joined = jnp.concatenate([far, own[...].astype(jnp.float32)], axis=0)
+    padded = jnp.concatenate([joined, jnp.zeros((rows, HALF), jnp.float32)], axis=1)
+    k_e[...] = padded.astype(jnp.bfloat16)
+    k_o[...] = pltpu.roll(padded, HALF, axis=1).astype(jnp.bfloat16)
+
+
 def token_part(tok):
     return 64 if tok % 64 == 0 else tok
 
@@ -129,8 +140,7 @@
 
 
 def attn_kernel(
-    owned, head_parts, ahead, anc_count, ancestors, incoming, own, q, do, dq, ds, keys_e, keys_o, sent,
-    *rest
+    owned, head_parts, ahead, anc_count, ancestors, incoming, own, q, do, dq, ds, sent, *rest
 ):
     own_parts = rest[:head_parts]
     scratch = rest[head_parts:]
@@ -145,15 +155,7 @@
 
     @pl.when(step == 0)
     def _():
-        row, owner, second = slot_places(ancestors, owned)
-        sel = one_hot((owner * CAP + second) * BLK + mod(row, BLK), incoming.shape[0])
-        far = mm(sel, incoming[...], NN)
-        joined = jnp.concatenate([far, own[...].astype(jnp.float32)], axis=0)
-        padded = jnp.concatenate([joined, jnp.zeros((rows, HALF), jnp.float32)], axis=1)
-        k_e[...] = padded.astype(jnp.bfloat16)
-        k_o[...] = pltpu.roll(padded, HALF, axis=1).astype(jnp.bfloat16)
-        keys_e[...] = k_e[...]
-        keys_o[...] = k_o[...]
+        build_keys(k_e, k_o, ancestors, incoming, own, owned)
         live = anc_count[lax.axis_index("leaf")]
         slot = div(lax.broadcasted_iota(jnp.int32, far_bias.shape, 0) + least, BLK)
         far_bias[...] = jnp.where(slot < live, 0.0, MASKED)
@@ -173,13 +175,13 @@
         toks = pl.ds(j * sub, sub)
         for i in range(PAIRS):
             at = i * 2 * LATENT
-            q_st[pl.ds(j * stack + i * sub, sub), :] = q[toks, at:at + WIDTH]
-            odd = q[toks, at + LATENT - HALF:at + 2 * LATENT]
-            odd = pltpu.roll(odd, WIDTH - HALF, axis=1)
-            q_st[pl.ds(j * stack + (PAIRS + i) * sub, sub), :] = odd
-            for par in range(2):
-                block = do[toks, pl.ds((2 * i + par) * RANK, RANK)]
-                do_st[pl.ds(j * stack + (par * PAIRS + i) * sub, sub), :] = block
+            half, pair = divmod(i, PAIRS // 2)
+            even, odd = [j * stack + (half * PAIRS + par * PAIRS // 2 + pair) * sub for par in range(2)]
+            q_st[pl.ds(even, sub), :] = q[toks, at:at + WIDTH]
+            moved = pltpu.roll(q[toks, at + LATENT - HALF:at + 2 * LATENT], WIDTH - HALF, axis=1)
+            q_st[pl.ds(odd, sub), :] = moved
+            do_st[pl.ds(even, sub), :] = do[toks, pl.ds(2 * i * RANK, RANK)]
+            do_st[pl.ds(odd, sub), :] = do[toks, pl.ds((2 * i + 1) * RANK, RANK)]
 
     def fold(x):
         return x.reshape(-1, 8, x.shape[1])
@@ -255,14 +257,21 @@
         for job in jobs_of(i):
             job()
 
+    wide = stack // 4
+    for half in range(2):
+        for j in range(parts):
+            for par in range(2):
+                n = seen(j)
+                to = pl.ds((par * parts + j) * wide, wide)
+                at = pl.ds(j * stack + (2 * half + par) * wide, wide)
+                ds[half, :n, to] = d_low[:n, at]
+                if n < rows:
+                    ds[half, n:, to] = jnp.zeros((rows - n, wide), ds.dtype)
+
     @pl.when(step < ahead)
     def _():
-        put_queries(dq, d_low, k_e, k_o)
-
-    @pl.when(step >= ahead)
-    def _():
-        for j in range(parts):
-            ds[0, :seen(j), lanes(j)] = d_low[:seen(j), lanes(j)]
+        for half in range(2):
+            put_queries(dq, half * PAIRS * LATENT, ds[half], k_e[...], k_o[...])
 
     @pl.when(step == pl.num_programs(0) - 1)
     def _():
@@ -319,16 +328,12 @@
             pl.BlockSpec(
                 (tok, 2 * PAIRS * LATENT), lambda i: (0, jnp.minimum(i, max(ahead - 1, 0)))
             ),
-            pl.BlockSpec((1, rows, toks), lambda i: (jnp.maximum(i - ahead, 0), 0, 0)),
-            pl.BlockSpec((rows, WIDTH), whole),
-            pl.BlockSpec((rows, WIDTH), whole),
+            pl.BlockSpec((2, rows, toks // 2), lambda i: (jnp.maximum(i - ahead, 0), 0, 0)),
             pl.BlockSpec(incoming.shape, whole),
         ] + [pl.BlockSpec(own_part, whole)] * head_parts,
         out_shape=[
             jax.ShapeDtypeStruct(queries.shape, bf16),
-            jax.ShapeDtypeStruct((steps - ahead, rows, toks), bf16),
-            jax.ShapeDtypeStruct((rows, WIDTH), bf16),
-            jax.ShapeDtypeStruct((rows, WIDTH), bf16),
+            jax.ShapeDtypeStruct((2 * (steps - ahead), rows, toks // 2), bf16),
             jax.ShapeDtypeStruct(incoming.shape, bf16),
         ] + [jax.ShapeDtypeStruct(own_part, f32)] * head_parts,
         scratch_shapes=[
@@ -356,55 +361,63 @@
     )(anc_count, ancestors, incoming, own, queries, d_out)
 
 
-def put_queries(dq, ds, keys_e, keys_o):
+def put_queries(dq, first, ds, keys_e, keys_o):
     tok = dq.shape[0]
-    rows = ds.shape[0]
     sub = token_part(tok)
-    stack = PAIRS * sub
+    pairs = PAIRS // 2
+    toks = pairs * tok
     low = LATENT - HALF
+    even = mm(ds[:, :toks], keys_e, TN) * SCALE
+    odd = mm(ds[:, toks:], keys_o, TN) * SCALE
     for j in range(tok // sub):
-        n = rows - tok + (j + 1) * sub
-        even = mm(ds[:n, pl.ds(2 * j * stack, stack)], keys_e[:n, :], TN) * SCALE
-        odd = mm(ds[:n, pl.ds((2 * j + 1) * stack, stack)], keys_o[:n, :], TN) * SCALE
-        for i in range(PAIRS):
-            at = i * 2 * LATENT
-            part = slice(i * sub, (i + 1) * sub)
-            toks = pl.ds(j * sub, sub)
-            dq[toks, at:at + low] = even[part, :low].astype(dq.dtype)
+        for i in range(pairs):
+            at = first + i * 2 * LATENT
+            part = slice((j * pairs + i) * sub, (j * pairs + i + 1) * sub)
+            to = pl.ds(j * sub, sub)
+            dq[to, at:at + low] = even[part, :low].astype(dq.dtype)
             joint = even[part, low:] + odd[part, :2 * HALF]
-            dq[toks, at + low:at + low + 2 * HALF] = joint.astype(dq.dtype)
-            dq[toks, at + low + 2 * HALF:at + 2 * LATENT] = odd[part, 2 * HALF:].astype(dq.dtype)
-
-
-def query_kernel(keys_e, keys_o, ds, started, dq):
-    put_queries(dq, ds.at[0], keys_e, keys_o)
-
-
-def query_gradients(keys_e, keys_o, ds, started):
+            dq[to, at + low:at + low + 2 * HALF] = joint.astype(dq.dtype)
+            dq[to, at + low + 2 * HALF:at + 2 * LATENT] = odd[part, 2 * HALF:].astype(dq.dtype)
+
+
+def query_kernel(owned, ancestors, incoming, own, ds, started, dq, k_e, k_o):
+    @pl.when(pl.program_id(0) == 0)
+    def _():
+        build_keys(k_e, k_o, ancestors, incoming, own, owned)
+
+    put_queries(dq, 0, ds[0], k_e[...], k_o[...])
+
+
+def query_gradients(owned, ancestors, incoming, own, ds, started):
     tok = started.shape[0]
-    steps = ds.shape[0]
-    ahead = started.shape[1] // (2 * PAIRS * LATENT) - steps
-    rows = ds.shape[1]
+    steps, rows = ds.shape[0], ds.shape[1]
+    ahead = started.shape[1] // (PAIRS * LATENT) - steps
+
+    def whole(i):
+        return (0, 0)
+
     return pl.pallas_call(
-        query_kernel,
+        functools.partial(query_kernel, owned),
         grid=(steps,),
         in_specs=[
-            pl.BlockSpec(keys_e.shape, lambda i: (0, 0)),
-            pl.BlockSpec(keys_o.shape, lambda i: (0, 0)),
+            pl.BlockSpec(ancestors.shape, whole),
+            pl.BlockSpec(incoming.shape, whole),
+            pl.BlockSpec(own.shape, whole),
             pl.BlockSpec((1,) + ds.shape[1:], lambda i: (i, 0, 0)),
             pl.BlockSpec(memory_space=pl.ANY),
         ],
-        out_specs=pl.BlockSpec((tok, 2 * PAIRS * LATENT), lambda i: (0, i + ahead)),
+        out_specs=pl.BlockSpec((tok, PAIRS * LATENT), lambda i: (0, i + ahead)),
         out_shape=jax.ShapeDtypeStruct(started.shape, started.dtype),
-        input_output_aliases={3: 0},
+        scratch_shapes=[pltpu.VMEM((rows, WIDTH), jnp.bfloat16)] * 2,
+        input_output_aliases={4: 0},
         compiler_params=pltpu.CompilerParams(vmem_limit_bytes=60 * MIB),
         cost_estimate=pl.CostEstimate(
-            flops=4 * tok * steps * PAIRS * rows * LATENT,
-            bytes_accessed=4 * tok * steps * PAIRS * (LATENT + rows),
+            flops=2 * tok * steps * PAIRS * rows * LATENT,
+            bytes_accessed=2 * tok * steps * PAIRS * (LATENT + rows),
             transcendentals=0,
         ),
         name="query_gradients",
-    )(keys_e, keys_o, ds, started)
+    )(ancestors, incoming, own, ds, started)
 
 
 def local(queries, d_out, branch_latent, trunk_latent, ancestors, anc_count):
@@ -418,7 +431,7 @@
         outgoing.reshape(leafs, CAP * BLK, LATENT), "leaf", split_axis=0, concat_axis=0, tiled=True
     ).reshape(leafs * CAP * BLK, LATENT)
 
-    started, ds, keys_e, keys_o, sent, mine, *others = attention(
+    started, ds, sent, mine, *others = attention(
         owned, head_parts, anc_count, ancestors, incoming, branch_latent, queries, d_out
     )
 
@@ -431,7 +444,7 @@
         route = [(i, (i + hop) % head_parts) for i in range(head_parts)]
         theirs.append(lax.ppermute(part, "head", route))
 
-    d_queries = query_gradients(keys_e, keys_o, ds, started)
+    d_queries = query_gradients(owned, ancestors, incoming, branch_latent, ds, started)
     d_branch, d_trunk = finish(ancestors, got, mine, theirs, owned, part_rows)
     return d_queries, d_branch, d_trunk
 

time: 79.6 us -> 83.7 us (1.052)
  Pallas kernels: 54.9 us -> 58.9 us
    pallas_call x1, Pallas kernels: 11 us -> 13.6 us  [query_gradients(): pl.pallas_call(functools.partial(query_kernel, owned), grid=(steps,), in_...]
    pallas_call x1, Pallas kernels: 41 us -> 42.3 us  [attention(): pl.pallas_call(functools.partial(attn_kernel, owned, head_parts, ahead),...]
  transfers between devices with their start and end apart: 2 -> 2, of which waited for: 0 -> 0; matrix products, arithmetic and copies ran while one was open for 0% -> 0% of each run, Pallas kernels for 14% -> 16%
where the time goes in v6:
time: 83.7 us; the launch traced here: 83.1 us
  Pallas kernels  58.9 us (70%)
  blocking collectives  18.6 us (22%)
  starting transfers between devices  5.04 us (6%)
    pallas_call x1, Pallas kernels, attention(): pl.pallas_call(functools.partial(attn_kernel, owned, head_parts, ahead),...  42.3 us
    all_to_all x1, blocking collectives, local(): lax.all_to_all(outgoing.reshape(leafs, CAP * BLK, LATENT), 'leaf', split_...  18.6 us
    pallas_call x1, Pallas kernels, query_gradients(): pl.pallas_call(functools.partial(query_kernel, owned), grid=(steps,), in_...  13.6 us
    all_to_all x1, starting transfers between devices, local(): lax.all_to_all(sent.reshape(leafs * head_parts, CAP * part_rows, LATENT),...  3.21 us
    pallas_call x1, Pallas kernels, pick(): pl.pallas_call(pick_kernel, out_shape=jax.ShapeDtypeStruct((rows, LATENT)...  1.97 us
    ppermute x1, starting transfers between devices, local(): theirs.append(lax.ppermute(part, 'head', route))  1.83 us
  transfers between devices with their start and end apart: 2, of which 0 were waited for; matrix products, arithmetic and copies ran while one was open for 0% of the time, Pallas kernels for 16%

profile of v6, /device:TPU:0, one launch (start us, length us, event | category | flops | bytes accessed | tf_op | source)
XLA Modules:
  0.0 83.1 jit_solution(6660358338194102900)
XLA Ops:
  0.6 2.0 %pick_blocks.1 = bf16[256,576]{1,0:T(8,128)(2,1)} custom-call(s32[16,32]{1,0:T(8,128)} %ancestors.7, bf16[128,576]{1,0:T(8,128)(2,1)} %bitcast.10), custom_call_target="tpu_custom_call" | custom-call | tf_op jit(solution)/shard_map/pick_blocks/pallas_call | solution.py:95
  2.6 18.6 %all_to_all.10 = bf16[16,16,576]{2,1,0:T(8,128)(2,1)} all-to-all(bf16[16,16,576]{2,1,0:T(8,128)(2,1)} %bitcast.8), channel_id=1, replica_groups=mesh['leaf'=16,'head'=2] {'leaf'}, dimensions={0} | all-to-all | bytes 589824 | tf_op jit(solution)/shard_map/all_to_all | solution.py:430
  21.2 42.3 %score_gradients.1 = (bf16[192,36864]{1,0:T(8,128)(2,1)}, bf16[10,448,768]{2,1,0:T(8,128)(2,1)}, bf16[256,576]{1,0:T(8,128)(2,1)}, f32[96,576]{1,0:T(8,128)}, f32[96,576]{1,0:T(8,128)}) custom-call(s32[16]{0:T(128)} %anc_count.1, s32[16,32]{1,0:T(8,128)} %ancestors.7, bf16[256,576]{1,0:T(8,128)(2,1)} %bitcast.6, bf16[192,576]{1,0:T(8,128)(2,1)} %own.3, ...), custom_call_target="tpu_custom_call" | custom-call | flops 23957864448 | bytes 37748736 | tf_op jit(solution)/shard_map/score_gradients/pallas_call | solution.py:316
  63.5 3.2 %all-to-all-start.1 = ((bf16[32,8,576]{2,1,0:T(8,128)(2,1)}), bf16[32,8,576]{2,1,0:T(8,128)(2,1)S(1)}, u32[]{:S(2)}, u32[]{:S(2)}) async-start(bf16[32,8,576]{2,1,0:T(8,128)(2,1)} %bitcast.9), calls=%async_computation.1 | async-start | bytes 655360 | tf_op jit(solution)/shard_map/all_to_all | solution.py:438
  66.7 1.8 %collective-permute-start = (f32[96,576]{1,0:T(8,128)}, f32[96,576]{1,0:T(8,128)S(1)}, u32[]{:S(2)}, u32[]{:S(2)}) collective-permute-start(f32[96,576]{1,0:T(8,128)} %get-tuple-element.14), channel_id=1, source_target_pairs={{0,1},{1,0},{2,3},{3,2},{4,5},{5,4},{6,7},{7,6},{8,9},{9,8},{10,11... | collective-permute-start | bytes 663560 | tf_op jit(solution)/shard_map/ppermute | solution.py:445
  68.5 0.0 copy-start
  68.5 0.0 copy-start.1
  68.5 13.6 %query_gradients.1 = bf16[192,36864]{1,0:T(8,128)(2,1)} custom-call(s32[16,32]{1,0:T(8,128)} %ancestors.7, bf16[256,576]{1,0:T(8,128)(2,1)} %bitcast.7, bf16[192,576]{1,0:T(8,128)(2,1)} %own.3, bf16[10,448,768]{2,1,0:T(8,128)(2,1)} %get-tuple-element.10.ds, bf16[192,36864]{1,0:T(8,128)(2,1)} %get-tuple-element.11.started), custom_call_target="tpu_custom_call", output_to_operand_aliasing={{}: (4, {})} | custom-call | flops 3963617280 | bytes 15728640 | tf_op jit(solution)/shard_map/query_gradients/pallas_call | solution.py:399
  82.1 0.0 collective-permute-done.rest_0_
  82.1 0.0 all-to-all-done.1
  82.1 0.0 copy-done
  82.1 0.0 copy-done.1
  82.1 1.0 %sum_gradients.1 = (f32[96,576]{1,0:T(8,128)}, f32[16,4,576]{2,1,0:T(4,128)}) custom-call(s32[16,32]{1,0:T(8,128)S(1)} %copy-done.1, bf16[256,576]{1,0:T(8,128)(2,1)S(1)} %bitcast.5, f32[96,576]{1,0:T(8,128)S(1)} %copy-done, f32[96,576]{1,0:T(8,128)S(1)} %collective-permute-done.rest_0_), custom_call_target="tpu_custom_call" | custom-call | tf_op jit(solution)/shard_map/sum_gradients/pallas_call | solution.py:118
Async XLA Ops:
  63.5 18.6 %all-to-all-start.1 = ((bf16[32,8,576]{2,1,0:T(8,128)(2,1)}), bf16[32,8,576]{2,1,0:T(8,128)(2,1)S(1)}, u32[]{:S(2)}, u32[]{:S(2)}) async-start(bf16[32,8,576]{2,1,0:T(8,128)(2,1)} %bitcast.9), calls=%async_computation.1 | async-start | bytes 655360 | tf_op jit(solution)/shard_map/all_to_all | solution.py:438
  66.7 15.4 %collective-permute-start = (f32[96,576]{1,0:T(8,128)}, f32[96,576]{1,0:T(8,128)S(1)}, u32[]{:S(2)}, u32[]{:S(2)}) collective-permute-start(f32[96,576]{1,0:T(8,128)} %get-tuple-element.14), channel_id=1, source_target_pairs={{0,1},{1,0},{2,3},{3,2},{4,5},{5,4},{6,7},{7,6},{8,9},{9,8},{10,11... | collective-permute-start | bytes 663560 | tf_op jit(solution)/shard_map/ppermute | solution.py:445
  68.5 13.6 %copy-start = (f32[96,576]{1,0:T(8,128)S(1)}, f32[96,576]{1,0:T(8,128)}, u32[]{:S(2)}) copy-start(f32[96,576]{1,0:T(8,128)} %get-tuple-element.13.mine) | copy-start | bytes 663556
  68.5 13.6 %copy-start.1 = (s32[16,32]{1,0:T(8,128)S(1)}, s32[16,32]{1,0:T(8,128)}, u32[]{:S(2)}) copy-start(s32[16,32]{1,0:T(8,128)} %ancestors.7) | copy-start | bytes 6148

commit v7 on v4

--- a/solution.py
+++ b/solution.py
@@ -128,9 +128,92 @@
     return row, owner, second
 
 
+def stack_heads(q, do, q_st, do_st, toks, to, heads):
+    sub = toks.size
+    pairs = heads // 2
+    for i in range(pairs):
+        at = i * 2 * LATENT
+        even, odd = pl.ds(to + i * sub, sub), pl.ds(to + (pairs + i) * sub, sub)
+        q_st[even, :] = q[toks, at:at + WIDTH]
+        moved = q[toks, at + LATENT - HALF:at + 2 * LATENT]
+        q_st[odd, :] = pltpu.roll(moved, WIDTH - HALF, axis=1)
+        do_st[even, :] = do[toks, pl.ds(2 * i * RANK, RANK)]
+        do_st[odd, :] = do[toks, pl.ds((2 * i + 1) * RANK, RANK)]
+
+
+def causal_bias(shape, sub):
+    key_at = lax.broadcasted_iota(jnp.int32, shape, 0)
+    tok_at = mod(lax.broadcasted_iota(jnp.int32, shape, 1), sub)
+    return jnp.where(key_at <= tok_at, 0.0, MASKED)
+
+
+def own_kernel(own, q, do, s_own, dp_own, keys, causal, q_st, do_st):
+    tok = own.shape[0]
+    sub = q.shape[0]
+    heads = 2 * PAIRS
+
+    @pl.when(pl.program_id(0) == 0)
+    def _():
+        pad = jnp.zeros((tok, HALF), jnp.float32)
+        padded = jnp.concatenate([own[...].astype(jnp.float32), pad], axis=1)
+        keys[...] = padded.astype(jnp.bfloat16)
+        causal[...] = causal_bias(causal.shape, sub)
+
+    for group in range(s_own.shape[0]):
+        cols = pl.ds(group * heads * LATENT, heads * LATENT)
+        grad_cols = pl.ds(group * heads * RANK, heads * RANK)
+        base = group * heads * sub
+        block = pl.ds(base, heads * sub)
+        stack_heads(
+            q.at[:, cols], do.at[:, grad_cols], q_st, do_st, pl.ds(0, sub), base, heads
+        )
+        out = mm(keys[...], q_st[block, :], NT)
+        s_own[group, :tok - sub] = out[:tok - sub]
+        s_own[group, tok - sub:] = out[tok - sub:] + causal[...]
+        dp_own[group] = mm(keys[:, :RANK], do_st[block, :], NT).astype(dp_own.dtype)
+
+
+def own_scores(own, queries, d_out):
+    tok = own.shape[0]
+    heads = queries.shape[1] // LATENT
+    steps = heads // (2 * PAIRS)
+    sub = token_part(tok)
+    parts = tok // sub
+    unit = 2 * PAIRS * sub
+    group = 2 if steps % 2 == 0 else 1
+    bf16, f32 = jnp.bfloat16, jnp.float32
+    return pl.pallas_call(
+        own_kernel,
+        grid=(steps // group,),
+        in_specs=[
+            pl.BlockSpec(own.shape, lambda i: (0, 0)),
+            pl.BlockSpec((sub, group * 2 * PAIRS * LATENT), lambda i: (parts - 1, i)),
+            pl.BlockSpec((sub, group * 2 * PAIRS * RANK), lambda i: (parts - 1, i)),
+        ],
+        out_specs=[pl.BlockSpec((group, tok, unit), lambda i: (i, 0, 0))] * 2,
+        out_shape=[
+            jax.ShapeDtypeStruct((steps, tok, unit), f32),
+            jax.ShapeDtypeStruct((steps, tok, unit), bf16),
+        ],
+        scratch_shapes=[
+            pltpu.VMEM((tok, WIDTH), bf16),
+            pltpu.VMEM((sub, unit), f32),
+            pltpu.VMEM((group * unit, WIDTH), bf16),
+            pltpu.VMEM((group * unit, RANK), bf16),
+        ],
+        compiler_params=pltpu.CompilerParams(vmem_limit_bytes=60 * MIB),
+        cost_estimate=pl.CostEstimate(
+            flops=2 * sub * heads * tok * (LATENT + RANK),
+            bytes_accessed=2 * sub * heads * (LATENT + RANK + 3 * tok),
+            transcendentals=0,
+        ),
+        name="own_scores",
+    )(own, queries, d_out)
+
+
 def attn_kernel(
-    owned, head_parts, ahead, anc_count, ancestors, incoming, own, q, do, dq, ds, keys_e, keys_o, sent,
-    *rest
+    owned, head_parts, ahead, anc_count, ancestors, incoming, own, s_own, dp_own, q, do,
+    dq, ds, keys_e, keys_o, sent, *rest
 ):
     own_parts = rest[:head_parts]
     far_bias, causal, q_st, s, dp, p_low, tops, acc_k, acc_v = rest[head_parts:]
@@ -154,9 +237,7 @@
         live = anc_count[lax.axis_index("leaf")]
         slot = div(lax.broadcasted_iota(jnp.int32, far_bias.shape, 0) + least, BLK)
         far_bias[...] = jnp.where(slot < live, 0.0, MASKED)
-        key_at = lax.broadcasted_iota(jnp.int32, causal.shape, 0)
-        tok_at = mod(lax.broadcasted_iota(jnp.int32, causal.shape, 1), sub)
-        causal[...] = jnp.where(key_at <= tok_at, 0.0, MASKED)
+        causal[...] = causal_bias(causal.shape, sub)
         acc_k[...] = jnp.zeros_like(acc_k)
         acc_v[...] = jnp.zeros_like(acc_v)
 
@@ -185,14 +266,20 @@
     def fold(x):
         return x.reshape(-1, 8, x.shape[1])
 
+    def given(j):
+        return j == parts - 1
+
     def score(j, at):
         n, cols = seen(j), pl.ds(j * stack + at, stack // 2)
-        out = mm(keys_e[:n, :], q_st[cols, :].T, NN)
+        out = mm(keys_e[:far_rows if given(j) else n, :], q_st[cols, :].T, NN)
         near = [(0, out[:least]), (least, out[least:far_rows] + far_bias[...])]
-        if j > 0:
-            near.append((far_rows, out[far_rows:n - sub]))
-        near.append((n - sub, out[n - sub:] + causal[...]))
         top = None
+        if given(j):
+            top = jnp.max(fold(s_own[0, :, pl.ds(at, stack // 2)]), axis=0)
+        else:
+            if j > 0:
+                near.append((far_rows, out[far_rows:n - sub]))
+            near.append((n - sub, out[n - sub:] + causal[...]))
         for r, part in near:
             s[pl.ds(r, part.shape[0]), cols] = part
             part = jnp.max(fold(part), axis=0)
@@ -200,10 +287,20 @@
         tops[:, cols] = top
 
     def prob(j, at):
-        n, cols = seen(j), pl.ds(j * stack + at, stack // 2)
+        n, cols = far_rows if given(j) else seen(j), pl.ds(j * stack + at, stack // 2)
         dp[:n, cols] = mm(keys_e[:n, :RANK], grads(j, at // sub, PAIRS).T, NN)
 
     state = {}
+
+    def scores_at(j, r, n, at):
+        if given(j) and r >= far_rows:
+            return s_own[0, pl.ds(r - far_rows, n), pl.ds(at, LANES)]
+        return s[pl.ds(r, n), pl.ds(j * stack + at, LANES)]
+
+    def probs_at(j, r, n, at):
+        if given(j) and r >= far_rows:
+            return dp_own[0, pl.ds(r - far_rows, n), pl.ds(at, LANES)].astype(jnp.float32)
+        return dp[pl.ds(r, n), pl.ds(j * stack + at, LANES)]
 
     def soft_sums(j, at):
         lane = pl.ds(j * stack + at, LANES)
@@ -211,10 +308,10 @@
         total = jnp.zeros((8, LANES), jnp.float32)
         delta = jnp.zeros((8, LANES), jnp.float32)
         for r, n in pieces(seen(j), 64):
-            e = jnp.exp2((s[pl.ds(r, n), lane] - top) * EXP_SCALE)
+            e = jnp.exp2((scores_at(j, r, n, at) - top) * EXP_SCALE)
             s[pl.ds(r, n), lane] = e
             total += jnp.sum(fold(e), axis=0)
-            delta += jnp.sum(fold(e * dp[pl.ds(r, n), lane]), axis=0)
+            delta += jnp.sum(fold(e * probs_at(j, r, n, at)), axis=0)
         inv = 1.0 / jnp.sum(total, axis=0, keepdims=True)
         state[j, at] = inv, jnp.sum(delta, axis=0, keepdims=True) * inv
 
@@ -224,7 +321,7 @@
         for r, n in pieces(seen(j), 64):
             p = s[pl.ds(r, n), lane] * inv
             p_low[pl.ds(r, n), lane] = p.astype(jnp.bfloat16)
-            ds[0, pl.ds(r, n), lane] = (p * (dp[pl.ds(r, n), lane] - delta)).astype(ds.dtype)
+            ds[0, pl.ds(r, n), lane] = (p * (probs_at(j, r, n, at) - delta)).astype(ds.dtype)
 
     def grad_values(j, at, size):
         n, cols = seen(j), pl.ds(at, size)
@@ -283,7 +380,9 @@
     return steps * 3 // 8
 
 
-def attention(owned, head_parts, anc_count, ancestors, incoming, own, queries, d_out):
+def attention(
+    owned, head_parts, anc_count, ancestors, incoming, own, s_own, dp_own, queries, d_out
+):
     tok = queries.shape[0]
     heads = queries.shape[1] // LATENT
     steps = heads // (2 * PAIRS)
@@ -308,6 +407,8 @@
             pl.BlockSpec(ancestors.shape, whole),
             pl.BlockSpec(incoming.shape, whole),
             pl.BlockSpec(own.shape, whole),
+            pl.BlockSpec((1,) + s_own.shape[1:], lambda i: (i, 0, 0)),
+            pl.BlockSpec((1,) + dp_own.shape[1:], lambda i: (i, 0, 0)),
             pl.BlockSpec((tok, 2 * PAIRS * LATENT), along),
             pl.BlockSpec((tok, 2 * PAIRS * RANK), along),
         ],
@@ -345,7 +446,7 @@
             transcendentals=tok * heads * rows,
         ),
         name="score_gradients",
-    )(anc_count, ancestors, incoming, own, queries, d_out)
+    )(anc_count, ancestors, incoming, own, s_own, dp_own, queries, d_out)
 
 
 def put_queries(dq, ds, keys_e, keys_o):
@@ -410,8 +511,11 @@
         outgoing.reshape(leafs, CAP * BLK, LATENT), "leaf", split_axis=0, concat_axis=0, tiled=True
     ).reshape(leafs * CAP * BLK, LATENT)
 
+    s_own, dp_own = own_scores(branch_latent, queries, d_out)
+
     started, ds, keys_e, keys_o, sent, mine, *others = attention(
-        owned, head_parts, anc_count, ancestors, incoming, branch_latent, queries, d_out
+        owned, head_parts, anc_count, ancestors, incoming, branch_latent, s_own, dp_own,
+        queries, d_out,
     )
 
     got = lax.all_to_all(

time: 79.2 us -> 78.5 us (level)
  blocking collectives: 18.6 us -> 0 us
  starting transfers between devices: 5.02 us -> 12.4 us
  Pallas kernels: 54.5 us -> 60.7 us
  waiting for transfers between devices: 0.01 us -> 3.46 us
    all_to_all x1 -> x0, blocking collectives: 18.6 us -> none  [local(): lax.all_to_all(outgoing.reshape(leafs, CAP * BLK, LATENT), 'leaf', split_...]
    pallas_call x0 -> x1, Pallas kernels: none -> 7.65 us  [own_scores(): pl.pallas_call(own_kernel, grid=(steps // group,), in_specs=[pl.BlockSpec...]
    all_to_all x0 -> x1, starting transfers between devices: none -> 7.36 us  [local(): lax.all_to_all(outgoing.reshape(leafs, CAP * BLK, LATENT), 'leaf', split_...]
    all_to_all x0 -> x1, waiting for transfers between devices: none -> 3.45 us  [local(): lax.all_to_all(outgoing.reshape(leafs, CAP * BLK, LATENT), 'leaf', split_...]
    pallas_call x1, Pallas kernels: 40.6 us -> 39.2 us  [attention(): pl.pallas_call(functools.partial(attn_kernel, owned, head_parts, ahead),...]
  transfers between devices with their start and end apart: 2 -> 3, of which waited for: 0 -> 1; matrix products, arithmetic and copies ran while one was open for 0% -> 0% of each run, Pallas kernels for 14% -> 24%
where the time goes in v7:
time: 78.5 us; the launch traced here: 78 us
  Pallas kernels  60.7 us (77%)
  starting transfers between devices  12.4 us (16%)
  waiting for transfers between devices  3.46 us (4%)
    pallas_call x1, Pallas kernels, attention(): pl.pallas_call(functools.partial(attn_kernel, owned, head_parts, ahead),...  39.2 us
    pallas_call x1, Pallas kernels, query_gradients(): pl.pallas_call(query_kernel, grid=(steps,), in_specs=[pl.BlockSpec(keys_e...  11 us
    pallas_call x1, Pallas kernels, own_scores(): pl.pallas_call(own_kernel, grid=(steps // group,), in_specs=[pl.BlockSpec...  7.65 us
    all_to_all x1, starting transfers between devices, local(): lax.all_to_all(outgoing.reshape(leafs, CAP * BLK, LATENT), 'leaf', split_...  7.36 us
    all_to_all x1, waiting for transfers between devices, local(): lax.all_to_all(outgoing.reshape(leafs, CAP * BLK, LATENT), 'leaf', split_...  3.45 us
    all_to_all x1, starting transfers between devices, local(): lax.all_to_all(sent.reshape(leafs * head_parts, CAP * part_rows, LATENT),...  3.2 us
    pallas_call x1, Pallas kernels, pick(): pl.pallas_call(pick_kernel, out_shape=jax.ShapeDtypeStruct((rows, LATENT)...  1.97 us
    ppermute x1, starting transfers between devices, local(): theirs.append(lax.ppermute(part, 'head', route))  1.83 us
  transfers between devices with their start and end apart: 3, of which 1 were waited for; matrix products, arithmetic and copies ran while one was open for 0% of the time, Pallas kernels for 24%

profile of v7, /device:TPU:0, one launch (start us, length us, event | category | flops | bytes accessed | tf_op | source)
XLA Modules:
  0.0 78.0 jit_solution(14907723629661332168)
XLA Ops:
  0.6 2.0 %pick_blocks.1 = bf16[256,576]{1,0:T(8,128)(2,1)} custom-call(s32[16,32]{1,0:T(8,128)} %ancestors.5, bf16[128,576]{1,0:T(8,128)(2,1)} %bitcast.9), custom_call_target="tpu_custom_call" | custom-call | tf_op jit(solution)/shard_map/pick_blocks/pallas_call | solution.py:84
  2.6 7.4 %all-to-all-start = ((bf16[16,16,576]{2,1,0:T(8,128)(2,1)}), bf16[16,16,576]{2,1,0:T(8,128)(2,1)S(1)}, u32[]{:S(2)}, u32[]{:S(2)}) async-start(bf16[16,16,576]{2,1,0:T(8,128)(2,1)} %bitcast.6), calls=%async_computation | async-start | bytes 655360 | tf_op jit(solution)/shard_map/all_to_all | solution.py:510
  10.0 7.6 %own_scores.1 = (f32[8,192,512]{2,1,0:T(8,128)}, bf16[8,192,512]{2,1,0:T(8,128)(2,1)}) custom-call(bf16[192,576]{1,0:T(8,128)(2,1)} %own.3, bf16[192,36864]{1,0:T(8,128)(2,1)} %q.3, bf16[192,32768]{1,0:T(8,128)(2,1)} %do.3), custom_call_target="tpu_custom_call" | custom-call | flops 1711276032 | bytes 13631488 | tf_op jit(solution)/shard_map/own_scores/pallas_call | solution.py:185
  17.6 3.5 %all-to-all-done = bf16[16,16,576]{2,1,0:T(8,128)(2,1)S(1)} async-done(((bf16[16,16,576]{2,1,0:T(8,128)(2,1)}), bf16[16,16,576]{2,1,0:T(8,128)(2,1)S(1)}, u32[]{:S(2)}, u32[]{:S(2)}) %all-to-all-start) | async-done | bytes 294944 | tf_op jit(solution)/shard_map/all_to_all | solution.py:510
  21.1 0.0 copy-start.2
  21.1 0.8 copy-done.2
  21.8 39.2 %score_gradients.1 = (bf16[192,36864]{1,0:T(8,128)(2,1)}, bf16[5,448,1536]{2,1,0:T(8,128)(2,1)}, bf16[448,640]{1,0:T(8,128)(2,1)}, bf16[448,640]{1,0:T(8,128)(2,...) custom-call(s32[16]{0:T(128)} %anc_count.1, s32[16,32]{1,0:T(8,128)} %ancestors.5, ...), custom_call_target="tpu_custom_call" | custom-call | flops 23957864448 | bytes 37748736 | tf_op jit(solution)/shard_map/score_gradients/pallas_call | solution.py:402
  61.0 3.2 %all-to-all-start.1 = ((bf16[32,8,576]{2,1,0:T(8,128)(2,1)}), bf16[32,8,576]{2,1,0:T(8,128)(2,1)S(1)}, u32[]{:S(2)}, u32[]{:S(2)}) async-start(bf16[32,8,576]{2,1,0:T(8,128)(2,1)} %bitcast.7), calls=%async_computation.1 | async-start | bytes 655360 | tf_op jit(solution)/shard_map/all_to_all | solution.py:521
  64.2 1.8 %collective-permute-start = (f32[96,576]{1,0:T(8,128)}, f32[96,576]{1,0:T(8,128)S(1)}, u32[]{:S(2)}, u32[]{:S(2)}) collective-permute-start(f32[96,576]{1,0:T(8,128)} %get-tuple-element.22), channel_id=1, source_target_pairs={{0,1},{1,0},{2,3},{3,2},{4,5},{5,4},{6,7},{7,6},{8,9},{9,8},{10,11... | collective-permute-start | bytes 663560 | tf_op jit(solution)/shard_map/ppermute | solution.py:528
  66.0 0.0 copy-start
  66.1 0.0 copy-start.1
  66.1 11.0 %query_gradients.1 = bf16[192,36864]{1,0:T(8,128)(2,1)} custom-call(bf16[448,640]{1,0:T(8,128)(2,1)} %get-tuple-element.16.keys_e, bf16[448,640]{1,0:T(8,128)(2,1)} %get-tuple-element.17.keys_o, bf16[5,448,1536]{2,1,0:T(8,128)(2,1)} %get-tuple-element.18.ds, bf16[192,36864]{1,0:T(8,128)(2,1)} %get-tuple-element.19.started), custom_call_target="tpu_custom_call", output_to_operand_aliasing={{}: (3, {})} | custom-call | flops 3963617280 | bytes 15728640 | tf_op jit(solution)/shard_map/query_gradients/pallas_call | solution.py:481
  77.0 0.0 collective-permute-done.rest_0_
  77.0 0.0 all-to-all-done.1
  77.0 0.0 copy-done
  77.0 0.0 copy-done.1
  77.0 1.0 %sum_gradients.1 = (f32[96,576]{1,0:T(8,128)}, f32[16,4,576]{2,1,0:T(4,128)}) custom-call(s32[16,32]{1,0:T(8,128)S(1)} %copy-done.1, bf16[256,576]{1,0:T(8,128)(2,1)S(1)} %bitcast.5, f32[96,576]{1,0:T(8,128)S(1)} %copy-done, f32[96,576]{1,0:T(8,128)S(1)} %collective-permute-done.rest_0_), custom_call_target="tpu_custom_call" | custom-call | tf_op jit(solution)/shard_map/sum_gradients/pallas_call | solution.py:107
Async XLA Ops:
  2.6 18.5 %all-to-all-start = ((bf16[16,16,576]{2,1,0:T(8,128)(2,1)}), bf16[16,16,576]{2,1,0:T(8,128)(2,1)S(1)}, u32[]{:S(2)}, u32[]{:S(2)}) async-start(bf16[16,16,576]{2,1,0:T(8,128)(2,1)} %bitcast.6), calls=%async_computation | async-start | bytes 655360 | tf_op jit(solution)/shard_map/all_to_all | solution.py:510
  21.1 0.8 copy-start.2
  61.0 16.0 %all-to-all-start.1 = ((bf16[32,8,576]{2,1,0:T(8,128)(2,1)}), bf16[32,8,576]{2,1,0:T(8,128)(2,1)S(1)}, u32[]{:S(2)}, u32[]{:S(2)}) async-start(bf16[32,8,576]{2,1,0:T(8,128)(2,1)} %bitcast.7), calls=%async_computation.1 | async-start | bytes 655360 | tf_op jit(solution)/shard_map/all_to_all | solution.py:521
  64.2 12.8 %collective-permute-start = (f32[96,576]{1,0:T(8,128)}, f32[96,576]{1,0:T(8,128)S(1)}, u32[]{:S(2)}, u32[]{:S(2)}) collective-permute-start(f32[96,576]{1,0:T(8,128)} %get-tuple-element.22), channel_id=1, source_target_pairs={{0,1},{1,0},{2,3},{3,2},{4,5},{5,4},{6,7},{7,6},{8,9},{9,8},{10,11... | collective-permute-start | bytes 663560 | tf_op jit(solution)/shard_map/ppermute | solution.py:528
  66.0 11.0 %copy-start = (f32[96,576]{1,0:T(8,128)S(1)}, f32[96,576]{1,0:T(8,128)}, u32[]{:S(2)}) copy-start(f32[96,576]{1,0:T(8,128)} %get-tuple-element.21.mine) | copy-start | bytes 663556
  66.1 11.0 %copy-start.1 = (s32[16,32]{1,0:T(8,128)S(1)}, s32[16,32]{1,0:T(8,128)}, u32[]{:S(2)}) copy-start(s32[16,32]{1,0:T(8,128)} %ancestors.5) | copy-start | bytes 6148

commit v8 on v7

--- a/solution.py
+++ b/solution.py
@@ -71,18 +71,19 @@
     return jnp.where(second, high, low).astype(jnp.int32) - first
 
 
-def pick_kernel(ancestors, trunk, out):
+def pick_kernel(head_parts, ancestors, trunk, out):
     owned = trunk.shape[0] // BLK
-    row = column(out.shape[0])
-    block = listed_blocks(ancestors, owned, mod(div(row, BLK), CAP) == 1)
+    share = CAP * BLK // head_parts
+    row = lax.axis_index("head") * share + mod(column(out.shape[0]), share)
+    block = listed_blocks(ancestors, owned, div(row, BLK) == 1)
     sel = one_hot(block * BLK + mod(row, BLK), trunk.shape[0])
     out[...] = mm(sel, trunk[...], NN).astype(out.dtype)
 
 
-def pick(ancestors, trunk):
+def pick(head_parts, ancestors, trunk):
     rows = ancestors.shape[0] * CAP * BLK
     return pl.pallas_call(
-        pick_kernel,
+        functools.partial(pick_kernel, head_parts),
         out_shape=jax.ShapeDtypeStruct((rows, LATENT), trunk.dtype),
         name="pick_blocks",
     )(ancestors, trunk)
@@ -506,9 +507,10 @@
     owned = trunk_latent.shape[0]
     part_rows = BLK // head_parts
 
-    outgoing = pick(ancestors, trunk_latent.reshape(owned * BLK, LATENT))
+    outgoing = pick(head_parts, ancestors, trunk_latent.reshape(owned * BLK, LATENT))
     incoming = lax.all_to_all(
-        outgoing.reshape(leafs, CAP * BLK, LATENT), "leaf", split_axis=0, concat_axis=0, tiled=True
+        outgoing.reshape(leafs * head_parts, CAP * part_rows, LATENT),
+        ("leaf", "head"), split_axis=0, concat_axis=0, tiled=True,
     ).reshape(leafs * CAP * BLK, LATENT)
 
     s_own, dp_own = own_scores(branch_latent, queries, d_out)

time: 78.5 us -> 78.5 us (level)
  no operation moved by 1% of the time
where the time goes in v8:
time: 78.5 us; the launch traced here: 78.1 us
  Pallas kernels  60.8 us (77%)
  starting transfers between devices  11.8 us (15%)
  waiting for transfers between devices  4.08 us (5%)
    pallas_call x1, Pallas kernels, attention(): pl.pallas_call(functools.partial(attn_kernel, owned, head_parts, ahead),...  39.2 us
    pallas_call x1, Pallas kernels, query_gradients(): pl.pallas_call(query_kernel, grid=(steps,), in_specs=[pl.BlockSpec(keys_e...  11 us
    pallas_call x1, Pallas kernels, own_scores(): pl.pallas_call(own_kernel, grid=(steps // group,), in_specs=[pl.BlockSpec...  7.64 us
    all_to_all x1, starting transfers between devices, local(): lax.all_to_all(outgoing.reshape(leafs * head_parts, CAP * part_rows, LATE...  7.3 us
    all_to_all x1, waiting for transfers between devices, local(): lax.all_to_all(outgoing.reshape(leafs * head_parts, CAP * part_rows, LATE...  4.08 us
    all_to_all x1, starting transfers between devices, local(): lax.all_to_all(sent.reshape(leafs * head_parts, CAP * part_rows, LATENT),...  2.69 us
    pallas_call x1, Pallas kernels, pick(): pl.pallas_call(functools.partial(pick_kernel, head_parts), out_shape=jax....  1.98 us
    ppermute x1, starting transfers between devices, local(): theirs.append(lax.ppermute(part, 'head', route))  1.83 us
  transfers between devices with their start and end apart: 3, of which 1 were waited for; matrix products, arithmetic and copies ran while one was open for 0% of the time, Pallas kernels for 24%

profile of v8, /device:TPU:0, one launch (start us, length us, event | category | flops | bytes accessed | tf_op | source)
XLA Modules:
  0.0 78.1 jit_solution(7629063245738904613)
XLA Ops:
  0.6 2.0 %pick_blocks.1 = bf16[256,576]{1,0:T(8,128)(2,1)} custom-call(s32[16,32]{1,0:T(8,128)} %ancestors.5, bf16[128,576]{1,0:T(8,128)(2,1)} %bitcast.9), custom_call_target="tpu_custom_call" | custom-call | tf_op jit(solution)/shard_map/pick_blocks/pallas_call | solution.py:85
  2.6 7.3 %all-to-all-start = ((bf16[32,8,576]{2,1,0:T(8,128)(2,1)}), bf16[32,8,576]{2,1,0:T(8,128)(2,1)S(1)}, u32[]{:S(2)}, u32[]{:S(2)}) async-start(bf16[32,8,576]{2,1,0:T(8,128)(2,1)} %bitcast.6), calls=%async_computation | async-start | bytes 655360 | tf_op jit(solution)/shard_map/all_to_all | solution.py:511
  9.9 7.6 %own_scores.1 = (f32[8,192,512]{2,1,0:T(8,128)}, bf16[8,192,512]{2,1,0:T(8,128)(2,1)}) custom-call(bf16[192,576]{1,0:T(8,128)(2,1)} %own.3, bf16[192,36864]{1,0:T(8,128)(2,1)} %q.3, bf16[192,32768]{1,0:T(8,128)(2,1)} %do.3), custom_call_target="tpu_custom_call" | custom-call | flops 1711276032 | bytes 13631488 | tf_op jit(solution)/shard_map/own_scores/pallas_call | solution.py:186
  17.6 4.1 %all-to-all-done = bf16[32,8,576]{2,1,0:T(8,128)(2,1)S(1)} async-done(((bf16[32,8,576]{2,1,0:T(8,128)(2,1)}), bf16[32,8,576]{2,1,0:T(8,128)(2,1)S(1)}, u32[]{:S(2)}, u32[]{:S(2)}) %all-to-all-start) | async-done | bytes 294944 | tf_op jit(solution)/shard_map/all_to_all | solution.py:511
  21.6 0.0 copy-start.2
  21.6 0.8 copy-done.2
  22.4 39.2 %score_gradients.1 = (bf16[192,36864]{1,0:T(8,128)(2,1)}, bf16[5,448,1536]{2,1,0:T(8,128)(2,1)}, bf16[448,640]{1,0:T(8,128)(2,1)}, bf16[448,640]{1,0:T(8,128)(2,...) custom-call(s32[16]{0:T(128)} %anc_count.1, s32[16,32]{1,0:T(8,128)} %ancestors.5, ...), custom_call_target="tpu_custom_call" | custom-call | flops 23957864448 | bytes 37748736 | tf_op jit(solution)/shard_map/score_gradients/pallas_call | solution.py:403
  61.6 2.7 %all-to-all-start.1 = ((bf16[32,8,576]{2,1,0:T(8,128)(2,1)}), bf16[32,8,576]{2,1,0:T(8,128)(2,1)S(1)}, u32[]{:S(2)}, u32[]{:S(2)}) async-start(bf16[32,8,576]{2,1,0:T(8,128)(2,1)} %bitcast.7), calls=%async_computation.1 | async-start | bytes 655360 | tf_op jit(solution)/shard_map/all_to_all | solution.py:523
  64.3 1.8 %collective-permute-start = (f32[96,576]{1,0:T(8,128)}, f32[96,576]{1,0:T(8,128)S(1)}, u32[]{:S(2)}, u32[]{:S(2)}) collective-permute-start(f32[96,576]{1,0:T(8,128)} %get-tuple-element.22), channel_id=1, source_target_pairs={{0,1},{1,0},{2,3},{3,2},{4,5},{5,4},{6,7},{7,6},{8,9},{9,8},{10,11... | collective-permute-start | bytes 663560 | tf_op jit(solution)/shard_map/ppermute | solution.py:530
  66.1 0.0 copy-start
  66.1 0.0 copy-start.1
  66.1 11.0 %query_gradients.1 = bf16[192,36864]{1,0:T(8,128)(2,1)} custom-call(bf16[448,640]{1,0:T(8,128)(2,1)} %get-tuple-element.16.keys_e, bf16[448,640]{1,0:T(8,128)(2,1)} %get-tuple-element.17.keys_o, bf16[5,448,1536]{2,1,0:T(8,128)(2,1)} %get-tuple-element.18.ds, bf16[192,36864]{1,0:T(8,128)(2,1)} %get-tuple-element.19.started), custom_call_target="tpu_custom_call", output_to_operand_aliasing={{}: (3, {})} | custom-call | flops 3963617280 | bytes 15728640 | tf_op jit(solution)/shard_map/query_gradients/pallas_call | solution.py:482
  77.1 0.0 collective-permute-done.rest_0_
  77.1 0.0 all-to-all-done.1
  77.1 0.0 copy-done
  77.1 0.0 copy-done.1
  77.1 1.0 %sum_gradients.1 = (f32[96,576]{1,0:T(8,128)}, f32[16,4,576]{2,1,0:T(4,128)}) custom-call(s32[16,32]{1,0:T(8,128)S(1)} %copy-done.1, bf16[256,576]{1,0:T(8,128)(2,1)S(1)} %bitcast.5, f32[96,576]{1,0:T(8,128)S(1)} %copy-done, f32[96,576]{1,0:T(8,128)S(1)} %collective-permute-done.rest_0_), custom_call_target="tpu_custom_call" | custom-call | tf_op jit(solution)/shard_map/sum_gradients/pallas_call | solution.py:108
Async XLA Ops:
  2.6 19.0 %all-to-all-start = ((bf16[32,8,576]{2,1,0:T(8,128)(2,1)}), bf16[32,8,576]{2,1,0:T(8,128)(2,1)S(1)}, u32[]{:S(2)}, u32[]{:S(2)}) async-start(bf16[32,8,576]{2,1,0:T(8,128)(2,1)} %bitcast.6), calls=%async_computation | async-start | bytes 655360 | tf_op jit(solution)/shard_map/all_to_all | solution.py:511
  21.6 0.8 copy-start.2
  61.6 15.5 %all-to-all-start.1 = ((bf16[32,8,576]{2,1,0:T(8,128)(2,1)}), bf16[32,8,576]{2,1,0:T(8,128)(2,1)S(1)}, u32[]{:S(2)}, u32[]{:S(2)}) async-start(bf16[32,8,576]{2,1,0:T(8,128)(2,1)} %bitcast.7), calls=%async_computation.1 | async-start | bytes 655360 | tf_op jit(solution)/shard_map/all_to_all | solution.py:523
  64.3 12.8 %collective-permute-start = (f32[96,576]{1,0:T(8,128)}, f32[96,576]{1,0:T(8,128)S(1)}, u32[]{:S(2)}, u32[]{:S(2)}) collective-permute-start(f32[96,576]{1,0:T(8,128)} %get-tuple-element.22), channel_id=1, source_target_pairs={{0,1},{1,0},{2,3},{3,2},{4,5},{5,4},{6,7},{7,6},{8,9},{9,8},{10,11... | collective-permute-start | bytes 663560 | tf_op jit(solution)/shard_map/ppermute | solution.py:530
  66.1 11.0 %copy-start = (f32[96,576]{1,0:T(8,128)S(1)}, f32[96,576]{1,0:T(8,128)}, u32[]{:S(2)}) copy-start(f32[96,576]{1,0:T(8,128)} %get-tuple-element.21.mine) | copy-start | bytes 663556
  66.1 11.0 %copy-start.1 = (s32[16,32]{1,0:T(8,128)S(1)}, s32[16,32]{1,0:T(8,128)}, u32[]{:S(2)}) copy-start(s32[16,32]{1,0:T(8,128)} %ancestors.5) | copy-start | bytes 6148

commit v9 on v7

--- a/solution.py
+++ b/solution.py
@@ -54,6 +54,12 @@
     return jnp.where(lane == place, 1.0, 0.0).astype(jnp.bfloat16)
 
 
+def seen_rows(rows, tok):
+    sub = token_part(tok)
+    seen = [rows - tok + (j + 1) * sub for j in range(tok // sub)]
+    return seen, [sum(seen[:j]) for j in range(len(seen) + 1)]
+
+
 def token_part(tok):
     return 64 if tok % 64 == 0 else tok
 
@@ -84,6 +90,7 @@
     return pl.pallas_call(
         pick_kernel,
         out_shape=jax.ShapeDtypeStruct((rows, LATENT), trunk.dtype),
+        compiler_params=pltpu.CompilerParams(vmem_limit_bytes=8 * MIB),
         name="pick_blocks",
     )(ancestors, trunk)
 
@@ -213,10 +220,11 @@
 
 def attn_kernel(
     owned, head_parts, ahead, anc_count, ancestors, incoming, own, s_own, dp_own, q, do,
-    dq, ds, keys_e, keys_o, sent, *rest
+    dq, ds, keys_out_e, keys_out_o, sent, *rest
 ):
     own_parts = rest[:head_parts]
-    far_bias, causal, q_st, s, dp, p_low, tops, acc_k, acc_v = rest[head_parts:]
+    scratch = rest[head_parts:]
+    k_e, k_o, sems, far_bias, causal, q_st, s, dp, p_low, tops, acc_k, acc_v = scratch
     tok = q.shape[0]
     far_rows, rows = ANC * BLK, ANC * BLK + tok
     sub = token_part(tok)
@@ -224,6 +232,10 @@
     stack = 2 * PAIRS * sub
     least = LEAST_LIVE * BLK
     step = pl.program_id(0)
+    key_copies = [
+        pltpu.make_async_copy(k_e, keys_out_e, sems.at[0]),
+        pltpu.make_async_copy(k_o, keys_out_o, sems.at[1]),
+    ]
 
     @pl.when(step == 0)
     def _():
@@ -232,8 +244,10 @@
         far = mm(sel, incoming[...], NN)
         joined = jnp.concatenate([far, own[...].astype(jnp.float32)], axis=0)
         padded = jnp.concatenate([joined, jnp.zeros((rows, HALF), jnp.float32)], axis=1)
-        keys_e[...] = padded.astype(jnp.bfloat16)
-        keys_o[...] = pltpu.roll(padded, HALF, axis=1).astype(jnp.bfloat16)
+        k_e[...] = padded.astype(jnp.bfloat16)
+        k_o[...] = pltpu.roll(padded, HALF, axis=1).astype(jnp.bfloat16)
+        for copy in key_copies:
+            copy.start()
         live = anc_count[lax.axis_index("leaf")]
         slot = div(lax.broadcasted_iota(jnp.int32, far_bias.shape, 0) + least, BLK)
         far_bias[...] = jnp.where(slot < live, 0.0, MASKED)
@@ -241,8 +255,10 @@
         acc_k[...] = jnp.zeros_like(acc_k)
         acc_v[...] = jnp.zeros_like(acc_v)
 
+    seen_of, starts = seen_rows(rows, tok)
+
     def seen(j):
-        return far_rows + (j + 1) * sub
+        return seen_of[j]
 
     def lanes(j):
         return pl.ds(j * stack, stack)
@@ -271,7 +287,7 @@
 
     def score(j, at):
         n, cols = seen(j), pl.ds(j * stack + at, stack // 2)
-        out = mm(keys_e[:far_rows if given(j) else n, :], q_st[cols, :].T, NN)
+        out = mm(k_e[:far_rows if given(j) else n, :], q_st[cols, :].T, NN)
         near = [(0, out[:least]), (least, out[least:far_rows] + far_bias[...])]
         top = None
         if given(j):
@@ -288,7 +304,7 @@
 
     def prob(j, at):
         n, cols = far_rows if given(j) else seen(j), pl.ds(j * stack + at, stack // 2)
-        dp[:n, cols] = mm(keys_e[:n, :RANK], grads(j, at // sub, PAIRS).T, NN)
+        dp[:n, cols] = mm(k_e[:n, :RANK], grads(j, at // sub, PAIRS).T, NN)
 
     state = {}
 
@@ -321,7 +337,7 @@
         for r, n in pieces(seen(j), 64):
             p = s[pl.ds(r, n), lane] * inv
             p_low[pl.ds(r, n), lane] = p.astype(jnp.bfloat16)
-            ds[0, pl.ds(r, n), lane] = (p * (probs_at(j, r, n, at) - delta)).astype(ds.dtype)
+            ds[0, pl.ds(starts[j] + r, n), pl.ds(at, LANES)] = (p * (probs_at(j, r, n, at) - delta)).astype(ds.dtype)
 
     def grad_values(j, at, size):
         n, cols = seen(j), pl.ds(at, size)
@@ -329,7 +345,7 @@
 
     def grad_keys(j, at, size):
         n, cols = seen(j), pl.ds(at, size)
-        acc_k[:n, cols] += mm(ds[0, :n, lanes(j)], q_st[lanes(j), cols], NN)
+        acc_k[:n, cols] += mm(ds[0, pl.ds(starts[j], n), :], q_st[lanes(j), cols], NN)
 
     def jobs_of(i):
         products, passes = [], []
@@ -355,7 +371,7 @@
 
     @pl.when(step < ahead)
     def _():
-        put_queries(dq, ds, keys_e, keys_o)
+        put_queries(dq, ds, k_e, k_o)
 
     @pl.when(step == pl.num_programs(0) - 1)
     def _():
@@ -374,6 +390,8 @@
             part = lax.rem(lax.axis_index("head") + hop, head_parts)
             at = pl.multiple_of(far_rows + part * own_rows, 8)
             out[...] = acc_k[pl.ds(at, own_rows), :LATENT]
+        for copy in key_copies:
+            copy.wait()
 
 
 def steps_ahead(steps):
@@ -390,6 +408,7 @@
     far_rows, rows = ANC * BLK, ANC * BLK + tok
     toks = 2 * PAIRS * tok
     stack = 2 * PAIRS * token_part(tok)
+    ds_rows = seen_rows(rows, tok)[1][-1]
     bf16, f32 = jnp.bfloat16, jnp.float32
 
     def whole(i):
@@ -416,19 +435,22 @@
             pl.BlockSpec(
                 (tok, 2 * PAIRS * LATENT), lambda i: (0, jnp.minimum(i, max(ahead - 1, 0)))
             ),
-            pl.BlockSpec((1, rows, toks), lambda i: (jnp.maximum(i - ahead, 0), 0, 0)),
-            pl.BlockSpec((rows, WIDTH), whole),
-            pl.BlockSpec((rows, WIDTH), whole),
+            pl.BlockSpec((1, ds_rows, stack), lambda i: (jnp.maximum(i - ahead, 0), 0, 0)),
+            pl.BlockSpec(memory_space=pl.ANY),
+            pl.BlockSpec(memory_space=pl.ANY),
             pl.BlockSpec(incoming.shape, whole),
         ] + [pl.BlockSpec(own_part, whole)] * head_parts,
         out_shape=[
             jax.ShapeDtypeStruct(queries.shape, bf16),
-            jax.ShapeDtypeStruct((steps - ahead, rows, toks), bf16),
+            jax.ShapeDtypeStruct((steps - ahead, ds_rows, stack), bf16),
             jax.ShapeDtypeStruct((rows, WIDTH), bf16),
             jax.ShapeDtypeStruct((rows, WIDTH), bf16),
             jax.ShapeDtypeStruct(incoming.shape, bf16),
         ] + [jax.ShapeDtypeStruct(own_part, f32)] * head_parts,
         scratch_shapes=[
+            pltpu.VMEM((rows, WIDTH), bf16),
+            pltpu.VMEM((rows, WIDTH), bf16),
+            pltpu.SemaphoreType.DMA((2,)),
             pltpu.VMEM((far_rows - LEAST_LIVE * BLK, stack // 2), f32),
             pltpu.VMEM((token_part(tok), stack // 2), f32),
             pltpu.VMEM((toks, WIDTH), bf16),
@@ -451,14 +473,14 @@
 
 def put_queries(dq, ds, keys_e, keys_o):
     tok = dq.shape[0]
-    rows = ds.shape[1]
     sub = token_part(tok)
     stack = PAIRS * sub
     low = LATENT - HALF
-    for j in range(tok // sub):
-        n = rows - tok + (j + 1) * sub
-        even = mm(ds[0, :n, pl.ds(2 * j * stack, stack)], keys_e[:n, :], TN) * SCALE
-        odd = mm(ds[0, :n, pl.ds((2 * j + 1) * stack, stack)], keys_o[:n, :], TN) * SCALE
+    seen, starts = seen_rows(keys_e.shape[0], tok)
+    for j, n in enumerate(seen):
+        block = pl.ds(starts[j], n)
+        even = mm(ds[0, block, :stack], keys_e[:n, :], TN) * SCALE
+        odd = mm(ds[0, block, stack:], keys_o[:n, :], TN) * SCALE
         for i in range(PAIRS):
             at = i * 2 * LATENT
             part = slice(i * sub, (i + 1) * sub)
@@ -475,9 +497,8 @@
 
 def query_gradients(keys_e, keys_o, ds, started):
     tok = started.shape[0]
-    steps = ds.shape[0]
+    steps, rows = ds.shape[0], keys_e.shape[0]
     ahead = started.shape[1] // (2 * PAIRS * LATENT) - steps
-    rows = ds.shape[1]
     return pl.pallas_call(
         query_kernel,
         grid=(steps,),
@@ -518,15 +539,14 @@
         queries, d_out,
     )
 
+    theirs = []
+    for hop, part in enumerate(others, 1):
+        route = [(i, (i + hop) % head_parts) for i in range(head_parts)]
+        theirs.append(lax.ppermute(part, "head", route))
     got = lax.all_to_all(
         sent.reshape(leafs * head_parts, CAP * part_rows, LATENT),
         ("leaf", "head"), split_axis=0, concat_axis=0, tiled=True,
     ).reshape(leafs * CAP * BLK, LATENT)
-    theirs = []
-    for hop, part in enumerate(others, 1):
-        route = [(i, (i + hop) % head_parts) for i in range(head_parts)]
-        theirs.append(lax.ppermute(part, "head", route))
-
     d_queries = query_gradients(keys_e, keys_o, ds, started)
     d_branch, d_trunk = finish(ancestors, got, mine, theirs, owned, part_rows)
     return d_queries, d_branch, d_trunk

time: 78.5 us -> 78.7 us (level)
  local copies, waits for them, and re-layouts: 0.77 us -> 2.33 us
  Pallas kernels: 60.7 us -> 59.4 us
    unnamed x6 -> x10, local copies, waits for them, and re-layouts: 0.77 us -> 2.33 us
    pallas_call x1, Pallas kernels: 1.97 us -> 1.04 us  [pick(): pl.pallas_call(pick_kernel, out_shape=jax.ShapeDtypeStruct((rows, LATENT)...]
where the time goes in v9:
time: 78.7 us; the launch traced here: 78.2 us
  Pallas kernels  59.4 us (75%)
  starting transfers between devices  12.4 us (16%)
  waiting for transfers between devices  3.41 us (4%)
  local copies, waits for them, and re-layouts  2.33 us (3%)
    pallas_call x1, Pallas kernels, attention(): pl.pallas_call(functools.partial(attn_kernel, owned, head_parts, ahead),...  38.9 us
    pallas_call x1, Pallas kernels, query_gradients(): pl.pallas_call(query_kernel, grid=(steps,), in_specs=[pl.BlockSpec(keys_e...  10.8 us
    pallas_call x1, Pallas kernels, own_scores(): pl.pallas_call(own_kernel, grid=(steps // group,), in_specs=[pl.BlockSpec...  7.69 us
    all_to_all x1, starting transfers between devices, local(): lax.all_to_all(outgoing.reshape(leafs, CAP * BLK, LATENT), 'leaf', split_...  7.36 us
    all_to_all x1, waiting for transfers between devices, local(): lax.all_to_all(outgoing.reshape(leafs, CAP * BLK, LATENT), 'leaf', split_...  3.41 us
    all_to_all x1, starting transfers between devices, local(): lax.all_to_all(sent.reshape(leafs * head_parts, CAP * part_rows, LATENT),...  3.19 us
    unnamed x10, local copies, waits for them, and re-layouts  2.33 us
    ppermute x1, starting transfers between devices, local(): theirs.append(lax.ppermute(part, 'head', route))  1.83 us
  transfers between devices with their start and end apart: 3, of which 1 were waited for; matrix products, arithmetic and copies ran while one was open for 0% of the time, Pallas kernels for 24%

profile of v9, /device:TPU:0, one launch (start us, length us, event | category | flops | bytes accessed | tf_op | source)
XLA Modules:
  0.0 78.2 jit_solution(16059312529706153365)
XLA Ops:
  0.6 0.0 copy-start.1
  0.6 0.9 %copy-done.1 = bf16[16,8,576]{2,1,0:T(8,128)(2,1)S(1)} copy-done((bf16[16,8,576]{2,1,0:T(8,128)(2,1)S(1)}, bf16[16,8,576]{2,1,0:T(8,128)(2,1)}, u32[]{:S(2)}) %copy-start.1) | copy-done | bytes 147480
  1.5 0.0 copy-start.2
  1.5 0.7 copy-done.2
  2.2 1.0 %pick_blocks.1 = bf16[256,576]{1,0:T(8,128)(2,1)} custom-call(s32[16,32]{1,0:T(8,128)S(1)} %copy-done.2, bf16[128,576]{1,0:T(8,128)(2,1)S(1)} %bitcast.6), custom_call_target="tpu_custom_call" | custom-call | tf_op jit(solution)/shard_map/pick_blocks/pallas_call | solution.py:90
  3.3 7.4 %all-to-all-start = ((bf16[16,16,576]{2,1,0:T(8,128)(2,1)}), bf16[16,16,576]{2,1,0:T(8,128)(2,1)S(1)}, u32[]{:S(2)}, u32[]{:S(2)}) async-start(bf16[16,16,576]{2,1,0:T(8,128)(2,1)} %bitcast.1), calls=%async_computation | async-start | bytes 655360 | tf_op jit(solution)/shard_map/all_to_all | solution.py:531
  10.6 7.7 %own_scores.1 = (f32[8,192,512]{2,1,0:T(8,128)}, bf16[8,192,512]{2,1,0:T(8,128)(2,1)}) custom-call(bf16[192,576]{1,0:T(8,128)(2,1)} %own.3, bf16[192,36864]{1,0:T(8,128)(2,1)} %q.3, bf16[192,32768]{1,0:T(8,128)(2,1)} %do.3), custom_call_target="tpu_custom_call" | custom-call | flops 1711276032 | bytes 13631488 | tf_op jit(solution)/shard_map/own_scores/pallas_call | solution.py:192
  18.3 3.4 %all-to-all-done = bf16[16,16,576]{2,1,0:T(8,128)(2,1)S(1)} async-done(((bf16[16,16,576]{2,1,0:T(8,128)(2,1)}), bf16[16,16,576]{2,1,0:T(8,128)(2,1)S(1)}, u32[]{:S(2)}, u32[]{:S(2)}) %all-to-all-start) | async-done | bytes 294944 | tf_op jit(solution)/shard_map/all_to_all | solution.py:531
  21.8 0.0 copy-start.4
  21.8 0.7 copy-done.4
  22.5 38.9 %score_gradients.1 = (bf16[192,36864]{1,0:T(8,128)(2,1)}, bf16[5,1152,512]{2,1,0:T(8,128)(2,1)}, bf16[448,640]{1,0:T(8,128)(2,1)}, bf16[448,640]{1,0:T(8,128)(2,...) custom-call(s32[16]{0:T(128)} %anc_count.1, s32[16,32]{1,0:T(8,128)} %ancestors.5, ...), custom_call_target="tpu_custom_call" | custom-call | flops 23957864448 | bytes 37748736 | tf_op jit(solution)/shard_map/score_gradients/pallas_call | solution.py:421
  61.4 3.2 %all-to-all-start.1 = ((bf16[32,8,576]{2,1,0:T(8,128)(2,1)}), bf16[32,8,576]{2,1,0:T(8,128)(2,1)S(1)}, u32[]{:S(2)}, u32[]{:S(2)}) async-start(bf16[32,8,576]{2,1,0:T(8,128)(2,1)} %bitcast.7), calls=%async_computation.1 | async-start | bytes 655360 | tf_op jit(solution)/shard_map/all_to_all | solution.py:546
  64.5 1.8 %collective-permute-start = (f32[96,576]{1,0:T(8,128)}, f32[96,576]{1,0:T(8,128)S(1)}, u32[]{:S(2)}, u32[]{:S(2)}) collective-permute-start(f32[96,576]{1,0:T(8,128)} %get-tuple-element.22), channel_id=1, source_target_pairs={{0,1},{1,0},{2,3},{3,2},{4,5},{5,4},{6,7},{7,6},{8,9},{9,8},{10,11... | collective-permute-start | bytes 663560 | tf_op jit(solution)/shard_map/ppermute | solution.py:545
  66.4 0.0 copy-start
  66.4 0.0 copy-start.3
  66.4 10.8 %query_gradients.1 = bf16[192,36864]{1,0:T(8,128)(2,1)} custom-call(bf16[448,640]{1,0:T(8,128)(2,1)} %get-tuple-element.16.keys_e, bf16[448,640]{1,0:T(8,128)(2,1)} %get-tuple-element.17.keys_o, bf16[5,1152,512]{2,1,0:T(8,128)(2,1)} %get-tuple-element.18.ds, bf16[192,36864]{1,0:T(8,128)(2,1)} %get-tuple-element.19.started), custom_call_target="tpu_custom_call", output_to_operand_aliasing={{}: (3, {})} | custom-call | flops 3963617280 | bytes 15728640 | tf_op jit(solution)/shard_map/query_gradients/pallas_call | solution.py:502
  77.1 0.0 collective-permute-done.rest_0_
  77.1 0.0 all-to-all-done.1
  77.2 0.0 copy-done
  77.2 0.0 copy-done.3
  77.2 1.0 %sum_gradients.1 = (f32[96,576]{1,0:T(8,128)}, f32[16,4,576]{2,1,0:T(4,128)}) custom-call(s32[16,32]{1,0:T(8,128)S(1)} %copy-done.3, bf16[256,576]{1,0:T(8,128)(2,1)S(1)} %bitcast.5, f32[96,576]{1,0:T(8,128)S(1)} %copy-done, f32[96,576]{1,0:T(8,128)S(1)} %collective-permute-done.rest_0_), custom_call_target="tpu_custom_call" | custom-call | tf_op jit(solution)/shard_map/sum_gradients/pallas_call | solution.py:114
Async XLA Ops:
  0.6 0.9 %copy-start.1 = (bf16[16,8,576]{2,1,0:T(8,128)(2,1)S(1)}, bf16[16,8,576]{2,1,0:T(8,128)(2,1)}, u32[]{:S(2)}) copy-start(bf16[16,8,576]{2,1,0:T(8,128)(2,1)} %param.9) | copy-start | bytes 442372
  1.5 0.7 copy-start.2
  3.3 18.5 %all-to-all-start = ((bf16[16,16,576]{2,1,0:T(8,128)(2,1)}), bf16[16,16,576]{2,1,0:T(8,128)(2,1)S(1)}, u32[]{:S(2)}, u32[]{:S(2)}) async-start(bf16[16,16,576]{2,1,0:T(8,128)(2,1)} %bitcast.1), calls=%async_computation | async-start | bytes 655360 | tf_op jit(solution)/shard_map/all_to_all | solution.py:531
  21.8 0.7 copy-start.4
  61.4 15.8 %all-to-all-start.1 = ((bf16[32,8,576]{2,1,0:T(8,128)(2,1)}), bf16[32,8,576]{2,1,0:T(8,128)(2,1)S(1)}, u32[]{:S(2)}, u32[]{:S(2)}) async-start(bf16[32,8,576]{2,1,0:T(8,128)(2,1)} %bitcast.7), calls=%async_computation.1 | async-start | bytes 655360 | tf_op jit(solution)/shard_map/all_to_all | solution.py:546
  64.5 12.6 %collective-permute-start = (f32[96,576]{1,0:T(8,128)}, f32[96,576]{1,0:T(8,128)S(1)}, u32[]{:S(2)}, u32[]{:S(2)}) collective-permute-start(f32[96,576]{1,0:T(8,128)} %get-tuple-element.22), channel_id=1, source_target_pairs={{0,1},{1,0},{2,3},{3,2},{4,5},{5,4},{6,7},{7,6},{8,9},{9,8},{10,11... | collective-permute-start | bytes 663560 | tf_op jit(solution)/shard_map/ppermute | solution.py:545
  66.4 10.8 %copy-start = (f32[96,576]{1,0:T(8,128)S(1)}, f32[96,576]{1,0:T(8,128)}, u32[]{:S(2)}) copy-start(f32[96,576]{1,0:T(8,128)} %get-tuple-element.21.mine) | copy-start | bytes 663556
  66.4 10.8 %copy-start.3 = (s32[16,32]{1,0:T(8,128)S(1)}, s32[16,32]{1,0:T(8,128)}, u32[]{:S(2)}) copy-start(s32[16,32]{1,0:T(8,128)} %ancestors.5) | copy-start | bytes 6148

commit v10 on v9

--- a/solution.py
+++ b/solution.py
@@ -90,7 +90,6 @@
     return pl.pallas_call(
         pick_kernel,
         out_shape=jax.ShapeDtypeStruct((rows, LATENT), trunk.dtype),
-        compiler_params=pltpu.CompilerParams(vmem_limit_bytes=8 * MIB),
         name="pick_blocks",
     )(ancestors, trunk)
 
@@ -395,7 +394,7 @@
 
 
 def steps_ahead(steps):
-    return steps * 3 // 8
+    return steps // 2
 
 
 def attention(
@@ -461,7 +460,7 @@
             pltpu.VMEM((rows, WIDTH), f32),
             pltpu.VMEM((rows, RANK), f32),
         ],
-        compiler_params=pltpu.CompilerParams(vmem_limit_bytes=60 * MIB),
+        compiler_params=pltpu.CompilerParams(vmem_limit_bytes=52 * MIB),
         cost_estimate=pl.CostEstimate(
             flops=2 * tok * heads * rows * (2 * LATENT + 2 * RANK),
             bytes_accessed=2 * tok * heads * (LATENT + RANK + rows),

time: 78.7 us -> 78.1 us (level)
  local copies, waits for them, and re-layouts: 2.33 us -> 0.83 us
    pallas_call x1, Pallas kernels: 10.8 us -> 8.88 us  [query_gradients(): pl.pallas_call(query_kernel, grid=(steps,), in_specs=[pl.BlockSpec(keys_e...]
    unnamed x10 -> x8, local copies, waits for them, and re-layouts: 2.33 us -> 0.83 us
    pallas_call x1, Pallas kernels: 38.9 us -> 39.8 us  [attention(): pl.pallas_call(functools.partial(attn_kernel, owned, head_parts, ahead),...]
    pallas_call x1, Pallas kernels: 1.04 us -> 1.97 us  [pick(): pl.pallas_call(pick_kernel, out_shape=jax.ShapeDtypeStruct((rows, LATENT)...]
  transfers between devices with their start and end apart: 3 -> 3, of which waited for: 1 -> 3; matrix products, arithmetic and copies ran while one was open for 0% -> 0% of each run, Pallas kernels for 24% -> 22%
where the time goes in v10:
time: 78.1 us; the launch traced here: 77.6 us
  Pallas kernels  59.9 us (77%)
  starting transfers between devices  12.4 us (16%)
  waiting for transfers between devices  3.86 us (5%)
  local copies, waits for them, and re-layouts  0.83 us (1%)
    pallas_call x1, Pallas kernels, attention(): pl.pallas_call(functools.partial(attn_kernel, owned, head_parts, ahead),...  39.8 us
    pallas_call x1, Pallas kernels, query_gradients(): pl.pallas_call(query_kernel, grid=(steps,), in_specs=[pl.BlockSpec(keys_e...  8.88 us
    pallas_call x1, Pallas kernels, own_scores(): pl.pallas_call(own_kernel, grid=(steps // group,), in_specs=[pl.BlockSpec...  8.2 us
    all_to_all x1, starting transfers between devices, local(): lax.all_to_all(outgoing.reshape(leafs, CAP * BLK, LATENT), 'leaf', split_...  7.36 us
    all_to_all x1, starting transfers between devices, local(): lax.all_to_all(sent.reshape(leafs * head_parts, CAP * part_rows, LATENT),...  3.18 us
    all_to_all x1, waiting for transfers between devices, local(): lax.all_to_all(outgoing.reshape(leafs, CAP * BLK, LATENT), 'leaf', split_...  2.86 us
    pallas_call x1, Pallas kernels, pick(): pl.pallas_call(pick_kernel, out_shape=jax.ShapeDtypeStruct((rows, LATENT)...  1.97 us
    ppermute x1, starting transfers between devices, local(): theirs.append(lax.ppermute(part, 'head', route))  1.83 us
  transfers between devices with their start and end apart: 3, of which 3 were waited for; matrix products, arithmetic and copies ran while one was open for 0% of the time, Pallas kernels for 22%

profile of v10, /device:TPU:0, one launch (start us, length us, event | category | flops | bytes accessed | tf_op | source)
XLA Modules:
  0.0 77.6 jit_solution(13881439453235029064)
XLA Ops:
  0.6 2.0 %pick_blocks.1 = bf16[256,576]{1,0:T(8,128)(2,1)} custom-call(s32[16,32]{1,0:T(8,128)} %ancestors.5, bf16[128,576]{1,0:T(8,128)(2,1)} %bitcast.8), custom_call_target="tpu_custom_call" | custom-call | tf_op jit(solution)/shard_map/pick_blocks/pallas_call | solution.py:90
  2.6 7.4 %all-to-all-start = ((bf16[16,16,576]{2,1,0:T(8,128)(2,1)}), bf16[16,16,576]{2,1,0:T(8,128)(2,1)S(1)}, u32[]{:S(2)}, u32[]{:S(2)}) async-start(bf16[16,16,576]{2,1,0:T(8,128)(2,1)} %bitcast.7), calls=%async_computation | async-start | bytes 655360 | tf_op jit(solution)/shard_map/all_to_all | solution.py:530
  10.0 0.0 copy-start.1
  10.0 0.0 copy-start.2
  10.0 0.0 copy-start.3
  10.0 8.2 %own_scores.1 = (f32[8,192,512]{2,1,0:T(8,128)}, bf16[8,192,512]{2,1,0:T(8,128)(2,1)}) custom-call(bf16[192,576]{1,0:T(8,128)(2,1)} %own.3, bf16[192,36864]{1,0:T(8,128)(2,1)} %q.3, bf16[192,32768]{1,0:T(8,128)(2,1)} %do.3), custom_call_target="tpu_custom_call" | custom-call | flops 1711276032 | bytes 13631488 | tf_op jit(solution)/shard_map/own_scores/pallas_call | solution.py:191
  18.2 2.9 %all-to-all-done = bf16[16,16,576]{2,1,0:T(8,128)(2,1)S(1)} async-done(((bf16[16,16,576]{2,1,0:T(8,128)(2,1)}), bf16[16,16,576]{2,1,0:T(8,128)(2,1)S(1)}, u32[]{:S(2)}, u32[]{:S(2)}) %all-to-all-start) | async-done | bytes 294944 | tf_op jit(solution)/shard_map/all_to_all | solution.py:530
  21.1 0.0 copy-done.1
  21.1 0.0 copy-done.2
  21.1 0.0 copy-done.3
  21.1 39.8 %score_gradients.1 = (bf16[192,36864]{1,0:T(8,128)(2,1)}, bf16[4,1152,512]{2,1,0:T(8,128)(2,1)}, bf16[448,640]{1,0:T(8,128)(2,1)S(1)}, bf16[448,640]{1,0:T(8,128...) custom-call(s32[16]{0:T(128)S(1)} %copy-done.3, s32[16,32]{1,0:T(8,128)S(1)} %copy-done.2, ...), custom_call_target="tpu_custom_call" | custom-call | flops 23957864448 | bytes 37748736 | tf_op jit(solution)/shard_map/score_gradients/pallas_call | solution.py:420
  60.9 0.0 copy-start
  60.9 0.8 %copy-done = bf16[448,640]{1,0:T(8,128)(2,1)} copy-done((bf16[448,640]{1,0:T(8,128)(2,1)}, bf16[448,640]{1,0:T(8,128)(2,1)S(1)}, u32[]{:S(2)}) %copy-start) | copy-done | bytes 573464
  61.7 3.2 %all-to-all-start.1 = ((bf16[32,8,576]{2,1,0:T(8,128)(2,1)}), bf16[32,8,576]{2,1,0:T(8,128)(2,1)S(1)}, u32[]{:S(2)}, u32[]{:S(2)}) async-start(bf16[32,8,576]{2,1,0:T(8,128)(2,1)} %bitcast.3), calls=%async_computation.1 | async-start | bytes 655360 | tf_op jit(solution)/shard_map/all_to_all | solution.py:545
  64.9 1.8 %collective-permute-start = (f32[96,576]{1,0:T(8,128)S(1)}, f32[96,576]{1,0:T(8,128)S(1)}, u32[]{:S(2)}, u32[]{:S(2)}) collective-permute-start(f32[96,576]{1,0:T(8,128)S(1)} %get-tuple-element.22), channel_id=1, source_target_pairs={{0,1},{1,0},{2,3},{3,2},{4,5},{5,4},{6,7},{7,6},{8,9},{9,8},{10,11... | collective-permute-start | bytes 663560 | tf_op jit(solution)/shard_map/ppermute | solution.py:544
  66.7 8.9 %query_gradients.1 = bf16[192,36864]{1,0:T(8,128)(2,1)} custom-call(bf16[448,640]{1,0:T(8,128)(2,1)} %copy-done, bf16[448,640]{1,0:T(8,128)(2,1)} %get-tuple-element.17.keys_o, bf16[4,1152,512]{2,1,0:T(8,128)(2,1)} %get-tuple-element.18.ds, bf16[192,36864]{1,0:T(8,128)(2,1)} %get-tuple-element.19.started), custom_call_target="tpu_custom_call", output_to_operand_aliasing={{}: (3, {})} | custom-call | flops 3170893824 | bytes 12582912 | tf_op jit(solution)/shard_map/query_gradients/pallas_call | solution.py:501
  75.6 0.7 collective-permute-done.rest_0_
  76.3 0.3 all-to-all-done.1
  76.6 1.0 %sum_gradients.1 = (f32[96,576]{1,0:T(8,128)}, f32[16,4,576]{2,1,0:T(4,128)}) custom-call(s32[16,32]{1,0:T(8,128)S(1)} %copy-done.2, bf16[256,576]{1,0:T(8,128)(2,1)S(1)} %bitcast.5, f32[96,576]{1,0:T(8,128)S(1)} %get-tuple-element.21.mine, f32[96,576]{1,0:T(8,128)S(1)} %collective-permute-done.rest_0_), custom_call_target="tpu_custom_call" | custom-call | tf_op jit(solution)/shard_map/sum_gradients/pallas_call | solution.py:113
Async XLA Ops:
  2.6 18.5 %all-to-all-start = ((bf16[16,16,576]{2,1,0:T(8,128)(2,1)}), bf16[16,16,576]{2,1,0:T(8,128)(2,1)S(1)}, u32[]{:S(2)}, u32[]{:S(2)}) async-start(bf16[16,16,576]{2,1,0:T(8,128)(2,1)} %bitcast.7), calls=%async_computation | async-start | bytes 655360 | tf_op jit(solution)/shard_map/all_to_all | solution.py:530
  10.0 11.1 %copy-start.1 = (bf16[192,576]{1,0:T(8,128)(2,1)S(1)}, bf16[192,576]{1,0:T(8,128)(2,1)}, u32[]{:S(2)}) copy-start(bf16[192,576]{1,0:T(8,128)(2,1)} %own.3) | copy-start | bytes 663556
  10.0 11.1 %copy-start.2 = (s32[16,32]{1,0:T(8,128)S(1)}, s32[16,32]{1,0:T(8,128)}, u32[]{:S(2)}) copy-start(s32[16,32]{1,0:T(8,128)} %ancestors.5) | copy-start | bytes 6148
  10.0 11.1 %copy-start.3 = (s32[16]{0:T(128)S(1)}, s32[16]{0:T(128)}, u32[]{:S(2)}) copy-start(s32[16]{0:T(128)} %anc_count.1) | copy-start | bytes 196
  60.9 0.8 %copy-start = (bf16[448,640]{1,0:T(8,128)(2,1)}, bf16[448,640]{1,0:T(8,128)(2,1)S(1)}, u32[]{:S(2)}) copy-start(bf16[448,640]{1,0:T(8,128)(2,1)S(1)} %get-tuple-element.16.keys_e) | copy-start | bytes 1720324
  61.7 14.9 %all-to-all-start.1 = ((bf16[32,8,576]{2,1,0:T(8,128)(2,1)}), bf16[32,8,576]{2,1,0:T(8,128)(2,1)S(1)}, u32[]{:S(2)}, u32[]{:S(2)}) async-start(bf16[32,8,576]{2,1,0:T(8,128)(2,1)} %bitcast.3), calls=%async_computation.1 | async-start | bytes 655360 | tf_op jit(solution)/shard_map/all_to_all | solution.py:545
  64.9 11.4 %collective-permute-start = (f32[96,576]{1,0:T(8,128)S(1)}, f32[96,576]{1,0:T(8,128)S(1)}, u32[]{:S(2)}, u32[]{:S(2)}) collective-permute-start(f32[96,576]{1,0:T(8,128)S(1)} %get-tuple-element.22), channel_id=1, source_target_pairs={{0,1},{1,0},{2,3},{3,2},{4,5},{5,4},{6,7},{7,6},{8,9},{9,8},{10,11... | collective-permute-start | bytes 663560 | tf_op jit(solution)/shard_map/ppermute | solution.py:544

commit v11 on v10

--- a/solution.py
+++ b/solution.py
@@ -219,11 +219,11 @@
 
 def attn_kernel(
     owned, head_parts, ahead, anc_count, ancestors, incoming, own, s_own, dp_own, q, do,
-    dq, ds, keys_out_e, keys_out_o, sent, *rest
+    dq, ds, keys_out, sent, *rest
 ):
     own_parts = rest[:head_parts]
     scratch = rest[head_parts:]
-    k_e, k_o, sems, far_bias, causal, q_st, s, dp, p_low, tops, acc_k, acc_v = scratch
+    keys, sem, far_bias, causal, q_st, s, dp, p_low, tops, acc_k, acc_v = scratch
     tok = q.shape[0]
     far_rows, rows = ANC * BLK, ANC * BLK + tok
     sub = token_part(tok)
@@ -231,10 +231,7 @@
     stack = 2 * PAIRS * sub
     least = LEAST_LIVE * BLK
     step = pl.program_id(0)
-    key_copies = [
-        pltpu.make_async_copy(k_e, keys_out_e, sems.at[0]),
-        pltpu.make_async_copy(k_o, keys_out_o, sems.at[1]),
-    ]
+    keys_copy = pltpu.make_async_copy(keys, keys_out, sem)
 
     @pl.when(step == 0)
     def _():
@@ -243,10 +240,8 @@
         far = mm(sel, incoming[...], NN)
         joined = jnp.concatenate([far, own[...].astype(jnp.float32)], axis=0)
         padded = jnp.concatenate([joined, jnp.zeros((rows, HALF), jnp.float32)], axis=1)
-        k_e[...] = padded.astype(jnp.bfloat16)
-        k_o[...] = pltpu.roll(padded, HALF, axis=1).astype(jnp.bfloat16)
-        for copy in key_copies:
-            copy.start()
+        keys[...] = padded.astype(jnp.bfloat16)
+        keys_copy.start()
         live = anc_count[lax.axis_index("leaf")]
         slot = div(lax.broadcasted_iota(jnp.int32, far_bias.shape, 0) + least, BLK)
         far_bias[...] = jnp.where(slot < live, 0.0, MASKED)
@@ -286,7 +281,7 @@
 
     def score(j, at):
         n, cols = seen(j), pl.ds(j * stack + at, stack // 2)
-        out = mm(k_e[:far_rows if given(j) else n, :], q_st[cols, :].T, NN)
+        out = mm(keys[:far_rows if given(j) else n, :], q_st[cols, :].T, NN)
         near = [(0, out[:least]), (least, out[least:far_rows] + far_bias[...])]
         top = None
         if given(j):
@@ -303,7 +298,7 @@
 
     def prob(j, at):
         n, cols = far_rows if given(j) else seen(j), pl.ds(j * stack + at, stack // 2)
-        dp[:n, cols] = mm(k_e[:n, :RANK], grads(j, at // sub, PAIRS).T, NN)
+        dp[:n, cols] = mm(keys[:n, :RANK], grads(j, at // sub, PAIRS).T, NN)
 
     state = {}
 
@@ -370,7 +365,7 @@
 
     @pl.when(step < ahead)
     def _():
-        put_queries(dq, ds, k_e, k_o)
+        put_queries(dq, ds, keys)
 
     @pl.when(step == pl.num_programs(0) - 1)
     def _():
@@ -389,8 +384,7 @@
             part = lax.rem(lax.axis_index("head") + hop, head_parts)
             at = pl.multiple_of(far_rows + part * own_rows, 8)
             out[...] = acc_k[pl.ds(at, own_rows), :LATENT]
-        for copy in key_copies:
-            copy.wait()
+        keys_copy.wait()
 
 
 def steps_ahead(steps):
@@ -435,21 +429,18 @@
                 (tok, 2 * PAIRS * LATENT), lambda i: (0, jnp.minimum(i, max(ahead - 1, 0)))
             ),
             pl.BlockSpec((1, ds_rows, stack), lambda i: (jnp.maximum(i - ahead, 0), 0, 0)),
-            pl.BlockSpec(memory_space=pl.ANY),
-            pl.BlockSpec(memory_space=pl.ANY),
+            pl.BlockSpec(memory_space=pltpu.HBM),
             pl.BlockSpec(incoming.shape, whole),
         ] + [pl.BlockSpec(own_part, whole)] * head_parts,
         out_shape=[
             jax.ShapeDtypeStruct(queries.shape, bf16),
             jax.ShapeDtypeStruct((steps - ahead, ds_rows, stack), bf16),
             jax.ShapeDtypeStruct((rows, WIDTH), bf16),
-            jax.ShapeDtypeStruct((rows, WIDTH), bf16),
             jax.ShapeDtypeStruct(incoming.shape, bf16),
         ] + [jax.ShapeDtypeStruct(own_part, f32)] * head_parts,
         scratch_shapes=[
             pltpu.VMEM((rows, WIDTH), bf16),
-            pltpu.VMEM((rows, WIDTH), bf16),
-            pltpu.SemaphoreType.DMA((2,)),
+            pltpu.SemaphoreType.DMA(()),
             pltpu.VMEM((far_rows - LEAST_LIVE * BLK, stack // 2), f32),
             pltpu.VMEM((token_part(tok), stack // 2), f32),
             pltpu.VMEM((toks, WIDTH), bf16),
@@ -470,54 +461,53 @@
     )(anc_count, ancestors, incoming, own, s_own, dp_own, queries, d_out)
 
 
-def put_queries(dq, ds, keys_e, keys_o):
+def put_queries(dq, ds, keys):
     tok = dq.shape[0]
     sub = token_part(tok)
     stack = PAIRS * sub
     low = LATENT - HALF
-    seen, starts = seen_rows(keys_e.shape[0], tok)
+    seen, starts = seen_rows(keys.shape[0], tok)
     for j, n in enumerate(seen):
-        block = pl.ds(starts[j], n)
-        even = mm(ds[0, block, :stack], keys_e[:n, :], TN) * SCALE
-        odd = mm(ds[0, block, stack:], keys_o[:n, :], TN) * SCALE
+        both = mm(ds[0, pl.ds(starts[j], n), :], keys[:n, :], TN) * SCALE
+        both = both.astype(dq.dtype)
+        even, odd = both[:stack], pltpu.roll(both[stack:], HALF, axis=1)
         for i in range(PAIRS):
             at = i * 2 * LATENT
             part = slice(i * sub, (i + 1) * sub)
             toks = pl.ds(j * sub, sub)
-            dq[toks, at:at + low] = even[part, :low].astype(dq.dtype)
+            dq[toks, at:at + low] = even[part, :low]
             joint = even[part, low:] + odd[part, :2 * HALF]
-            dq[toks, at + low:at + low + 2 * HALF] = joint.astype(dq.dtype)
-            dq[toks, at + low + 2 * HALF:at + 2 * LATENT] = odd[part, 2 * HALF:].astype(dq.dtype)
-
-
-def query_kernel(keys_e, keys_o, ds, started, dq):
-    put_queries(dq, ds, keys_e, keys_o)
-
-
-def query_gradients(keys_e, keys_o, ds, started):
+            dq[toks, at + low:at + low + 2 * HALF] = joint
+            dq[toks, at + low + 2 * HALF:at + 2 * LATENT] = odd[part, 2 * HALF:]
+
+
+def query_kernel(keys, ds, started, dq):
+    put_queries(dq, ds, keys)
+
+
+def query_gradients(keys, ds, started):
     tok = started.shape[0]
-    steps, rows = ds.shape[0], keys_e.shape[0]
+    steps, rows = ds.shape[0], keys.shape[0]
     ahead = started.shape[1] // (2 * PAIRS * LATENT) - steps
     return pl.pallas_call(
         query_kernel,
         grid=(steps,),
         in_specs=[
-            pl.BlockSpec(keys_e.shape, lambda i: (0, 0)),
-            pl.BlockSpec(keys_o.shape, lambda i: (0, 0)),
+            pl.BlockSpec(keys.shape, lambda i: (0, 0)),
             pl.BlockSpec((1,) + ds.shape[1:], lambda i: (i, 0, 0)),
             pl.BlockSpec(memory_space=pl.ANY),
         ],
         out_specs=pl.BlockSpec((tok, 2 * PAIRS * LATENT), lambda i: (0, i + ahead)),
         out_shape=jax.ShapeDtypeStruct(started.shape, started.dtype),
-        input_output_aliases={3: 0},
-        compiler_params=pltpu.CompilerParams(vmem_limit_bytes=60 * MIB),
+        input_output_aliases={2: 0},
+        compiler_params=pltpu.CompilerParams(vmem_limit_bytes=239 * MIB // 4),
         cost_estimate=pl.CostEstimate(
             flops=4 * tok * steps * PAIRS * rows * LATENT,
             bytes_accessed=4 * tok * steps * PAIRS * (LATENT + rows),
             transcendentals=0,
         ),
         name="query_gradients",
-    )(keys_e, keys_o, ds, started)
+    )(keys, ds, started)
 
 
 def local(queries, d_out, branch_latent, trunk_latent, ancestors, anc_count):
@@ -533,7 +523,7 @@
 
     s_own, dp_own = own_scores(branch_latent, queries, d_out)
 
-    started, ds, keys_e, keys_o, sent, mine, *others = attention(
+    started, ds, keys, sent, mine, *others = attention(
         owned, head_parts, anc_count, ancestors, incoming, branch_latent, s_own, dp_own,
         queries, d_out,
     )
@@ -546,7 +536,7 @@
         sent.reshape(leafs * head_parts, CAP * part_rows, LATENT),
         ("leaf", "head"), split_axis=0, concat_axis=0, tiled=True,
     ).reshape(leafs * CAP * BLK, LATENT)
-    d_queries = query_gradients(keys_e, keys_o, ds, started)
+    d_queries = query_gradients(keys, ds, started)
     d_branch, d_trunk = finish(ancestors, got, mine, theirs, owned, part_rows)
     return d_queries, d_branch, d_trunk
 

time: 78.1 us -> 78.3 us (level)
  no operation moved by 1% of the time
where the time goes in v11:
time: 78.3 us; the launch traced here: 77.9 us
  Pallas kernels  60.2 us (77%)
  starting transfers between devices  12.4 us (16%)
  waiting for transfers between devices  3.8 us (5%)
  local copies, waits for them, and re-layouts  0.83 us (1%)
    pallas_call x1, Pallas kernels, attention(): pl.pallas_call(functools.partial(attn_kernel, owned, head_parts, ahead),...  40.1 us
    pallas_call x1, Pallas kernels, query_gradients(): pl.pallas_call(query_kernel, grid=(steps,), in_specs=[pl.BlockSpec(keys.s...  8.95 us
    pallas_call x1, Pallas kernels, own_scores(): pl.pallas_call(own_kernel, grid=(steps // group,), in_specs=[pl.BlockSpec...  8.2 us
    all_to_all x1, starting transfers between devices, local(): lax.all_to_all(outgoing.reshape(leafs, CAP * BLK, LATENT), 'leaf', split_...  7.36 us
    all_to_all x1, starting transfers between devices, local(): lax.all_to_all(sent.reshape(leafs * head_parts, CAP * part_rows, LATENT),...  3.18 us
    all_to_all x1, waiting for transfers between devices, local(): lax.all_to_all(outgoing.reshape(leafs, CAP * BLK, LATENT), 'leaf', split_...  2.86 us
    pallas_call x1, Pallas kernels, pick(): pl.pallas_call(pick_kernel, out_shape=jax.ShapeDtypeStruct((rows, LATENT)...  1.97 us
    ppermute x1, starting transfers between devices, local(): theirs.append(lax.ppermute(part, 'head', route))  1.83 us
  transfers between devices with their start and end apart: 3, of which 3 were waited for; matrix products, arithmetic and copies ran while one was open for 0% of the time, Pallas kernels for 22%

profile of v11, /device:TPU:0, one launch (start us, length us, event | category | flops | bytes accessed | tf_op | source)
XLA Modules:
  0.0 77.9 jit_solution(11192445609380426297)
XLA Ops:
  0.6 2.0 %pick_blocks.1 = bf16[256,576]{1,0:T(8,128)(2,1)} custom-call(s32[16,32]{1,0:T(8,128)} %ancestors.5, bf16[128,576]{1,0:T(8,128)(2,1)} %bitcast.8), custom_call_target="tpu_custom_call" | custom-call | tf_op jit(solution)/shard_map/pick_blocks/pallas_call | solution.py:90
  2.6 7.4 %all-to-all-start = ((bf16[16,16,576]{2,1,0:T(8,128)(2,1)}), bf16[16,16,576]{2,1,0:T(8,128)(2,1)S(1)}, u32[]{:S(2)}, u32[]{:S(2)}) async-start(bf16[16,16,576]{2,1,0:T(8,128)(2,1)} %bitcast.7), calls=%async_computation | async-start | bytes 655360 | tf_op jit(solution)/shard_map/all_to_all | solution.py:520
  10.0 0.0 copy-start.1
  10.0 0.0 copy-start.2
  10.0 0.0 copy-start.3
  10.0 8.2 %own_scores.1 = (f32[8,192,512]{2,1,0:T(8,128)}, bf16[8,192,512]{2,1,0:T(8,128)(2,1)}) custom-call(bf16[192,576]{1,0:T(8,128)(2,1)} %own.3, bf16[192,36864]{1,0:T(8,128)(2,1)} %q.3, bf16[192,32768]{1,0:T(8,128)(2,1)} %do.3), custom_call_target="tpu_custom_call" | custom-call | flops 1711276032 | bytes 13631488 | tf_op jit(solution)/shard_map/own_scores/pallas_call | solution.py:191
  18.2 2.9 %all-to-all-done = bf16[16,16,576]{2,1,0:T(8,128)(2,1)S(1)} async-done(((bf16[16,16,576]{2,1,0:T(8,128)(2,1)}), bf16[16,16,576]{2,1,0:T(8,128)(2,1)S(1)}, u32[]{:S(2)}, u32[]{:S(2)}) %all-to-all-start) | async-done | bytes 294944 | tf_op jit(solution)/shard_map/all_to_all | solution.py:520
  21.1 0.0 copy-done.1
  21.1 0.0 copy-done.2
  21.1 0.0 copy-done.3
  21.1 40.1 %score_gradients.1 = (bf16[192,36864]{1,0:T(8,128)(2,1)}, bf16[4,1152,512]{2,1,0:T(8,128)(2,1)}, bf16[448,640]{1,0:T(8,128)(2,1)S(1)}, bf16[256,576]{1,0:T(8,128...) custom-call(s32[16]{0:T(128)S(1)} %copy-done.3, s32[16,32]{1,0:T(8,128)S(1)} %copy-done.2, ...), custom_call_target="tpu_custom_call" | custom-call | flops 23957864448 | bytes 37748736 | tf_op jit(solution)/shard_map/score_gradients/pallas_call | solution.py:414
  61.1 0.0 copy-start
  61.2 0.8 %copy-done = bf16[448,640]{1,0:T(8,128)(2,1)} copy-done((bf16[448,640]{1,0:T(8,128)(2,1)}, bf16[448,640]{1,0:T(8,128)(2,1)S(1)}, u32[]{:S(2)}) %copy-start) | copy-done | bytes 573464
  62.0 3.2 %all-to-all-start.1 = ((bf16[32,8,576]{2,1,0:T(8,128)(2,1)}), bf16[32,8,576]{2,1,0:T(8,128)(2,1)S(1)}, u32[]{:S(2)}, u32[]{:S(2)}) async-start(bf16[32,8,576]{2,1,0:T(8,128)(2,1)} %bitcast.3), calls=%async_computation.1 | async-start | bytes 655360 | tf_op jit(solution)/shard_map/all_to_all | solution.py:535
  65.1 1.8 %collective-permute-start = (f32[96,576]{1,0:T(8,128)S(1)}, f32[96,576]{1,0:T(8,128)S(1)}, u32[]{:S(2)}, u32[]{:S(2)}) collective-permute-start(f32[96,576]{1,0:T(8,128)S(1)} %get-tuple-element.20), channel_id=1, source_target_pairs={{0,1},{1,0},{2,3},{3,2},{4,5},{5,4},{6,7},{7,6},{8,9},{9,8},{10,11... | collective-permute-start | bytes 663560 | tf_op jit(solution)/shard_map/ppermute | solution.py:534
  67.0 8.9 %query_gradients.1 = bf16[192,36864]{1,0:T(8,128)(2,1)} custom-call(bf16[448,640]{1,0:T(8,128)(2,1)} %copy-done, bf16[4,1152,512]{2,1,0:T(8,128)(2,1)} %get-tuple-element.16.ds, bf16[192,36864]{1,0:T(8,128)(2,1)} %get-tuple-element.17.started), custom_call_target="tpu_custom_call", output_to_operand_aliasing={{}: (2, {})} | custom-call | flops 3170893824 | bytes 12582912 | tf_op jit(solution)/shard_map/query_gradients/pallas_call | solution.py:492
  75.9 0.6 collective-permute-done.rest_0_
  76.6 0.3 all-to-all-done.1
  76.9 1.0 %sum_gradients.1 = (f32[96,576]{1,0:T(8,128)}, f32[16,4,576]{2,1,0:T(4,128)}) custom-call(s32[16,32]{1,0:T(8,128)S(1)} %copy-done.2, bf16[256,576]{1,0:T(8,128)(2,1)S(1)} %bitcast.5, f32[96,576]{1,0:T(8,128)S(1)} %get-tuple-element.19.mine, f32[96,576]{1,0:T(8,128)S(1)} %collective-permute-done.rest_0_), custom_call_target="tpu_custom_call" | custom-call | tf_op jit(solution)/shard_map/sum_gradients/pallas_call | solution.py:113
Async XLA Ops:
  2.6 18.5 %all-to-all-start = ((bf16[16,16,576]{2,1,0:T(8,128)(2,1)}), bf16[16,16,576]{2,1,0:T(8,128)(2,1)S(1)}, u32[]{:S(2)}, u32[]{:S(2)}) async-start(bf16[16,16,576]{2,1,0:T(8,128)(2,1)} %bitcast.7), calls=%async_computation | async-start | bytes 655360 | tf_op jit(solution)/shard_map/all_to_all | solution.py:520
  10.0 11.1 %copy-start.1 = (bf16[192,576]{1,0:T(8,128)(2,1)S(1)}, bf16[192,576]{1,0:T(8,128)(2,1)}, u32[]{:S(2)}) copy-start(bf16[192,576]{1,0:T(8,128)(2,1)} %own.3) | copy-start | bytes 663556
  10.0 11.1 %copy-start.2 = (s32[16,32]{1,0:T(8,128)S(1)}, s32[16,32]{1,0:T(8,128)}, u32[]{:S(2)}) copy-start(s32[16,32]{1,0:T(8,128)} %ancestors.5) | copy-start | bytes 6148
  10.0 11.1 %copy-start.3 = (s32[16]{0:T(128)S(1)}, s32[16]{0:T(128)}, u32[]{:S(2)}) copy-start(s32[16]{0:T(128)} %anc_count.1) | copy-start | bytes 196
  61.1 0.8 %copy-start = (bf16[448,640]{1,0:T(8,128)(2,1)}, bf16[448,640]{1,0:T(8,128)(2,1)S(1)}, u32[]{:S(2)}) copy-start(bf16[448,640]{1,0:T(8,128)(2,1)S(1)} %get-tuple-element.15.keys) | copy-start | bytes 1720324
  62.0 14.9 %all-to-all-start.1 = ((bf16[32,8,576]{2,1,0:T(8,128)(2,1)}), bf16[32,8,576]{2,1,0:T(8,128)(2,1)S(1)}, u32[]{:S(2)}, u32[]{:S(2)}) async-start(bf16[32,8,576]{2,1,0:T(8,128)(2,1)} %bitcast.3), calls=%async_computation.1 | async-start | bytes 655360 | tf_op jit(solution)/shard_map/all_to_all | solution.py:535
  65.1 11.4 %collective-permute-start = (f32[96,576]{1,0:T(8,128)S(1)}, f32[96,576]{1,0:T(8,128)S(1)}, u32[]{:S(2)}, u32[]{:S(2)}) collective-permute-start(f32[96,576]{1,0:T(8,128)S(1)} %get-tuple-element.20), channel_id=1, source_target_pairs={{0,1},{1,0},{2,3},{3,2},{4,5},{5,4},{6,7},{7,6},{8,9},{9,8},{10,11... | collective-permute-start | bytes 663560 | tf_op jit(solution)/shard_map/ppermute | solution.py:534

commit v12 on v11

--- a/solution.py
+++ b/solution.py
@@ -388,7 +388,7 @@
 
 
 def steps_ahead(steps):
-    return steps // 2
+    return steps * 3 // 8
 
 
 def attention(
@@ -500,7 +500,7 @@
         out_specs=pl.BlockSpec((tok, 2 * PAIRS * LATENT), lambda i: (0, i + ahead)),
         out_shape=jax.ShapeDtypeStruct(started.shape, started.dtype),
         input_output_aliases={2: 0},
-        compiler_params=pltpu.CompilerParams(vmem_limit_bytes=239 * MIB // 4),
+        compiler_params=pltpu.CompilerParams(vmem_limit_bytes=32 * MIB),
         cost_estimate=pl.CostEstimate(
             flops=4 * tok * steps * PAIRS * rows * LATENT,
             bytes_accessed=4 * tok * steps * PAIRS * (LATENT + rows),

time: 78.3 us -> 77.2 us (0.986)
  Pallas kernels: 60.2 us -> 58.3 us
  local copies, waits for them, and re-layouts: 0.83 us -> 2.69 us
  waiting for transfers between devices: 3.8 us -> 2.85 us
    unnamed x8, local copies, waits for them, and re-layouts: 0.83 us -> 2.69 us
    pallas_call x1, Pallas kernels: 40.1 us -> 38.6 us  [attention(): pl.pallas_call(functools.partial(attn_kernel, owned, head_parts, ahead),...]
  transfers between devices with their start and end apart: 3 -> 3, of which waited for: 3 -> 1; matrix products, arithmetic and copies ran while one was open for 0% -> 0% of each run, Pallas kernels for 22% -> 22%
where the time goes in v12:
time: 77.2 us; the launch traced here: 76.9 us
  Pallas kernels  58.3 us (76%)
  starting transfers between devices  12.4 us (16%)
  waiting for transfers between devices  2.85 us (4%)
  local copies, waits for them, and re-layouts  2.69 us (3%)
    pallas_call x1, Pallas kernels, attention(): pl.pallas_call(functools.partial(attn_kernel, owned, head_parts, ahead),...  38.6 us
    pallas_call x1, Pallas kernels, query_gradients(): pl.pallas_call(query_kernel, grid=(steps,), in_specs=[pl.BlockSpec(keys.s...  8.45 us
    pallas_call x1, Pallas kernels, own_scores(): pl.pallas_call(own_kernel, grid=(steps // group,), in_specs=[pl.BlockSpec...  8.22 us
    all_to_all x1, starting transfers between devices, local(): lax.all_to_all(outgoing.reshape(leafs, CAP * BLK, LATENT), 'leaf', split_...  7.36 us
    all_to_all x1, starting transfers between devices, local(): lax.all_to_all(sent.reshape(leafs * head_parts, CAP * part_rows, LATENT),...  3.19 us
    all_to_all x1, waiting for transfers between devices, local(): lax.all_to_all(outgoing.reshape(leafs, CAP * BLK, LATENT), 'leaf', split_...  2.85 us
    unnamed x8, local copies, waits for them, and re-layouts  2.69 us
    pallas_call x1, Pallas kernels, pick(): pl.pallas_call(pick_kernel, out_shape=jax.ShapeDtypeStruct((rows, LATENT)...  1.97 us
  transfers between devices with their start and end apart: 3, of which 1 were waited for; matrix products, arithmetic and copies ran while one was open for 0% of the time, Pallas kernels for 22%

profile of v12, /device:TPU:0, one launch (start us, length us, event | category | flops | bytes accessed | tf_op | source)
XLA Modules:
  0.0 76.9 jit_solution(784764008153643464)
XLA Ops:
  0.6 2.0 %pick_blocks.1 = bf16[256,576]{1,0:T(8,128)(2,1)} custom-call(s32[16,32]{1,0:T(8,128)} %ancestors.5, bf16[128,576]{1,0:T(8,128)(2,1)} %bitcast.8), custom_call_target="tpu_custom_call" | custom-call | tf_op jit(solution)/shard_map/pick_blocks/pallas_call | solution.py:90
  2.6 7.4 %all-to-all-start = ((bf16[16,16,576]{2,1,0:T(8,128)(2,1)}), bf16[16,16,576]{2,1,0:T(8,128)(2,1)S(1)}, u32[]{:S(2)}, u32[]{:S(2)}) async-start(bf16[16,16,576]{2,1,0:T(8,128)(2,1)} %bitcast.7), calls=%async_computation | async-start | bytes 655360 | tf_op jit(solution)/shard_map/all_to_all | solution.py:520
  10.0 0.0 copy-start.1
  10.0 0.0 copy-start.2
  10.0 0.0 copy-start.3
  10.0 8.2 %own_scores.1 = (f32[8,192,512]{2,1,0:T(8,128)}, bf16[8,192,512]{2,1,0:T(8,128)(2,1)}) custom-call(bf16[192,576]{1,0:T(8,128)(2,1)} %own.3, bf16[192,36864]{1,0:T(8,128)(2,1)} %q.3, bf16[192,32768]{1,0:T(8,128)(2,1)} %do.3), custom_call_target="tpu_custom_call" | custom-call | flops 1711276032 | bytes 13631488 | tf_op jit(solution)/shard_map/own_scores/pallas_call | solution.py:191
  18.2 2.8 %all-to-all-done = bf16[16,16,576]{2,1,0:T(8,128)(2,1)S(1)} async-done(((bf16[16,16,576]{2,1,0:T(8,128)(2,1)}), bf16[16,16,576]{2,1,0:T(8,128)(2,1)S(1)}, u32[]{:S(2)}, u32[]{:S(2)}) %all-to-all-start) | async-done | bytes 294944 | tf_op jit(solution)/shard_map/all_to_all | solution.py:520
  21.1 0.0 copy-done.1
  21.1 0.0 copy-done.2
  21.1 0.0 copy-done.3
  21.1 38.6 %score_gradients.1 = (bf16[192,36864]{1,0:T(8,128)(2,1)}, bf16[5,1152,512]{2,1,0:T(8,128)(2,1)}, bf16[448,640]{1,0:T(8,128)(2,1)S(1)}, bf16[256,576]{1,0:T(8,128...) custom-call(s32[16]{0:T(128)S(1)} %copy-done.3, s32[16,32]{1,0:T(8,128)S(1)} %copy-done.2, ...), custom_call_target="tpu_custom_call" | custom-call | flops 23957864448 | bytes 37748736 | tf_op jit(solution)/shard_map/score_gradients/pallas_call | solution.py:414
  59.7 3.2 %all-to-all-start.1 = ((bf16[32,8,576]{2,1,0:T(8,128)(2,1)}), bf16[32,8,576]{2,1,0:T(8,128)(2,1)S(1)}, u32[]{:S(2)}, u32[]{:S(2)}) async-start(bf16[32,8,576]{2,1,0:T(8,128)(2,1)} %bitcast.3), calls=%async_computation.1 | async-start | bytes 655360 | tf_op jit(solution)/shard_map/all_to_all | solution.py:535
  62.9 1.8 %collective-permute-start = (f32[96,576]{1,0:T(8,128)S(1)}, f32[96,576]{1,0:T(8,128)S(1)}, u32[]{:S(2)}, u32[]{:S(2)}) collective-permute-start(f32[96,576]{1,0:T(8,128)S(1)} %get-tuple-element.20), channel_id=1, source_target_pairs={{0,1},{1,0},{2,3},{3,2},{4,5},{5,4},{6,7},{7,6},{8,9},{9,8},{10,11... | collective-permute-start | bytes 663560 | tf_op jit(solution)/shard_map/ppermute | solution.py:534
  64.7 0.0 copy-start
  64.7 2.7 %copy-done = bf16[5,1152,512]{2,1,0:T(8,128)(2,1)S(1)} copy-done((bf16[5,1152,512]{2,1,0:T(8,128)(2,1)S(1)}, bf16[5,1152,512]{2,1,0:T(8,128)(2,1)}, u32[]{:S(2)}) %copy-start) | copy-done | bytes 5898264
  67.4 8.4 %query_gradients.1 = bf16[192,36864]{1,0:T(8,128)(2,1)} custom-call(bf16[448,640]{1,0:T(8,128)(2,1)S(1)} %get-tuple-element.15.keys, bf16[5,1152,512]{2,1,0:T(8,128)(2,1)S(1)} %copy-done, bf16[192,36864]{1,0:T(8,128)(2,1)} %get-tuple-element.17.started), custom_call_target="tpu_custom_call", output_to_operand_aliasing={{}: (2, {})} | custom-call | flops 3963617280 | bytes 15728640 | tf_op jit(solution)/shard_map/query_gradients/pallas_call | solution.py:492
  75.9 0.0 collective-permute-done.rest_0_
  75.9 0.0 all-to-all-done.1
  75.9 1.0 %sum_gradients.1 = (f32[96,576]{1,0:T(8,128)}, f32[16,4,576]{2,1,0:T(4,128)}) custom-call(s32[16,32]{1,0:T(8,128)S(1)} %copy-done.2, bf16[256,576]{1,0:T(8,128)(2,1)S(1)} %bitcast.5, f32[96,576]{1,0:T(8,128)S(1)} %get-tuple-element.19.mine, f32[96,576]{1,0:T(8,128)S(1)} %collective-permute-done.rest_0_), custom_call_target="tpu_custom_call" | custom-call | tf_op jit(solution)/shard_map/sum_gradients/pallas_call | solution.py:113
Async XLA Ops:
  2.6 18.5 %all-to-all-start = ((bf16[16,16,576]{2,1,0:T(8,128)(2,1)}), bf16[16,16,576]{2,1,0:T(8,128)(2,1)S(1)}, u32[]{:S(2)}, u32[]{:S(2)}) async-start(bf16[16,16,576]{2,1,0:T(8,128)(2,1)} %bitcast.7), calls=%async_computation | async-start | bytes 655360 | tf_op jit(solution)/shard_map/all_to_all | solution.py:520
  10.0 11.1 %copy-start.1 = (bf16[192,576]{1,0:T(8,128)(2,1)S(1)}, bf16[192,576]{1,0:T(8,128)(2,1)}, u32[]{:S(2)}) copy-start(bf16[192,576]{1,0:T(8,128)(2,1)} %own.3) | copy-start | bytes 663556
  10.0 11.1 %copy-start.2 = (s32[16,32]{1,0:T(8,128)S(1)}, s32[16,32]{1,0:T(8,128)}, u32[]{:S(2)}) copy-start(s32[16,32]{1,0:T(8,128)} %ancestors.5) | copy-start | bytes 6148
  10.0 11.1 %copy-start.3 = (s32[16]{0:T(128)S(1)}, s32[16]{0:T(128)}, u32[]{:S(2)}) copy-start(s32[16]{0:T(128)} %anc_count.1) | copy-start | bytes 196
  59.7 16.2 %all-to-all-start.1 = ((bf16[32,8,576]{2,1,0:T(8,128)(2,1)}), bf16[32,8,576]{2,1,0:T(8,128)(2,1)S(1)}, u32[]{:S(2)}, u32[]{:S(2)}) async-start(bf16[32,8,576]{2,1,0:T(8,128)(2,1)} %bitcast.3), calls=%async_computation.1 | async-start | bytes 655360 | tf_op jit(solution)/shard_map/all_to_all | solution.py:535
  62.9 13.0 %collective-permute-start = (f32[96,576]{1,0:T(8,128)S(1)}, f32[96,576]{1,0:T(8,128)S(1)}, u32[]{:S(2)}, u32[]{:S(2)}) collective-permute-start(f32[96,576]{1,0:T(8,128)S(1)} %get-tuple-element.20), channel_id=1, source_target_pairs={{0,1},{1,0},{2,3},{3,2},{4,5},{5,4},{6,7},{7,6},{8,9},{9,8},{10,11... | collective-permute-start | bytes 663560 | tf_op jit(solution)/shard_map/ppermute | solution.py:534
  64.7 2.7 %copy-start = (bf16[5,1152,512]{2,1,0:T(8,128)(2,1)S(1)}, bf16[5,1152,512]{2,1,0:T(8,128)(2,1)}, u32[]{:S(2)}) copy-start(bf16[5,1152,512]{2,1,0:T(8,128)(2,1)} %get-tuple-element.16.ds) | copy-start | bytes 17694724

commit v13 on v12

--- a/solution.py
+++ b/solution.py
@@ -68,12 +68,17 @@
     leafs = ancestors.shape[0]
     rows = leafs * CAP * BLK
     named = ancestors[...].astype(jnp.float32)
-    named = jnp.broadcast_to(named[:, None, :], (leafs, CAP * BLK, ANC)).reshape(rows, ANC)
     first = lax.axis_index("leaf") * owned
     low_end = first.astype(jnp.float32)
     mine = (named >= low_end) & (named < low_end + owned)
     low = jnp.min(jnp.where(mine, named, float(FAR_OFF)), axis=1, keepdims=True)
     high = jnp.max(jnp.where(mine, named, -1.0), axis=1, keepdims=True)
+
+    def spread(x):
+        x = jnp.broadcast_to(x, (leafs, LANES))
+        return jnp.broadcast_to(x[:, None, :], (leafs, CAP * BLK, LANES)).reshape(rows, LANES)[:, :1]
+
+    low, high = spread(low), spread(high)
     return jnp.where(second, high, low).astype(jnp.int32) - first
 
 
@@ -500,7 +505,7 @@
         out_specs=pl.BlockSpec((tok, 2 * PAIRS * LATENT), lambda i: (0, i + ahead)),
         out_shape=jax.ShapeDtypeStruct(started.shape, started.dtype),
         input_output_aliases={2: 0},
-        compiler_params=pltpu.CompilerParams(vmem_limit_bytes=32 * MIB),
+        compiler_params=pltpu.CompilerParams(vmem_limit_bytes=51 * MIB),
         cost_estimate=pl.CostEstimate(
             flops=4 * tok * steps * PAIRS * rows * LATENT,
             bytes_accessed=4 * tok * steps * PAIRS * (LATENT + rows),

time: 77.2 us -> 76.9 us (level)
  local copies, waits for them, and re-layouts: 2.69 us -> 0.02 us
  Pallas kernels: 58.3 us -> 60.5 us
    unnamed x8 -> x6, local copies, waits for them, and re-layouts: 2.69 us -> 0.02 us
    pallas_call x1, Pallas kernels: 8.45 us -> 10.7 us  [query_gradients(): pl.pallas_call(query_kernel, grid=(steps,), in_specs=[pl.BlockSpec(keys.s...]
  transfers between devices with their start and end apart: 3 -> 3, of which waited for: 1 -> 1; matrix products, arithmetic and copies ran while one was open for 0% -> 0% of each run, Pallas kernels for 22% -> 25%
where the time goes in v13:
time: 76.9 us; the launch traced here: 76.4 us
  Pallas kernels  60.5 us (79%)
  starting transfers between devices  12.4 us (16%)
  waiting for transfers between devices  2.84 us (4%)
    pallas_call x1, Pallas kernels, attention(): pl.pallas_call(functools.partial(attn_kernel, owned, head_parts, ahead),...  38.6 us
    pallas_call x1, Pallas kernels, query_gradients(): pl.pallas_call(query_kernel, grid=(steps,), in_specs=[pl.BlockSpec(keys.s...  10.7 us
    pallas_call x1, Pallas kernels, own_scores(): pl.pallas_call(own_kernel, grid=(steps // group,), in_specs=[pl.BlockSpec...  8.23 us
    all_to_all x1, starting transfers between devices, local(): lax.all_to_all(outgoing.reshape(leafs, CAP * BLK, LATENT), 'leaf', split_...  7.36 us
    all_to_all x1, starting transfers between devices, local(): lax.all_to_all(sent.reshape(leafs * head_parts, CAP * part_rows, LATENT),...  3.19 us
    all_to_all x1, waiting for transfers between devices, local(): lax.all_to_all(outgoing.reshape(leafs, CAP * BLK, LATENT), 'leaf', split_...  2.84 us
    pallas_call x1, Pallas kernels, pick(): pl.pallas_call(pick_kernel, out_shape=jax.ShapeDtypeStruct((rows, LATENT)...  1.98 us
    ppermute x1, starting transfers between devices, local(): theirs.append(lax.ppermute(part, 'head', route))  1.83 us
  transfers between devices with their start and end apart: 3, of which 1 were waited for; matrix products, arithmetic and copies ran while one was open for 0% of the time, Pallas kernels for 25%

profile of v13, /device:TPU:0, one launch (start us, length us, event | category | flops | bytes accessed | tf_op | source)
XLA Modules:
  0.0 76.4 jit_solution(11681418038695606603)
XLA Ops:
  0.6 2.0 %pick_blocks.1 = bf16[256,576]{1,0:T(8,128)(2,1)} custom-call(s32[16,32]{1,0:T(8,128)} %ancestors.5, bf16[128,576]{1,0:T(8,128)(2,1)} %bitcast.8), custom_call_target="tpu_custom_call" | custom-call | tf_op jit(solution)/shard_map/pick_blocks/pallas_call | solution.py:95
  2.6 7.4 %all-to-all-start = ((bf16[16,16,576]{2,1,0:T(8,128)(2,1)}), bf16[16,16,576]{2,1,0:T(8,128)(2,1)S(1)}, u32[]{:S(2)}, u32[]{:S(2)}) async-start(bf16[16,16,576]{2,1,0:T(8,128)(2,1)} %bitcast.7), calls=%async_computation | async-start | bytes 655360 | tf_op jit(solution)/shard_map/all_to_all | solution.py:525
  10.0 0.0 copy-start
  10.0 0.0 copy-start.1
  10.0 0.0 copy-start.2
  10.0 8.2 %own_scores.1 = (f32[8,192,512]{2,1,0:T(8,128)}, bf16[8,192,512]{2,1,0:T(8,128)(2,1)}) custom-call(bf16[192,576]{1,0:T(8,128)(2,1)} %own.3, bf16[192,36864]{1,0:T(8,128)(2,1)} %q.3, bf16[192,32768]{1,0:T(8,128)(2,1)} %do.3), custom_call_target="tpu_custom_call" | custom-call | flops 1711276032 | bytes 13631488 | tf_op jit(solution)/shard_map/own_scores/pallas_call | solution.py:196
  18.2 2.8 %all-to-all-done = bf16[16,16,576]{2,1,0:T(8,128)(2,1)S(1)} async-done(((bf16[16,16,576]{2,1,0:T(8,128)(2,1)}), bf16[16,16,576]{2,1,0:T(8,128)(2,1)S(1)}, u32[]{:S(2)}, u32[]{:S(2)}) %all-to-all-start) | async-done | bytes 294944 | tf_op jit(solution)/shard_map/all_to_all | solution.py:525
  21.1 0.0 copy-done
  21.1 0.0 copy-done.1
  21.1 0.0 copy-done.2
  21.1 38.6 %score_gradients.1 = (bf16[192,36864]{1,0:T(8,128)(2,1)}, bf16[5,1152,512]{2,1,0:T(8,128)(2,1)}, bf16[448,640]{1,0:T(8,128)(2,1)S(1)}, bf16[256,576]{1,0:T(8,128...) custom-call(s32[16]{0:T(128)S(1)} %copy-done.2, s32[16,32]{1,0:T(8,128)S(1)} %copy-done.1, ...), custom_call_target="tpu_custom_call" | custom-call | flops 23957864448 | bytes 37748736 | tf_op jit(solution)/shard_map/score_gradients/pallas_call | solution.py:419
  59.7 3.2 %all-to-all-start.1 = ((bf16[32,8,576]{2,1,0:T(8,128)(2,1)}), bf16[32,8,576]{2,1,0:T(8,128)(2,1)S(1)}, u32[]{:S(2)}, u32[]{:S(2)}) async-start(bf16[32,8,576]{2,1,0:T(8,128)(2,1)} %bitcast.3), calls=%async_computation.1 | async-start | bytes 655360 | tf_op jit(solution)/shard_map/all_to_all | solution.py:540
  62.9 1.8 %collective-permute-start = (f32[96,576]{1,0:T(8,128)S(1)}, f32[96,576]{1,0:T(8,128)S(1)}, u32[]{:S(2)}, u32[]{:S(2)}) collective-permute-start(f32[96,576]{1,0:T(8,128)S(1)} %get-tuple-element.20), channel_id=1, source_target_pairs={{0,1},{1,0},{2,3},{3,2},{4,5},{5,4},{6,7},{7,6},{8,9},{9,8},{10,11... | collective-permute-start | bytes 663560 | tf_op jit(solution)/shard_map/ppermute | solution.py:539
  64.8 10.7 %query_gradients.1 = bf16[192,36864]{1,0:T(8,128)(2,1)} custom-call(bf16[448,640]{1,0:T(8,128)(2,1)S(1)} %get-tuple-element.15.keys, bf16[5,1152,512]{2,1,0:T(8,128)(2,1)} %get-tuple-element.16.ds, bf16[192,36864]{1,0:T(8,128)(2,1)} %get-tuple-element.17.started), custom_call_target="tpu_custom_call", output_to_operand_aliasing={{}: (2, {})} | custom-call | flops 3963617280 | bytes 15728640 | tf_op jit(solution)/shard_map/query_gradients/pallas_call | solution.py:497
  75.4 0.0 collective-permute-done.rest_0_
  75.4 0.0 all-to-all-done.1
  75.4 1.0 %sum_gradients.1 = (f32[96,576]{1,0:T(8,128)}, f32[16,4,576]{2,1,0:T(4,128)}) custom-call(s32[16,32]{1,0:T(8,128)S(1)} %copy-done.1, bf16[256,576]{1,0:T(8,128)(2,1)S(1)} %bitcast.5, f32[96,576]{1,0:T(8,128)S(1)} %get-tuple-element.19.mine, f32[96,576]{1,0:T(8,128)S(1)} %collective-permute-done.rest_0_), custom_call_target="tpu_custom_call" | custom-call | tf_op jit(solution)/shard_map/sum_gradients/pallas_call | solution.py:118
Async XLA Ops:
  2.6 18.5 %all-to-all-start = ((bf16[16,16,576]{2,1,0:T(8,128)(2,1)}), bf16[16,16,576]{2,1,0:T(8,128)(2,1)S(1)}, u32[]{:S(2)}, u32[]{:S(2)}) async-start(bf16[16,16,576]{2,1,0:T(8,128)(2,1)} %bitcast.7), calls=%async_computation | async-start | bytes 655360 | tf_op jit(solution)/shard_map/all_to_all | solution.py:525
  10.0 11.1 %copy-start = (bf16[192,576]{1,0:T(8,128)(2,1)S(1)}, bf16[192,576]{1,0:T(8,128)(2,1)}, u32[]{:S(2)}) copy-start(bf16[192,576]{1,0:T(8,128)(2,1)} %own.3) | copy-start | bytes 663556
  10.0 11.1 %copy-start.1 = (s32[16,32]{1,0:T(8,128)S(1)}, s32[16,32]{1,0:T(8,128)}, u32[]{:S(2)}) copy-start(s32[16,32]{1,0:T(8,128)} %ancestors.5) | copy-start | bytes 6148
  10.0 11.1 %copy-start.2 = (s32[16]{0:T(128)S(1)}, s32[16]{0:T(128)}, u32[]{:S(2)}) copy-start(s32[16]{0:T(128)} %anc_count.1) | copy-start | bytes 196
  59.7 15.7 %all-to-all-start.1 = ((bf16[32,8,576]{2,1,0:T(8,128)(2,1)}), bf16[32,8,576]{2,1,0:T(8,128)(2,1)S(1)}, u32[]{:S(2)}, u32[]{:S(2)}) async-start(bf16[32,8,576]{2,1,0:T(8,128)(2,1)} %bitcast.3), calls=%async_computation.1 | async-start | bytes 655360 | tf_op jit(solution)/shard_map/all_to_all | solution.py:540
  62.9 12.5 %collective-permute-start = (f32[96,576]{1,0:T(8,128)S(1)}, f32[96,576]{1,0:T(8,128)S(1)}, u32[]{:S(2)}, u32[]{:S(2)}) collective-permute-start(f32[96,576]{1,0:T(8,128)S(1)} %get-tuple-element.20), channel_id=1, source_target_pairs={{0,1},{1,0},{2,3},{3,2},{4,5},{5,4},{6,7},{7,6},{8,9},{9,8},{10,11... | collective-permute-start | bytes 663560 | tf_op jit(solution)/shard_map/ppermute | solution.py:539
